TPU v7x, 128 devices: a whole 4x4x4 slice. The times are simulated.
128 devices in a mesh: shot: 16 (over x_lo, z, core), node: 8 (over y, x_hi).
Axes of the slice: x: 4 (x_hi: 2, x_lo: 2; x = x_hi * 2 + x_lo), y: 4, z: 4, core: 2. Of those that a mesh axis runs over, the one named last changes fastest.
Arguments:
- up_time: bfloat16 [1024, 512, 1024], P(None, 'shot', 'node'), may hold values from -1 to 1
- downgoing: float32 [4, 2, 1024, 1024], P(None, None, 'shot', 'node'), may hold values from -0.1875 to 0.1875
- freq_idx: int32 [4], replicated, may hold values from 1 to 255
- node_map: int32 [1024], P('node'), may hold values from 0 to 127, as said below
Outputs:
- reflectivity: float32 [4, 2, 1024, 1024], P(None, None, None, 'node')
- residual: float32 [4, 2, 1024, 1024], P(None, None, 'shot', 'node')
Inputs may be any that keep to these rules, and one draw needn't show every extreme that they name: `node_map`: within each aligned block of 128 nodes the slots are a permutation of 0 to 127.
All inputs are finite; a program needn't handle non-finite values.
Results may differ from a plain program's by a relative error of at most 0.0023.
Values may be sent and summed in bfloat16 or wider, within the bound.
No kernel may reach another device: no remote copies, remote signals or barrier semaphores. Data moves between devices by JAX's collectives and lax.ppermute only.
A program may use at most 128 MiB of HBM per device.

v0:
```python
import math

import jax
import jax.numpy as jnp
from jax import lax
from jax.sharding import PartitionSpec as P

NODES = 1024
NT = 512
F = 4
ITERS = 2
S_DEV = 64


MAXIMUM_ACCURACY = lax.Precision.HIGHEST


def dft_table(freq_idx, sample_count):
    sample_index = jnp.arange(sample_count, dtype=jnp.int32)
    product = freq_idx[:, None] * sample_index[None, :] % NT
    phase_angle = product.astype(jnp.float32) * (2.0 * math.pi / NT)
    stacked = jnp.stack([jnp.cos(phase_angle), -jnp.sin(phase_angle)], axis=1)
    return stacked.reshape(2 * F, sample_count).astype(jnp.bfloat16)


def forward(full_down, field):
    downward_real, downward_imaginary = (full_down[:, 0], full_down[:, 1])
    wavefield_real, wavefield_imaginary = (field[:, 0], field[:, 1])
    output_real = jnp.einsum(
        "ylt,ytz->ylz", downward_real, wavefield_real, precision=MAXIMUM_ACCURACY
    ) - jnp.einsum(
        "ylt,ytz->ylz", downward_imaginary, wavefield_imaginary, precision=MAXIMUM_ACCURACY
    )
    output_imaginary = jnp.einsum(
        "ylt,ytz->ylz", downward_real, wavefield_imaginary, precision=MAXIMUM_ACCURACY
    ) + jnp.einsum("ylt,ytz->ylz", downward_imaginary, wavefield_real, precision=MAXIMUM_ACCURACY)
    return jnp.stack([output_real, output_imaginary], axis=1)


def adjoint(full_down, data):
    downward_real, downward_imaginary = (full_down[:, 0], full_down[:, 1])
    data_real_part, data_imaginary = (data[:, 0], data[:, 1])
    output_real = jnp.einsum(
        "ujc,ujq->ucq", downward_real, data_real_part, precision=MAXIMUM_ACCURACY
    ) + jnp.einsum("ujc,ujq->ucq", downward_imaginary, data_imaginary, precision=MAXIMUM_ACCURACY)
    output_imaginary = jnp.einsum(
        "ujc,ujq->ucq", downward_real, data_imaginary, precision=MAXIMUM_ACCURACY
    ) - jnp.einsum("ujc,ujq->ucq", downward_imaginary, data_real_part, precision=MAXIMUM_ACCURACY)
    return jnp.stack([output_real, output_imaginary], axis=1)


def gradient_of(full_down, residual):
    summed = lax.psum(adjoint(full_down, residual), "shot")
    swapped = lax.all_to_all(summed, "node", split_axis=2, concat_axis=2, tiled=True)
    node_width = summed.shape[3]
    node_blocks = summed.shape[2] // node_width
    mirrored = jnp.swapaxes(swapped.reshape(F, 2, node_blocks, node_width, node_width), 3, 4)
    return (summed + mirrored.reshape(summed.shape)) * 0.5


def squares(field):
    return jnp.sum(field * field, axis=(1, 2, 3))


def gradient_norm_of(gradient):
    return lax.psum(squares(gradient), "node")


def expand(values):
    return values[:, None, None, None]


def shards(up_time, downgoing, freq_idx, node_map):
    full_table = dft_table(freq_idx, NT)
    recorded = jnp.einsum(
        "ft,stn->fsn",
        full_table,
        lax.all_to_all(up_time, "shot", split_axis=0, concat_axis=1, tiled=True),
        preferred_element_type=jnp.float32,
    )
    node_width = recorded.shape[-1]
    recorded = recorded.reshape(F, 2, S_DEV, node_width)
    onehot = (node_map[:, None] == jnp.arange(node_width, dtype=jnp.int32)[None, :]).astype(
        jnp.float32
    )
    upgoing = jnp.einsum("fcsm,mj->fcsj", recorded, onehot, precision=MAXIMUM_ACCURACY)
    full_down = lax.all_gather(downgoing, "node", axis=3, tiled=True)
    reflectivity = jnp.zeros((F, 2, NODES, node_width), jnp.float32)
    residual = upgoing
    gradient = gradient_of(full_down, residual)
    grad_norm = gradient_norm_of(gradient)
    direction = gradient
    for iteration in range(ITERS):
        image = forward(full_down, direction)
        curvature = lax.psum(squares(image), ("shot", "node"))
        step_size = expand(grad_norm / curvature)
        reflectivity = reflectivity + step_size * direction
        residual = residual - step_size * image
        if iteration + 1 < ITERS:
            gradient = gradient_of(full_down, residual)
            new_norm = gradient_norm_of(gradient)
            direction = gradient + expand(new_norm / grad_norm) * direction
            grad_norm = new_norm
    return (reflectivity, residual)


def solution(mesh):
    return jax.shard_map(
        shards,
        mesh=mesh,
        in_specs=(P(None, "shot", "node"), P(None, None, "shot", "node"), P(), P("node")),
        out_specs=(P(None, None, None, "node"), P(None, None, "shot", "node")),
        check_vma=False,
    )
```

profile of v0, /device:TPU:1, one launch (start us, length us, event | category | flops | bytes accessed | tf_op | source)
XLA Modules:
  0.0 809.7 jit_solution(17190575930048589719)
XLA Ops:
  7.2 7.9 all-to-all-start
  15.1 0.7 copy.63
  15.9 0.2 cosine_convert_fusion
  16.1 118.0 %all-to-all-done = bf16[1024,32,128]{2,1,0:T(8,128)(2,1)} async-done(((bf16[1024,32,128]{2,1,0:T(8,128)(2,1)}), bf16[1024,32,128]{2,1,0:T(8,128)(2,1)}, u32[]{:S(2)}, u32[]{:S(2)}) %all-to-all-start) | async-done | bytes 8388640 | tf_op jit(solution)/shard_map/all_to_all | solution.py:78
  134.1 9.2 %copy.60 = bf16[64,16,32,128]{3,2,1,0:T(8,128)(2,1)} copy(bf16[64,16,32,128]{3,2,0,1:T(8,128)(2,1)} %bitcast.2) | data formatting | bytes 16777216 | tf_op jit(solution)/shard_map/all_to_all | solution.py:78
  143.3 4.6 fusion.28
  147.9 0.3 fusion.20
  148.3 3.2 fusion.18
  151.5 1.8 fusion.19
  153.4 1.9 subtract_bitcast_fusion.1
  155.3 1.9 add_bitcast_fusion.1
  157.2 2.3 pad_maximum_fusion
  159.6 138.7 %all-reduce.3.cloned.1.call-done = f32[4,2,1024,128]{2,3,0,1:T(8,128)} async-done(((f32[4,2,1024,128]{2,3,0,1:T(8,128)}), f32[4,2,1024,128]{2,3,0,1:T(8,128)}) %all-reduce.3.cloned.1.call-update) | async-done | bytes 4194320 | tf_op jit(solution)/shard_map/psum | solution.py:53
  298.3 5.2 copy.64
  303.6 55.6 %all_to_all.28 = f32[4,2,1024,128]{3,0,1,2:T(4,128)S(1)} all-to-all(f32[4,2,1024,128]{3,0,1,2:T(4,128)} %copy.64), channel_id=1, replica_groups=mesh['shot'=16,'node'=8] {'node'}, dimensions={2} | all-to-all | bytes 8388608 | tf_op jit(solution)/shard_map/all_to_all | solution.py:54
  359.2 4.4 copy.96
  363.7 4.9 reshape.118
  368.6 4.5 multiply_reduce_fusion.1
  373.1 0.4 broadcast_multiply_fusion
  373.5 1.6 copy-done.1
  375.1 2.4 fusion
  377.5 2.4 fusion.1
  380.0 2.4 fusion.15
  382.4 2.4 fusion.13
  384.9 0.1 multiply_reduce_fusion.3
  385.0 16.8 %psum.43 = f32[4]{0:T(128)S(1)} all-reduce(f32[4]{0:T(128)S(1)} %get-tuple-element.14), channel_id=1, replica_groups=mesh['shot'=16,'node'=8] {'node'}, use_global_device_ids=true, to_apply=%region_2.3 | all-reduce | flops 4 | bytes 32 | tf_op jit(solution)/shard_map/psum | solution.py:66
  401.7 77.0 %psum.44 = f32[4]{0:T(128)S(1)} all-reduce(f32[4]{0:T(128)S(1)} %multiply_reduce_fusion.3), channel_id=1, replica_groups=mesh['shot'=16,'node'=8] {'shot','node'}, use_global_device_ids=true, to_apply=%region_4.5 | all-reduce | flops 4 | bytes 32 | tf_op jit(solution)/shard_map/psum | solution.py:95
  478.9 1.8 fusion.16
  480.7 1.8 fusion.17
  482.6 1.9 subtract_bitcast_fusion
  484.5 1.9 add_bitcast_fusion
  486.4 2.3 pad_maximum_fusion.1
  488.7 125.9 %all-reduce.5.cloned.1.call-done = f32[4,2,1024,128]{2,3,0,1:T(8,128)} async-done(((f32[4,2,1024,128]{2,3,0,1:T(8,128)}), f32[4,2,1024,128]{2,3,0,1:T(8,128)}) %all-reduce.5.cloned.1.call-update) | async-done | bytes 4194320 | tf_op jit(solution)/shard_map/psum | solution.py:53
  614.6 5.2 copy.70
  619.9 55.4 %all_to_all.29 = f32[4,2,1024,128]{3,0,1,2:T(4,128)S(1)} all-to-all(f32[4,2,1024,128]{3,0,1,2:T(4,128)} %copy.70), channel_id=1, replica_groups=mesh['shot'=16,'node'=8] {'node'}, dimensions={2} | all-to-all | bytes 8388608 | tf_op jit(solution)/shard_map/all_to_all | solution.py:54
  675.3 4.4 copy.95
  679.7 4.9 reshape.120
  684.6 4.2 multiply_reduce_fusion
  688.7 17.0 %psum.46 = f32[4]{0:T(128)S(1)} all-reduce(f32[4]{0:T(128)S(1)} %multiply_reduce_fusion), channel_id=1, replica_groups=mesh['shot'=16,'node'=8] {'node'}, use_global_device_ids=true, to_apply=%region_7.8 | all-reduce | flops 4 | bytes 32 | tf_op jit(solution)/shard_map/psum | solution.py:66
  705.7 6.2 multiply_add_fusion.1
  711.9 2.4 fusion.4
  714.4 2.4 fusion.5
  716.8 2.4 fusion.11
  719.3 2.4 fusion.9
  721.8 67.8 %psum.47 = f32[4]{0:T(128)S(1)} all-reduce(f32[4]{0:T(128)S(1)} %multiply_reduce_fusion.2), channel_id=1, replica_groups=mesh['shot'=16,'node'=8] {'shot','node'}, use_global_device_ids=true, to_apply=%region_9.10 | all-reduce | flops 4 | bytes 32 | tf_op jit(solution)/shard_map/psum | solution.py:95
  789.6 0.8 multiply_subtract_fusion
  790.4 7.0 multiply_add_fusion
  797.4 5.3 copy.76
  (23 shorter events, 0.5 us)
Async XLA Ops:
  7.2 8.0 copy-start.3
  7.2 8.8 %copy-start.5 = (s32[4]{0:T(128)S(1)}, s32[4]{0:T(128)}, u32[]{:S(2)}) copy-start(s32[4]{0:T(128)} %param.6) | copy-start | bytes 52
  7.2 126.9 %all-to-all-start = ((bf16[1024,32,128]{2,1,0:T(8,128)(2,1)}), bf16[1024,32,128]{2,1,0:T(8,128)(2,1)}, u32[]{:S(2)}, u32[]{:S(2)}) async-start(bf16[1024,32,128]{2,1,0:T(8,128)(2,1)} %param.4), calls=%async_computation | async-start | bytes 16777216 | tf_op jit(solution)/shard_map/all_to_all | solution.py:78
  15.1 133.2 %all-gather.2.cloned.1.call-start = ((), (), s32[]{:S(2)}) async-start(), calls=%async_computation.3 | async-start | bytes 2359296 | tf_op jit(solution)/shard_map/all_gather | solution.py:87
  15.9 282.4 %all-reduce.3.cloned.1.call-start = ((), (), s32[]{:S(2)}) async-start(), calls=%async_computation.4 | async-start | bytes 8388608 | tf_op jit(solution)/shard_map/psum | solution.py:53
  143.3 4.6 copy-start.4
  148.3 3.2 copy-start
  159.5 455.1 %all-reduce.5.cloned.1.call-start = ((), (), s32[]{:S(2)}) async-start(), calls=%async_computation.5 | async-start | bytes 8388608 | tf_op jit(solution)/shard_map/psum | solution.py:53
  373.1 2.0 copy-start.1
  711.9 7.3 copy-start.2
Sparse Core Ops, SparseCore 0:
  18.7 69.8 all-gather.1
  159.7 138.6 all-reduce.2
  488.8 125.7 all-reduce.4
where the time goes:
time: 819 us; the launch traced here: 810 us
  waiting for transfers between devices  383 us (47%)
  blocking collectives  290 us (35%)
  local copies, waits for them, and re-layouts  46 us (6%)
  matrix products  40.8 us (5%)
  other arithmetic  28.2 us (3%)
  between operations  14.4 us (2%)
    psum x2, waiting for transfers between devices, gradient_of(): summed = lax.psum(adjoint(full_down, residual), 'shot')  265 us
    psum x2, blocking collectives, shards(): curvature = lax.psum(squares(image), ('shot', 'node'))  145 us
    all_to_all x1, waiting for transfers between devices, shards(): lax.all_to_all(up_time, 'shot', split_axis=0, concat_axis=1, tiled=True)  118 us
    all_to_all x2, blocking collectives, gradient_of(): lax.all_to_all(summed, 'node', split_axis=2, concat_axis=2, tiled=True)  111 us
    psum x2, blocking collectives, gradient_norm_of(): return lax.psum(squares(gradient), 'node')  33.7 us
  transfers between devices with their start and end apart: 4, of which 3 were waited for; matrix products, arithmetic and copies ran while one was open for 2% of the time, Pallas kernels for 0%

commit v1 on v0

v1 whole, which is shorter than its diff:
```python
import math

import jax
import jax.numpy as jnp
from jax import lax
from jax.sharding import Mesh, PartitionSpec as P

NODES = 1024
NT = 512
F = 4
SHOT = ("xl", "z", "core")
NODE = ("y", "xh")
PLANE = ("y", "xh", "xl", "core")
HIGH = lax.Precision.HIGH


def local_table(freq_idx, first, count):
    sample = first + jnp.arange(count, dtype=jnp.int32)
    product = freq_idx[:, None] * sample[None, :] % NT
    angle = product.astype(jnp.float32) * (2.0 * math.pi / NT)
    stacked = jnp.stack([jnp.cos(angle), -jnp.sin(angle)], axis=1)
    return stacked.reshape(2 * F, count).astype(jnp.bfloat16)


def mm(a, b):
    return lax.dot_general(a, b, (((1,), (0,)), ((), ())), precision=HIGH)


def mt(a, b):
    return lax.dot_general(a, b, (((1,), (1,)), ((), ())), precision=HIGH)


def adjoint_t(down, data):
    w = data.shape[1]
    both = data.reshape(2 * w, -1)
    with_real, with_imag = mm(both, down[0]), mm(both, down[1])
    return jnp.stack([with_real[:w] + with_imag[w:], with_real[w:] - with_imag[:w]])


def forward_t(down, field):
    w = field.shape[1]
    both = field.reshape(2 * w, -1)
    with_real, with_imag = mt(both, down[0]), mt(both, down[1])
    return jnp.stack([with_real[:w] - with_imag[w:], with_real[w:] + with_imag[:w]])


def symmetrize_t(field):
    w = field.shape[1]
    out = field.reshape(2, w, -1, w).transpose(2, 0, 3, 1)
    back = lax.all_to_all(out, PLANE, 0, 0, tiled=True)
    return (field + back.transpose(1, 2, 0, 3).reshape(field.shape)) * 0.5


def plane_sum(values):
    row = jnp.broadcast_to(jnp.stack(values)[None, :, None], (32, len(values), 128))
    return lax.all_to_all(row, PLANE, 0, 0, tiled=True).sum(0)[:, 0]


def dot(a, b):
    return jnp.sum(a * b)


def shards(up_time, downgoing, freq_idx, node_map):
    own = lax.all_to_all(downgoing, "z", 0, 0, tiled=True).transpose(1, 0, 2, 3)
    gathered = lax.all_gather(own.reshape(512, 128), PLANE, axis=0, tiled=True)
    down = gathered.reshape(8, 2, 2, 2, 4, 64, 128).transpose(3, 1, 4, 2, 5, 0, 6)
    down = down.reshape(2, NODES, NODES)

    count = up_time.shape[1]
    table = local_table(freq_idx, lax.axis_index(SHOT) * count, count)
    partial = jnp.einsum("ft,stn->fsn", table, up_time, preferred_element_type=jnp.float32)
    onehot = (node_map[:, None] == jnp.arange(128, dtype=jnp.int32)[None, :]).astype(jnp.float32)
    partial = jnp.einsum("fsm,mj->fjs", partial, onehot, precision=lax.Precision.HIGHEST)
    pieces = partial.reshape(F, 2, 2, 2, 32, 1024).transpose(2, 0, 3, 1, 4, 5)
    received = lax.all_to_all(pieces.reshape(16, 64, 1024), SHOT, 0, 0, tiled=True)
    data = received.sum(0).reshape(2, 32, 1024)

    gradient = symmetrize_t(adjoint_t(down, data))
    image = forward_t(down, gradient)
    again = symmetrize_t(adjoint_t(down, image))
    norm, curvature = plane_sum([dot(gradient, gradient), dot(image, image)])
    step = norm / curvature
    new_gradient = gradient - step * again
    change = image - step * forward_t(down, again)
    new_norm, change_change, change_image = plane_sum(
        [dot(new_gradient, new_gradient), dot(change, change), dot(change, image)]
    )
    beta = new_norm / norm
    new_curvature = change_change + 2.0 * beta * change_image + beta * beta * curvature
    new_step = new_norm / new_curvature
    result = step * gradient + new_step * (new_gradient + beta * gradient)
    residual = data - step * image - new_step * (change + beta * image)

    full = lax.all_gather(result.reshape(1, 64, 1024), SHOT, axis=0, tiled=True)
    full = full.reshape(2, F, 2, 2, 32, 1024).transpose(1, 3, 5, 0, 2, 4)
    out = residual.reshape(2, 32, 16, 64).transpose(2, 0, 3, 1)
    out = lax.all_to_all(out, SHOT, 0, 0, tiled=True)
    out = out.reshape(2, F, 2, 2, 64, 32).transpose(1, 3, 4, 0, 2, 5)
    return full.reshape(F, 2, 1024, 128), out.reshape(F, 2, 64, 128)


def solution(mesh):
    fine = Mesh(mesh.devices.reshape(2, 4, 2, 4, 2), SHOT + NODE)
    return jax.shard_map(
        shards,
        mesh=fine,
        in_specs=(P(None, SHOT, NODE), P(None, None, SHOT, NODE), P(), P(NODE)),
        out_specs=(P(None, None, None, NODE), P(None, None, SHOT, NODE)),
        check_vma=False,
    )
```

time: 819 us -> 295 us (0.36)
  waiting for transfers between devices: 383 us -> 36.7 us
  blocking collectives: 290 us -> 115 us
  matrix products: 40.8 us -> 32.2 us
    psum x2 -> x0, waiting for transfers between devices: 265 us -> none  [gradient_of(): summed = lax.psum(adjoint(full_down, residual), 'shot')]
    psum x4 -> x0, blocking collectives: 179 us -> none  [the longest x2 145 us: shards(): curvature = lax.psum(squares(image), ('shot', 'node'))]
    all_to_all x1 -> x3, waiting for transfers between devices: 118 us -> 16.6 us  [the longest x2 10.2 us: plane_sum(): return lax.all_to_all(row, PLANE, 0, 0, tiled=True).sum(0)[:, 0]]
    all_gather x1 -> x2, waiting for transfers between devices: 0.02 us -> 20.1 us  [the longest x1 20 us: shards(): full = lax.all_gather(result.reshape(1, 64, 1024), SHOT, axis=0, tiled=True)]
    psum x2 -> x0, local copies, waits for them, and re-layouts: 10.5 us -> none  [gradient_of(): summed = lax.psum(adjoint(full_down, residual), 'shot')]
    add x2 -> x4, other arithmetic: 13.1 us -> 3.65 us  [the longest x1 1.83 us: shards(): result = step * gradient + new_step * (new_gradient + beta * gradient)]
    dot_general x18 -> x10, matrix products: 40.8 us -> 32.2 us  [the longest x4 15.6 us: mt(): return lax.dot_general(a, b, (((1,), (1,)), ((), ())), precision=HIGH)]
    reshape x4 -> x7, local copies, waits for them, and re-layouts: 18.7 us -> 14.4 us  [the longest x1 11 us: shards(): gathered.reshape(8, 2, 2, 2, 4, 64, 128).transpose(3, 1, 4, 2, 5, 0, 6)]
  transfers between devices with their start and end apart: 4 -> 5, of which waited for: 3 -> 4; matrix products, arithmetic and copies ran while one was open for 2% -> 7% of each run, Pallas kernels for 0% -> 0%
where the time goes in v1:
time: 295 us; the launch traced here: 290 us
  blocking collectives  115 us (39%)
  local copies, waits for them, and re-layouts  45.2 us (15%)
  waiting for transfers between devices  36.7 us (12%)
  matrix products  32.2 us (11%)
  other arithmetic  28.8 us (10%)
  between operations  19.7 us (7%)
  starting transfers between devices  12.9 us (4%)
    all_to_all x1, blocking collectives, shards(): lax.all_to_all(pieces.reshape(16, 64, 1024), SHOT, 0, 0, tiled=True)  74.6 us
    all_gather x1, waiting for transfers between devices, shards(): full = lax.all_gather(result.reshape(1, 64, 1024), SHOT, axis=0, tiled=True)  20 us
    all_to_all x1, blocking collectives, symmetrize_t(): back = lax.all_to_all(out, PLANE, 0, 0, tiled=True)  16.4 us
    dot_general x4, matrix products, mt(): return lax.dot_general(a, b, (((1,), (1,)), ((), ())), precision=HIGH)  15.6 us
    unnamed x47, local copies, waits for them, and re-layouts  13.6 us
    all_to_all x1, blocking collectives, shards(): out = lax.all_to_all(out, SHOT, 0, 0, tiled=True)  12.4 us
    all_to_all x1, blocking collectives, shards(): own = lax.all_to_all(downgoing, 'z', 0, 0, tiled=True).transpose(1, 0, 2, 3)  11.4 us
    reshape x1, local copies, waits for them, and re-layouts, shards(): gathered.reshape(8, 2, 2, 2, 4, 64, 128).transpose(3, 1, 4, 2, 5, 0, 6)  11 us
  transfers between devices with their start and end apart: 5, of which 4 were waited for; matrix products, arithmetic and copies ran while one was open for 7% of the time, Pallas kernels for 0%

profile of v1, /device:TPU:1, one launch (start us, length us, event | category | flops | bytes accessed | tf_op | source)
XLA Modules:
  0.0 290.4 jit_solution(10844976996383158276)
XLA Ops:
  7.2 11.4 %all_to_all.35 = f32[4,2,64,128]{3,2,1,0:T(8,128)S(1)} all-to-all(f32[4,2,64,128]{3,2,1,0:T(8,128)} %param.5), channel_id=1, replica_groups=mesh['xl'=2,'z'=4,'core'=2,'y'=4,'xh'=2] {'z'}, dimensions={0} | all-to-all | bytes 524288 | tf_op jit(solution)/shard_map/all_to_all | solution.py:64
  19.4 0.8 cosine_convert_fusion
  20.2 4.6 %fusion.53 = f32[8,1024,128]{2,0,1:T(8,128)S(1)} fusion(bf16[8,32,1]{1,0,2:T(8,128)(2,1)S(1)} %bitcast.190, bf16[1024,32,128]{2,1,0:T(8,128)(2,1)} %param.4), kind=kOutput, calls=%fused_computation.93 | convolution fusion | flops 67108864 | bytes 12583424 | tf_op jit(solution)/shard_map/ft,stn->fsn/dot_general | solution.py:71
  24.8 2.7 fusion.16
  28.1 74.6 %all_to_all.36 = f32[16,64,1024]{2,1,0:T(8,128)} all-to-all(f32[16,64,1024]{2,1,0:T(8,128)S(1)} %bitcast.152), channel_id=1, replica_groups=mesh['xl'=2,'z'=4,'core'=2,'y'=4,'xh'=2] {'xl','z','core'}, dimensions={0} | all-to-all | bytes 8388608 | tf_op jit(solution)/shard_map/all_to_all | solution.py:75
  102.7 2.5 reduce_sum.72
  105.2 11.0 %copy.222 = f32[8,2,2,2,4,64,128]{6,0,5,2,4,1,3:T(8,128)S(1)} copy(f32[8,2,2,2,4,64,128]{6,5,4,3,2,1,0:T(8,128)} %bitcast.162) | data formatting | bytes 16777216 | tf_op jit(solution)/shard_map/reshape | solution.py:66
  116.3 0.9 fusion.50
  117.2 1.9 fusion.6
  119.1 2.3 fusion.14
  122.7 16.4 %all_to_all.37 = f32[32,1,2048]{2,1,0:T(1,128)S(1)} all-to-all(f32[32,1,2048]{2,1,0:T(1,128)S(1)} %reshape.346), channel_id=1, replica_groups=mesh['xl'=2,'z'=4,'core'=2,'y'=4,'xh'=2] {'y','xh','xl','core'}, dimensions={0} | all-to-all | bytes 524288 | tf_op jit(solution)/shard_map/all_to_all | solution.py:50
  139.7 1.2 reduce.2
  143.1 5.0 %fusion.4 = f32[64,1024]{1,0:T(8,128)S(1)} fusion(f32[64,1024]{1,0:T(8,128)S(1)} %bitcast.172, f32[128,8,8,128]{3,2,1,0:T(8,128)} %bitcast.147), kind=kOutput, calls=%fused_computation.5 | convolution fusion | flops 402653184 | bytes 4718592 | tf_op jit(solution)/shard_map/dot_general | solution.py:30
  148.1 2.4 fusion.12
  151.3 2.6 fusion.2
  153.8 2.6 fusion.10
  156.8 1.8 slice_add_fusion.1
  159.2 1.2 copy.174
  160.4 2.2 multiply_reduce_fusion
  162.7 1.3 pad_maximum_fusion.6
  164.7 4.5 %all-to-all-start.3 = ((f32[32,2,128]{2,1,0:T(2,128)}), f32[32,2,128]{2,1,0:T(2,128)}, u32[]{:S(2)}, u32[]{:S(2)}) async-start(f32[32,2,128]{2,1,0:T(2,128)} %broadcast_in_dim.4), calls=%async_computation.3 | async-start | bytes 65536 | tf_op jit(solution)/shard_map/all_to_all | solution.py:56
  169.2 1.1 fusion.31
  170.2 2.4 reshape.348
  172.6 3.8 %all-to-all-done.3 = f32[32,2,128]{2,1,0:T(2,128)} async-done(((f32[32,2,128]{2,1,0:T(2,128)}), f32[32,2,128]{2,1,0:T(2,128)}, u32[]{:S(2)}, u32[]{:S(2)}) %all-to-all-start.3) | async-done | bytes 32800 | tf_op jit(solution)/shard_map/all_to_all | solution.py:56
  176.4 4.6 %all-to-all-start.4 = ((f32[32,1,2048]{2,1,0:T(1,128)}), f32[32,1,2048]{2,1,0:T(1,128)}, u32[]{:S(2)}, u32[]{:S(2)}) async-start(f32[32,1,2048]{2,1,0:T(1,128)} %reshape.348), calls=%async_computation.4 | async-start | bytes 524288 | tf_op jit(solution)/shard_map/all_to_all | solution.py:50
  181.0 0.8 reduce_sum.75
  183.7 6.4 %all-to-all-done.4 = f32[32,1,2048]{2,1,0:T(1,128)} async-done(((f32[32,1,2048]{2,1,0:T(1,128)}), f32[32,1,2048]{2,1,0:T(1,128)}, u32[]{:S(2)}, u32[]{:S(2)}) %all-to-all-start.4) | async-done | bytes 262176 | tf_op jit(solution)/shard_map/all_to_all | solution.py:50
  190.1 2.9 reduce.3
  193.0 2.3 reshape.349
  195.2 1.8 copy.161
  197.1 1.2 reshape.337
  198.3 1.9 add_multiply_fusion
  200.2 5.2 %fusion = f32[64,1024]{1,0:T(8,128)} fusion(f32[64,1024]{1,0:T(8,128)S(1)} %bitcast.170, f32[128,8,8,128]{3,2,1,0:T(8,128)} %bitcast.148), kind=kOutput, calls=%fused_computation.1 | convolution fusion | flops 402653184 | bytes 4718592 | tf_op jit(solution)/shard_map/dot_general | solution.py:30
  205.4 3.1 %fusion.8 = f32[64,1024]{1,0:T(8,128)} fusion(f32[64,1024]{1,0:T(8,128)S(1)} %bitcast.171, f32[128,8,8,128]{3,2,1,0:T(8,128)S(1)} %bitcast.145), kind=kOutput, calls=%fused_computation.9 | convolution fusion | flops 402653184 | bytes 4718592 | tf_op jit(solution)/shard_map/dot_general | solution.py:30
  208.5 2.5 copy.160
  211.0 1.1 slice_subtract_fusion
  212.8 1.6 multiply_reduce_fusion.2
  214.4 2.8 fusion.29
  217.2 1.9 pad_maximum_fusion.7
  219.8 3.8 %all-to-all-start.5 = ((f32[32,3,128]{2,1,0:T(4,128)}), f32[32,3,128]{2,1,0:T(4,128)S(1)}, u32[]{:S(2)}, u32[]{:S(2)}) async-start(f32[32,3,128]{2,1,0:T(4,128)} %broadcast_in_dim.5), calls=%async_computation.5 | async-start | bytes 131072 | tf_op jit(solution)/shard_map/all_to_all | solution.py:56
  224.6 6.4 %all-to-all-done.5 = f32[32,3,128]{2,1,0:T(4,128)S(1)} async-done(((f32[32,3,128]{2,1,0:T(4,128)}), f32[32,3,128]{2,1,0:T(4,128)S(1)}, u32[]{:S(2)}, u32[]{:S(2)}) %all-to-all-start.5) | async-done | bytes 49184 | tf_op jit(solution)/shard_map/all_to_all | solution.py:56
  235.3 1.8 fusion.43
  238.4 12.4 %all_to_all.38 = f32[16,1,4096]{2,1,0:T(1,128)S(1)} all-to-all(f32[16,1,4096]{2,1,0:T(1,128)S(1)} %reshape.350), channel_id=1, replica_groups=mesh['xl'=2,'z'=4,'core'=2,'y'=4,'xh'=2] {'xl','z','core'}, dimensions={0} | all-to-all | bytes 524288 | tf_op jit(solution)/shard_map/all_to_all | solution.py:97
  250.8 1.2 reduce.4
  252.3 0.9 copy.168
  253.2 20.0 %all-gather.5.cloned.1.call-done = f32[16,64,1024]{2,1,0:T(8,128)} async-done(((f32[1,64,1024]{2,1,0:T(8,128)}), f32[16,64,1024]{2,1,0:T(8,128)}) %all-gather.5.cloned.1.call-update) | async-done | bytes 4194320 | tf_op jit(solution)/shard_map/all_gather | solution.py:94
  273.3 4.7 %copy.164 = f32[4,2,1024,2,2,32]{2,5,4,3,1,0:T(8,128)} copy(f32[4,2,1024,2,2,32]{2,5,1,4,0,3:T(8,128)} %bitcast.167) | data formatting | bytes 8388608 | tf_op jit(solution)/shard_map/transpose | solution.py:95
  278.0 5.3 %copy.167 = f32[4,2,1024,128]{3,2,1,0:T(8,128)} copy(f32[4,2,1024,128]{2,3,1,0:T(8,128)} %bitcast.153) | data formatting | bytes 8388608
  (81 shorter events, 12.9 us)
Async XLA Ops:
  7.2 98.1 %all-gather.3.cloned.1.call-start = ((), (), s32[]{:S(2)}) async-start(), calls=%async_computation.7 | async-start | bytes 8650752 | tf_op jit(solution)/shard_map/all_gather | solution.py:65
  20.2 4.6 %copy-start.18 = (s32[128]{0:T(128)S(1)}, s32[128]{0:T(128)}, u32[]{:S(2)}) copy-start(s32[128]{0:T(128)} %param.7) | copy-start | bytes 1540
  117.2 4.2 %copy-start = (f32[1,2,4,2,64,8,128]{6,5,4,3,2,1,0:T(8,128)}, f32[1,2,4,2,64,8,128]{6,5,4,3,2,1,0:T(8,128)S(1)}, u32[]{:S(2)}) copy-start(f32[1,2,4,2,64,8,128]{6,5,4,3,2,1,0:T(8,128)S(1)} %get-tuple-element.22) | copy-start | bytes 12582916
  117.2 4.2 %copy-start.3 = (f32[1,2,4,2,64,8,128]{6,5,4,3,2,1,0:T(8,128)}, f32[1,2,4,2,64,8,128]{6,5,4,3,2,1,0:T(8,128)S(1)}, u32[]{:S(2)}) copy-start(f32[1,2,4,2,64,8,128]{6,5,4,3,2,1,0:T(8,128)S(1)} %get-tuple-element.23) | copy-start | bytes 12582916
  121.4 0.7 copy-start.16
  121.7 19.6 %copy-start.5 = (f32[32,1024]{0,1:T(8,128)}, f32[32,1024]{0,1:T(8,128)S(1)}, u32[]{:S(2)}) copy-start(f32[32,1024]{0,1:T(8,128)S(1)} %copy.169) | copy-start | bytes 393220
  121.9 19.4 %copy-start.6 = (f32[32,1024]{0,1:T(8,128)}, f32[32,1024]{0,1:T(8,128)S(1)}, u32[]{:S(2)}) copy-start(f32[32,1024]{0,1:T(8,128)S(1)} %copy.170) | copy-start | bytes 393220
  122.7 19.7 %copy-start.17 = (f32[32,1024]{1,0:T(8,128)S(1)}, f32[32,1024]{1,0:T(8,128)}, u32[]{:S(2)}) copy-start(f32[32,1024]{1,0:T(8,128)} %copy-done.16) | copy-start | bytes 393220
  142.4 5.7 %copy-start.1 = (f32[1,2,4,2,64,8,128]{6,5,4,3,2,1,0:T(8,128)S(1)}, f32[1,2,4,2,64,8,128]{6,5,4,3,2,1,0:T(8,128)}, u32[]{:S(2)}) copy-start(f32[1,2,4,2,64,8,128]{6,5,4,3,2,1,0:T(8,128)} %copy-done) | copy-start | bytes 12582916
  148.1 3.2 %copy-start.4 = (f32[1,2,4,2,64,8,128]{6,5,4,3,2,1,0:T(8,128)S(1)}, f32[1,2,4,2,64,8,128]{6,5,4,3,2,1,0:T(8,128)}, u32[]{:S(2)}) copy-start(f32[1,2,4,2,64,8,128]{6,5,4,3,2,1,0:T(8,128)} %copy-done.3) | copy-start | bytes 12582916
  150.5 3.3 %copy-start.9 = (f32[32,1024]{1,0:T(8,128)}, f32[32,1024]{1,0:T(8,128)S(1)}, u32[]{:S(2)}) copy-start(f32[32,1024]{1,0:T(8,128)S(1)} %get-tuple-element.28) | copy-start | bytes 393220
  158.5 0.7 copy-start.15
  159.2 36.0 %copy-start.7 = (f32[32,1024]{0,1:T(8,128)}, f32[32,1024]{0,1:T(8,128)S(1)}, u32[]{:S(2)}) copy-start(f32[32,1024]{0,1:T(8,128)S(1)} %copy.173) | copy-start | bytes 393220
  160.4 34.8 %copy-start.8 = (f32[32,1024]{0,1:T(8,128)}, f32[32,1024]{0,1:T(8,128)S(1)}, u32[]{:S(2)}) copy-start(f32[32,1024]{0,1:T(8,128)S(1)} %copy.174) | copy-start | bytes 393220
  164.7 11.8 %all-to-all-start.3 = ((f32[32,2,128]{2,1,0:T(2,128)}), f32[32,2,128]{2,1,0:T(2,128)}, u32[]{:S(2)}, u32[]{:S(2)}) async-start(f32[32,2,128]{2,1,0:T(2,128)} %broadcast_in_dim.4), calls=%async_computation.3 | async-start | bytes 65536 | tf_op jit(solution)/shard_map/all_to_all | solution.py:56
  176.4 13.6 %all-to-all-start.4 = ((f32[32,1,2048]{2,1,0:T(1,128)}), f32[32,1,2048]{2,1,0:T(1,128)}, u32[]{:S(2)}, u32[]{:S(2)}) async-start(f32[32,1,2048]{2,1,0:T(1,128)} %reshape.348), calls=%async_computation.4 | async-start | bytes 524288 | tf_op jit(solution)/shard_map/all_to_all | solution.py:50
  198.3 7.1 %copy-start.2 = (f32[1,2,4,2,64,8,128]{6,5,4,3,2,1,0:T(8,128)S(1)}, f32[1,2,4,2,64,8,128]{6,5,4,3,2,1,0:T(8,128)}, u32[]{:S(2)}) copy-start(f32[1,2,4,2,64,8,128]{6,5,4,3,2,1,0:T(8,128)} %copy-done) | copy-start | bytes 12582916
  212.2 0.7 copy-start.11
  212.2 0.7 copy-start.13
  217.2 20.1 %copy-start.10 = (f32[32,1024]{1,0:T(8,128)S(1)}, f32[32,1024]{1,0:T(8,128)}, u32[]{:S(2)}) copy-start(f32[32,1024]{1,0:T(8,128)} %copy-done.9) | copy-start | bytes 393220
  217.2 20.3 %copy-start.14 = (f32[32,1024]{1,0:T(8,128)S(1)}, f32[32,1024]{1,0:T(8,128)}, u32[]{:S(2)}) copy-start(f32[32,1024]{1,0:T(8,128)} %copy-done.13) | copy-start | bytes 393220
  217.2 20.4 %copy-start.12 = (f32[32,1024]{1,0:T(8,128)S(1)}, f32[32,1024]{1,0:T(8,128)}, u32[]{:S(2)}) copy-start(f32[32,1024]{1,0:T(8,128)} %copy-done.11) | copy-start | bytes 393220
  219.8 11.2 %all-to-all-start.5 = ((f32[32,3,128]{2,1,0:T(4,128)}), f32[32,3,128]{2,1,0:T(4,128)S(1)}, u32[]{:S(2)}, u32[]{:S(2)}) async-start(f32[32,3,128]{2,1,0:T(4,128)} %broadcast_in_dim.5), calls=%async_computation.5 | async-start | bytes 131072 | tf_op jit(solution)/shard_map/all_to_all | solution.py:56
  223.6 49.7 %all-gather.5.cloned.1.call-start = ((), (), s32[]{:S(2)}) async-start(), calls=%async_computation.8 | async-start | bytes 4456448 | tf_op jit(solution)/shard_map/all_gather | solution.py:94
Sparse Core Ops, SparseCore 0:
  19.5 70.6 all-gather.2
  237.3 35.9 all-gather.4

commit v2 on v1

v2 whole, which is shorter than its diff:
```python
import math

import jax
import jax.numpy as jnp
from jax import lax
from jax.experimental import pallas as pl
from jax.experimental.pallas import tpu as pltpu
from jax.sharding import Mesh, PartitionSpec as P

NODES = 1024
NT = 512
F = 4
SHOT = ("xl", "z", "core")
NODE = ("y", "xh")
PLANE = ("y", "xh", "xl", "core")
BF = jnp.bfloat16
F32 = jnp.float32
PARAMS = pltpu.CompilerParams(vmem_limit_bytes=40 * 1024 * 1024)


def local_table(freq_idx, first, count):
    sample = first + jnp.arange(count, dtype=jnp.int32)
    product = freq_idx[:, None] * sample[None, :] % NT
    angle = product.astype(F32) * (2.0 * math.pi / NT)
    stacked = jnp.stack([jnp.cos(angle), -jnp.sin(angle)], axis=1)
    return stacked.reshape(2 * F, count).astype(BF)


def struct(shape, dtype=F32):
    return jax.ShapeDtypeStruct(shape, dtype)


def cost(flops, moved):
    return pl.CostEstimate(flops=flops, bytes_accessed=moved, transcendentals=0)


def split(x):
    high = x.astype(BF)
    return high, (x - high.astype(F32)).astype(BF)


def stacked_split(x):
    return jnp.concatenate(split(x), axis=0)


def dot(a, b, transposed=False):
    dims = (((1,), (1 if transposed else 0,)), ((), ()))
    return lax.dot_general(a, b, dims, preferred_element_type=F32)


def product(both, field, transposed):
    high, low = split(field)
    first = dot(both, high, transposed)
    return first[:64] + first[64:] + dot(both[:64], low, transposed)


def lanes_sum(x):
    total = x[:, :128]
    for i in range(1, x.shape[1] // 128):
        total = total + x[:, i * 128 : (i + 1) * 128]
    return jnp.sum(total, axis=0, keepdims=True)


def total(rows):
    return jnp.sum(rows, axis=(0, 1), keepdims=True)


def transform_body(up_ref, table_ref, inverse_ref, out_ref, sums, exponents):
    block = (pl.program_id(0) * 2 + pl.program_id(1)) * 2 + pl.program_id(2)
    index = jnp.broadcast_to(inverse_ref[0:1, :], (64, 128))
    largest = jnp.zeros((64, 128), F32)
    for part in range(2):
        for group in range(8):
            x = up_ref[0, part, 0, group * 8 : group * 8 + 8].reshape(256, 128)
            y = dot(table_ref[...], x)
            y = jnp.take_along_axis(y, index, axis=1)
            largest = jnp.maximum(largest, jnp.abs(y))
            row = part * 64 + group * 8
            for fc in range(8):
                sums[fc, row : row + 8, :] = y[fc * 8 : fc * 8 + 8]
    peak = jnp.maximum(jnp.max(largest, axis=(0, 1), keepdims=True), 1e-30)
    exponent = jnp.floor(jnp.log(peak) * (1.0 / math.log(2.0))) - 14.0
    scale = jnp.exp2(-exponent)
    exponents[pl.ds(block, 1), :] = jnp.broadcast_to(exponent, (1, 128))
    rows = pl.multiple_of(block * 64, 64)
    for fc in range(8):
        scaled = jnp.floor(sums[fc].T * scale + 0.5)
        coded = jnp.clip(scaled, -32767.0, 32767.0).astype(jnp.int32).astype(jnp.int16)
        for k in range(4):
            dest = ((k // 2) * 4 + fc // 2) * 2 + k % 2
            out_ref[dest, pl.ds(rows + (fc % 2) * 32, 32), :] = coded[k * 32 : k * 32 + 32]

    @pl.when(block == 7)
    def _():
        tile = jnp.concatenate([exponents[...], jnp.zeros((8, 128), F32)], axis=0)
        coded = tile.astype(jnp.int32).astype(jnp.int16)
        for dest in range(16):
            out_ref[dest, 512:528, :] = coded


def transform(up_time, table, inverse):
    return pl.pallas_call(
        transform_body,
        grid=(2, 2, 2),
        in_specs=[
            pl.BlockSpec((1, 2, 1, 64, 32, 128), lambda x, c, z: (x, z, c, 0, 0, 0)),
            pl.BlockSpec((64, 256), lambda x, c, z: (0, 0)),
            pl.BlockSpec((8, 128), lambda x, c, z: (0, 0)),
        ],
        out_specs=pl.BlockSpec((16, 528, 128), lambda x, c, z: (0, 0, 0)),
        out_shape=struct((16, 528, 128), jnp.int16),
        scratch_shapes=[pltpu.VMEM((8, 128, 128), F32), pltpu.VMEM((8, 128), F32)],
        compiler_params=PARAMS,
        cost_estimate=cost(600_000_000, 10_000_000),
        name="transform",
    )(up_time.reshape(2, 4, 2, 64, 32, 128), table, inverse)


def collect_body(in_ref, out_ref):
    scales = [jnp.exp2(in_ref[i, 512:528, :].astype(F32)) for i in range(16)]
    for block in range(8):
        summed = jnp.zeros((64, 128), F32)
        for i in range(16):
            piece = in_ref[i, block * 64 : block * 64 + 64, :].astype(F32)
            summed = summed + piece * scales[i][block : block + 1]
        out_ref[:, block * 128 : block * 128 + 128] = summed


def collect(received):
    return pl.pallas_call(
        collect_body,
        out_shape=struct((64, 1024)),
        compiler_params=PARAMS,
        cost_estimate=cost(10_000_000, 3_000_000),
        name="collect",
    )(received)


def tile_of(down_ref, k, c):
    first = down_ref[0, k, :, c].reshape(256, 128)
    second = down_ref[1, k, :, c].reshape(256, 128)
    return jnp.concatenate([first, second], axis=1)


def adjoint_step(down_ref, both_ref):
    sums = [None, None]
    for k in range(4):
        both = both_ref[:, k * 256 : k * 256 + 256]
        for c in range(2):
            term = product(both, tile_of(down_ref, k, c), False)
            sums[c] = term if k == 0 else sums[c] + term
    real = sums[0][:32] + sums[1][32:]
    imaginary = sums[0][32:] - sums[1][:32]
    return jnp.concatenate([real, imaginary], axis=0)


def forward_step(down_ref, field, sums_ref, first):
    both = stacked_split(field)
    for c in range(2):
        for k in range(4):
            term = product(both, tile_of(down_ref, k, c), True)
            lanes = slice(k * 256, k * 256 + 256)

            @pl.when(first)
            def _():
                sums_ref[c, :, lanes] = term

            @pl.when(jnp.logical_not(first))
            def _():
                sums_ref[c, :, lanes] += term


def forward_end(sums_ref):
    real = sums_ref[0, :32] - sums_ref[1, 32:]
    imaginary = sums_ref[0, 32:] + sums_ref[1, :32]
    return jnp.concatenate([real, imaginary], axis=0)


def pack(field, out_ref, first):
    turned = field.T
    for k in range(8):
        piece = turned[k * 32 : k * 32 + 32]
        out_ref[first + k, 0:16, :] = jnp.concatenate([piece[:16], piece[16:]], axis=1)


def unpack(in_ref, first):
    pieces = [in_ref[first + k, 0:16, :] for k in range(4)]
    rows = []
    for c in range(2):
        for half in range(2):
            at = half * 64 + c * 32
            rows.append(jnp.concatenate([p[:, at : at + 32] for p in pieces], axis=1))
    return jnp.concatenate(rows, axis=0)


def symmetric(field, in_ref, first):
    mirrored = jnp.concatenate([unpack(in_ref, first), unpack(in_ref, first + 4)], axis=1)
    return (field + mirrored) * 0.5


DOWN_BLOCK = (2, 4, 4, 2, 64, 128)


def whole(shape):
    return pl.BlockSpec(shape, lambda *_: (0,) * len(shape))


def first_adjoint_body(data_ref, down_ref, field_ref, pieces_ref, both):
    @pl.when(pl.program_id(0) == 0)
    def _():
        both[...] = stacked_split(data_ref[...])

    field = adjoint_step(down_ref, both)
    field_ref[...] = field
    pack(field, pieces_ref, 0)


def first_adjoint(data, down):
    return pl.pallas_call(
        first_adjoint_body,
        grid=(4,),
        in_specs=[whole((64, 1024)), pl.BlockSpec(DOWN_BLOCK, lambda j: (j, 0, 0, 0, 0, 0))],
        out_specs=[
            pl.BlockSpec((64, 256), lambda j: (0, j)),
            pl.BlockSpec((8, 16, 128), lambda j: (j, 0, 0)),
        ],
        out_shape=[struct((64, 1024)), struct((32, 16, 128))],
        scratch_shapes=[pltpu.VMEM((128, 1024), BF)],
        compiler_params=PARAMS,
        cost_estimate=cost(800_000_000, 9_000_000),
        name="first_adjoint",
    )(data, down)


def second_body(
    field_ref, in_ref, down_ref, gradient_ref, image_ref, again_ref, out_ref, sums, both, norm
):
    phase, j = pl.program_id(0), pl.program_id(1)
    lanes = pl.ds(pl.multiple_of(j * 256, 256), 256)

    @pl.when(phase == 0)
    def _():
        gradient = symmetric(field_ref[:, lanes], in_ref, j * 8)
        gradient_ref[:, lanes] = gradient
        forward_step(down_ref, gradient, sums, j == 0)
        part = lanes_sum(gradient * gradient)
        norm[0:1, :] = jnp.where(j == 0, part, norm[0:1, :] + part)

    @pl.when((phase == 1) & (j == 0))
    def _():
        image = forward_end(sums)
        image_ref[...] = image
        both[...] = stacked_split(image)
        norm[1:2, :] = lanes_sum(image * image)

    @pl.when(phase == 1)
    def _():
        field = adjoint_step(down_ref, both)
        again_ref[:, lanes] = field
        pack(field, out_ref, j * 8)
        for k in range(8):
            out_ref[j * 8 + k, 16:24, :] = norm[...]


def second(field, received, down):
    return pl.pallas_call(
        second_body,
        grid=(2, 4),
        in_specs=[
            whole((64, 1024)),
            whole((32, 16, 128)),
            pl.BlockSpec(DOWN_BLOCK, lambda p, j: (j, 0, 0, 0, 0, 0)),
        ],
        out_specs=[whole((64, 1024))] * 3 + [whole((32, 24, 128))],
        out_shape=[struct((64, 1024))] * 3 + [struct((32, 24, 128))],
        scratch_shapes=[
            pltpu.VMEM((2, 64, 1024), F32),
            pltpu.VMEM((128, 1024), BF),
            pltpu.VMEM((8, 128), F32),
        ],
        compiler_params=PARAMS,
        cost_estimate=cost(1_600_000_000, 18_000_000),
        name="second",
    )(field, received, down)


def join_body(gradient_ref, again_ref, in_ref, out_ref):
    out_ref[0:64, :] = gradient_ref[...]
    for j in range(4):
        lanes = slice(j * 256, j * 256 + 256)
        out_ref[64:128, lanes] = symmetric(again_ref[:, lanes], in_ref, j * 8)


def join(gradient, again, received):
    return pl.pallas_call(
        join_body,
        out_shape=struct((128, 1024)),
        compiler_params=PARAMS,
        cost_estimate=cost(1_000_000, 2_000_000),
        name="join",
    )(gradient, again, received)


def first_step(in_ref):
    norm = total(jnp.sum(in_ref[:, 16:17, :], axis=0))
    curvature = total(jnp.sum(in_ref[:, 17:18, :], axis=0))
    return norm, curvature


def change_body(pair_ref, image_ref, in_ref, down_ref, change_ref, out_ref, sums):
    j = pl.program_id(0)
    lanes = pl.ds(pl.multiple_of(j * 256, 256), 256)
    forward_step(down_ref, pair_ref[64:128, lanes], sums, j == 0)

    @pl.when(j == 3)
    def _():
        norm, curvature = first_step(in_ref)
        step = norm / curvature
        image = image_ref[...]
        change = image - step * forward_end(sums)
        change_ref[...] = change
        gradient = pair_ref[0:64, :] - step * pair_ref[64:128, :]
        rows = jnp.concatenate(
            [
                lanes_sum(gradient * gradient),
                lanes_sum(change * change),
                lanes_sum(change * image),
                jnp.zeros((5, 128), F32),
            ],
            axis=0,
        )
        for i in range(32):
            out_ref[i] = rows


def changed(pair, image, received, down):
    return pl.pallas_call(
        change_body,
        grid=(4,),
        in_specs=[
            whole((128, 1024)),
            whole((64, 1024)),
            whole((32, 24, 128)),
            pl.BlockSpec(DOWN_BLOCK, lambda j: (j, 0, 0, 0, 0, 0)),
        ],
        out_specs=[whole((64, 1024)), whole((32, 8, 128))],
        out_shape=[struct((64, 1024)), struct((32, 8, 128))],
        scratch_shapes=[pltpu.VMEM((2, 64, 1024), F32)],
        compiler_params=PARAMS,
        cost_estimate=cost(800_000_000, 9_000_000),
        name="change",
    )(pair, image, received, down)


def residual_body(data_ref, image_ref, change_ref, in_ref, sums_ref, out_ref):
    norm, curvature = first_step(in_ref)
    step = norm / curvature
    rows = jnp.sum(sums_ref[...], axis=0)
    new_norm, change_change, change_image = (total(rows[i : i + 1]) for i in range(3))
    beta = new_norm / norm
    new_step = new_norm / (change_change + 2.0 * beta * change_image + beta * beta * curvature)
    image = image_ref[...]
    left = data_ref[...] - step * image - new_step * (change_ref[...] + beta * image)
    turned = left.T
    scalars = jnp.concatenate(
        [
            jnp.broadcast_to(step + new_step * (1.0 + beta), (1, 128)),
            jnp.broadcast_to(-new_step * step, (1, 128)),
            jnp.zeros((6, 128), F32),
        ],
        axis=0,
    )
    for dest in range(16):
        at = ((dest // 8) * 2 + dest % 2) * 256 + (dest // 2 % 4) * 64
        piece = turned[at : at + 64]
        out_ref[dest, 0:32, :] = jnp.concatenate([piece[:32], piece[32:]], axis=1)
        out_ref[dest, 32:40, :] = scalars


def residual_of(data, image, change, received, sums):
    return pl.pallas_call(
        residual_body,
        out_shape=struct((16, 40, 128)),
        compiler_params=PARAMS,
        cost_estimate=cost(2_000_000, 2_000_000),
        name="residual",
    )(data, image, change, received, sums)


def place_body(in_ref, out_ref):
    for f in range(F):
        pieces = [in_ref[(k // 2 * 4 + f) * 2 + k % 2, 0:32, :] for k in range(4)]
        for c in range(2):
            for half in range(2):
                at = half * 64 + c * 32
                row = jnp.concatenate([p[:, at : at + 32] for p in pieces], axis=1)
                out_ref[f, c, half * 32 : half * 32 + 32, :] = row


def place(received):
    return pl.pallas_call(
        place_body,
        out_shape=struct((F, 2, 64, 128)),
        compiler_params=PARAMS,
        cost_estimate=cost(1_000_000, 1_000_000),
        name="place",
    )(received)


def combine_body(pairs_ref, scalars_ref, out_ref):
    first = scalars_ref[0, 0, 0, 0:1, :]
    second_ = scalars_ref[0, 0, 0, 1:2, :]
    for j in range(8):
        lanes = slice(j * 128, j * 128 + 128)
        rows = [
            pairs_ref[k // 2, 0, k % 2, 0, 0, :, lanes] * first
            + pairs_ref[k // 2, 0, k % 2, 1, 0, :, lanes] * second_
            for k in range(4)
        ]
        out_ref[0, 0, lanes, :] = jnp.concatenate(rows, axis=0).T


def combine(pairs, received):
    return pl.pallas_call(
        combine_body,
        grid=(F, 2),
        in_specs=[
            pl.BlockSpec((2, 1, 2, 2, 1, 32, 1024), lambda f, c: (0, f, 0, 0, c, 0, 0)),
            pl.BlockSpec((1, 1, 1, 8, 128), lambda f, c: (0, f, 0, 4, 0)),
        ],
        out_specs=pl.BlockSpec((1, 1, 1024, 128), lambda f, c: (f, c, 0, 0)),
        out_shape=struct((F, 2, 1024, 128)),
        compiler_params=PARAMS,
        cost_estimate=cost(10_000_000, 12_000_000),
        name="combine",
    )(pairs.reshape(2, F, 2, 2, 2, 32, 1024), received.reshape(2, F, 2, 40, 128))


def shards(up_time, downgoing, freq_idx, node_map):
    own = lax.all_to_all(downgoing, "z", 0, 0, tiled=True)
    down = lax.all_gather(own.reshape(512, 128), PLANE, axis=0, tiled=True)
    down = down.reshape(8, 4, 4, 2, 64, 128)

    count = up_time.shape[1]
    table = local_table(freq_idx, lax.axis_index(SHOT) * count, count)
    table = table[:, None, None, :] * jnp.eye(8, dtype=BF)[None, :, :, None]
    slots = jnp.arange(128, dtype=jnp.int32)
    inverse = jnp.sum(jnp.where(node_map[:, None] == slots[None, :], slots[:, None], 0), axis=0)
    inverse = jnp.broadcast_to(inverse[None, :], (8, 128))
    pieces = transform(up_time, table.reshape(64, 256), inverse)
    data = collect(lax.all_to_all(pieces, SHOT, 0, 0, tiled=True))

    field, pieces = first_adjoint(data, down)
    received = lax.all_to_all(pieces, PLANE, 0, 0, tiled=True)
    gradient, image, again, pieces = second(field, received, down)
    received = lax.all_to_all(pieces, PLANE, 0, 0, tiled=True)
    pair = join(gradient, again, received)
    pairs = lax.all_gather(pair, SHOT, axis=0, tiled=True)
    change, sums = changed(pair, image, received, down)
    sums = lax.all_to_all(sums, PLANE, 0, 0, tiled=True)
    left = lax.all_to_all(residual_of(data, image, change, received, sums), SHOT, 0, 0, tiled=True)
    return combine(pairs, left), place(left)


def solution(mesh):
    fine = Mesh(mesh.devices.reshape(2, 4, 2, 4, 2), SHOT + NODE)
    return jax.shard_map(
        shards,
        mesh=fine,
        in_specs=(P(None, SHOT, NODE), P(None, None, SHOT, NODE), P(), P(NODE)),
        out_specs=(P(None, None, None, NODE), P(None, None, SHOT, NODE)),
        check_vma=False,
    )
```

time: 295 us -> 201 us (0.68); the launches traced: 290 us -> 200 us
  Pallas kernels: 0 us -> 38.6 us
  matrix products: 32.2 us -> 0 us
  local copies, waits for them, and re-layouts: 45.2 us -> 13.7 us
  other arithmetic: 28.8 us -> 1.63 us
  waiting for transfers between devices: 36.7 us -> 18.2 us
  starting transfers between devices: 12.9 us -> 0.08 us
  between operations: 19.7 us -> 14.1 us
    pallas_call x0 -> x9, Pallas kernels: none -> 38.6 us  [the longest x1 11.9 us: second(): pl.pallas_call(second_body, grid=(2, 4), in_specs=[whole((64, 1024)), who...]
    dot_general x10 -> x0, matrix products: 32.2 us -> none  [the longest x4 15.6 us: mt(): return lax.dot_general(a, b, (((1,), (1,)), ((), ())), precision=HIGH)]
    all_to_all x3 -> x0, waiting for transfers between devices: 16.6 us -> none  [the longest x2 10.2 us: plane_sum(): return lax.all_to_all(row, PLANE, 0, 0, tiled=True).sum(0)[:, 0]]
    reshape x7 -> x0, local copies, waits for them, and re-layouts: 14.4 us -> none  [the longest x1 11 us: shards(): gathered.reshape(8, 2, 2, 2, 4, 64, 128).transpose(3, 1, 4, 2, 5, 0, 6)]
    all_to_all x3 -> x0, starting transfers between devices: 12.8 us -> none  [the longest x2 8.24 us: plane_sum(): return lax.all_to_all(row, PLANE, 0, 0, tiled=True).sum(0)[:, 0]]
    reduce_sum x7 -> x1, other arithmetic: 10.7 us -> 0.75 us  [shards(): jnp.sum(jnp.where(node_map[:, None] == slots[None, :], slots[:, None], 0)...]
    transpose x5 -> x0, local copies, waits for them, and re-layouts: 7.41 us -> none  [the longest x1 4.74 us: shards(): full = full.reshape(2, F, 2, 2, 32, 1024).transpose(1, 3, 5, 0, 2, 4)]
    all_to_all x3 -> x0, other arithmetic: 5.35 us -> none  [the longest x2 4.11 us: symmetrize_t(): back = lax.all_to_all(out, PLANE, 0, 0, tiled=True)]
  transfers between devices with their start and end apart: 5 -> 2, of which waited for: 4 -> 2; matrix products, arithmetic and copies ran while one was open for 7% -> 1% of each run, Pallas kernels for 0% -> 9%
where the time goes in v2:
time: 201 us; the launch traced here: 200 us
  blocking collectives  114 us (57%)
  Pallas kernels  38.6 us (19%)
  waiting for transfers between devices  18.2 us (9%)
  between operations  14.1 us (7%)
  local copies, waits for them, and re-layouts  13.7 us (7%)
    all_to_all x1, blocking collectives, shards(): data = collect(lax.all_to_all(pieces, SHOT, 0, 0, tiled=True))  44.4 us
    all_to_all x2, blocking collectives, shards(): received = lax.all_to_all(pieces, PLANE, 0, 0, tiled=True)  29 us
    all_to_all x1, blocking collectives, shards(): lax.all_to_all(residual_of(data, image, change, received, sums), SHOT, 0,...  16 us
    unnamed x10, local copies, waits for them, and re-layouts  13.5 us
    all_to_all x1, blocking collectives, shards(): sums = lax.all_to_all(sums, PLANE, 0, 0, tiled=True)  12.7 us
    pallas_call x1, Pallas kernels, second(): pl.pallas_call(second_body, grid=(2, 4), in_specs=[whole((64, 1024)), who...  11.9 us
    all_to_all x1, blocking collectives, shards(): own = lax.all_to_all(downgoing, 'z', 0, 0, tiled=True)  11.5 us
    all_gather x1, waiting for transfers between devices, shards(): pairs = lax.all_gather(pair, SHOT, axis=0, tiled=True)  11.3 us
  transfers between devices with their start and end apart: 2, of which 2 were waited for; matrix products, arithmetic and copies ran while one was open for 1% of the time, Pallas kernels for 9%

profile of v2, /device:TPU:1, one launch (start us, length us, event | category | flops | bytes accessed | tf_op | source)
XLA Modules:
  0.0 199.9 jit_solution(3139206134917463337)
XLA Ops:
  7.2 0.0 all-gather.3.cloned.1.call-start
  7.2 11.5 %all_to_all.30 = f32[4,2,64,128]{3,2,1,0:T(8,128)} all-to-all(f32[4,2,64,128]{3,2,1,0:T(8,128)} %param.5), channel_id=1, replica_groups=mesh['xl'=2,'z'=4,'core'=2,'y'=4,'xh'=2] {'z'}, dimensions={0} | all-to-all | bytes 524288 | tf_op jit(solution)/shard_map/all_to_all | solution.py:440
  18.7 0.0 all-gather.3.cloned.1.call-update
  18.8 0.0 all-gather.5.cloned.1.call-start
  18.8 0.8 cosine_convert_fusion
  19.6 0.1 broadcast_multiply_fusion
  19.7 0.1 mul.78.table_ref
  19.9 0.8 select_reduce_fusion
  20.6 0.0 copy-start.3
  20.6 3.4 %copy-done.3 = bf16[1024,32,128]{2,1,0:T(8,128)(2,1)S(1)} copy-done((bf16[1024,32,128]{2,1,0:T(8,128)(2,1)S(1)}, bf16[1024,32,128]{2,1,0:T(8,128)(2,1)}, u32[]{:S(2)}) %copy-start.3) | copy-done | bytes 8388632
  24.0 6.1 %transform.1 = s16[16,528,128]{2,1,0:T(8,128)(2,1)S(1)} custom-call(bf16[2,4,2,64,32,128]{5,4,3,2,1,0:T(8,128)(2,1)S(1)} %bitcast.11, bf16[64,256]{1,0:T(8,128)(2,1)S(1)} %mul.78.table_ref, s32[8,128]{1,0:T(8,128)S(1)} %broadcast_in_dim.16.inverse_ref), custom_call_target="tpu_custom_call" | custom-call | flops 600000000 | bytes 10000000 | tf_op jit(solution)/shard_map/transform/pallas_call | solution.py:102
  30.1 44.4 %all_to_all.31.in_ref = s16[16,528,128]{2,1,0:T(8,128)(2,1)S(1)} all-to-all(s16[16,528,128]{2,1,0:T(8,128)(2,1)S(1)} %transform.1), channel_id=1, replica_groups=mesh['xl'=2,'z'=4,'core'=2,'y'=4,'xh'=2] {'xl','z','core'}, dimensions={0} | all-to-all | bytes 4325376 | tf_op jit(solution)/shard_map/all_to_all | solution.py:451
  74.5 0.6 collect.1.data_ref
  75.1 6.9 %all-gather.3.cloned.1.call-done = f32[16384,128]{1,0:T(8,128)} async-done(((f32[512,128]{1,0:T(8,128)}), f32[16384,128]{1,0:T(8,128)}) %all-gather.3.cloned.1.call-update) | async-done | bytes 8388624 | tf_op jit(solution)/shard_map/all_gather | solution.py:441
  82.0 0.0 copy-start
  82.0 3.4 %copy-done = f32[16384,128]{1,0:T(8,128)S(1)} copy-done((f32[16384,128]{1,0:T(8,128)S(1)}, f32[16384,128]{1,0:T(8,128)}, u32[]{:S(2)}) %copy-start) | copy-done | bytes 8388632
  85.3 0.0 copy-start.1
  85.3 3.0 %first_adjoint.1 = (f32[64,1024]{1,0:T(8,128)S(1)}, f32[32,16,128]{2,1,0:T(8,128)S(1)}) custom-call(f32[64,1024]{1,0:T(8,128)S(1)} %collect.1.data_ref, f32[8,4,4,2,64,128]{5,4,3,2,1,0:T(8,128)S(1)} %bitcast.8), custom_call_target="tpu_custom_call" | custom-call | flops 800000000 | bytes 9000000 | tf_op jit(solution)/shard_map/first_adjoint/pallas_call | solution.py:219
  88.3 15.2 %all_to_all.32.in_ref = f32[32,16,128]{2,1,0:T(8,128)S(1)} all-to-all(f32[32,16,128]{2,1,0:T(8,128)S(1)} %get-tuple-element.11), channel_id=1, replica_groups=mesh['xl'=2,'z'=4,'core'=2,'y'=4,'xh'=2] {'y','xh','xl','core'}, dimensions={0} | all-to-all | bytes 524288 | tf_op jit(solution)/shard_map/all_to_all | solution.py:454
  103.6 0.0 copy-done.1
  103.6 11.9 %second.1 = (f32[64,1024]{1,0:T(8,128)S(1)}, f32[64,1024]{1,0:T(8,128)S(1)}, f32[64,1024]{1,0:T(8,128)S(1)}, f32[32,24,128]{2,1,0:T(8,128)S(1)}) custom-call(f32[64,1024]{1,0:T(8,128)S(1)} %get-tuple-element.10.field_ref, f32[32,16,128]{2,1,0:T(8,128)S(1)} %all_to_all.32.in_ref, f32[8,4,4,2,64,128]{5,4,3,2,1,0:T(8,128)S(1)} %bitcast.9), custom_call_target="tpu_custom_call" | custom-call | flops 1600000000 | bytes 18000000 | tf_op jit(solution)/shard_map/second/pallas_call | solution.py:266
  115.4 13.7 %all_to_all.33.in_ref = f32[32,24,128]{2,1,0:T(8,128)S(1)} all-to-all(f32[32,24,128]{2,1,0:T(8,128)S(1)} %get-tuple-element.14), channel_id=1, replica_groups=mesh['xl'=2,'z'=4,'core'=2,'y'=4,'xh'=2] {'y','xh','xl','core'}, dimensions={0} | all-to-all | bytes 786432 | tf_op jit(solution)/shard_map/all_to_all | solution.py:456
  129.2 1.1 join.1.pair_ref
  130.2 0.0 all-gather.5.cloned.1.call-update
  130.3 0.0 copy-start.2
  130.3 3.4 %copy-done.2 = f32[16384,128]{1,0:T(8,128)S(1)} copy-done((f32[16384,128]{1,0:T(8,128)S(1)}, f32[16384,128]{1,0:T(8,128)}, u32[]{:S(2)}) %copy-start.2) | copy-done | bytes 8388632
  133.6 10.1 %change.1 = (f32[64,1024]{1,0:T(8,128)S(1)}, f32[32,8,128]{2,1,0:T(8,128)S(1)}) custom-call(f32[128,1024]{1,0:T(8,128)} %join.1.pair_ref, f32[64,1024]{1,0:T(8,128)S(1)} %get-tuple-element.15.image_ref, f32[32,24,128]{2,1,0:T(8,128)S(1)} %all_to_all.33.in_ref, f32[8,4,4,2,64,128]{5,4,3,2,1,0:T(8,128)S(1)} %bitcast.10), custom_call_target="tpu_custom_call" | custom-call | flops 800000000 | bytes 9000000 | tf_op jit(solution)/shard_map/change/pallas_call | solution.py:337
  143.7 12.7 %all_to_all.34.sums_ref = f32[32,8,128]{2,1,0:T(8,128)S(1)} all-to-all(f32[32,8,128]{2,1,0:T(8,128)S(1)} %get-tuple-element.17), channel_id=1, replica_groups=mesh['xl'=2,'z'=4,'core'=2,'y'=4,'xh'=2] {'y','xh','xl','core'}, dimensions={0} | all-to-all | bytes 262144 | tf_op jit(solution)/shard_map/all_to_all | solution.py:460
  156.4 0.5 residual.1
  156.9 16.0 %all_to_all.35.in_ref = f32[16,40,128]{2,1,0:T(8,128)S(1)} all-to-all(f32[16,40,128]{2,1,0:T(8,128)S(1)} %residual.1), channel_id=1, replica_groups=mesh['xl'=2,'z'=4,'core'=2,'y'=4,'xh'=2] {'xl','z','core'}, dimensions={0} | all-to-all | bytes 655360 | tf_op jit(solution)/shard_map/all_to_all | solution.py:461
  172.8 1.0 place.1
  173.8 11.3 %all-gather.5.cloned.1.call-done = f32[2048,1024]{1,0:T(8,128)} async-done(((f32[128,1024]{1,0:T(8,128)}), f32[2048,1024]{1,0:T(8,128)}) %all-gather.5.cloned.1.call-update) | async-done | bytes 8388624 | tf_op jit(solution)/shard_map/all_gather | solution.py:458
  185.1 0.0 copy-start.4
  185.1 3.4 %copy-done.4 = f32[2048,1024]{1,0:T(8,128)S(1)} copy-done((f32[2048,1024]{1,0:T(8,128)S(1)}, f32[2048,1024]{1,0:T(8,128)}, u32[]{:S(2)}) %copy-start.4) | copy-done | bytes 8388632
  188.5 4.6 %combine.1 = f32[4,2,1024,128]{3,2,1,0:T(8,128)} custom-call(f32[2,4,2,2,2,32,1024]{6,5,4,3,2,1,0:T(8,128)S(1)} %bitcast.12, f32[2,4,2,40,128]{4,3,2,1,0:T(8,128)S(1)} %bitcast.13), custom_call_target="tpu_custom_call" | custom-call | flops 10000000 | bytes 12000000 | tf_op jit(solution)/shard_map/combine/pallas_call | solution.py:424
  (5 shorter events, 0.0 us)
Async XLA Ops:
  7.2 74.8 %all-gather.3.cloned.1.call-start = ((), (), s32[]{:S(2)}) async-start(), calls=%async_computation.6 | async-start | bytes 8650752 | tf_op jit(solution)/shard_map/all_gather | solution.py:441
  18.8 166.3 %all-gather.5.cloned.1.call-start = ((), (), s32[]{:S(2)}) async-start(), calls=%async_computation.7 | async-start | bytes 8912896 | tf_op jit(solution)/shard_map/all_gather | solution.py:458
  20.6 3.4 %copy-start.3 = (bf16[1024,32,128]{2,1,0:T(8,128)(2,1)S(1)}, bf16[1024,32,128]{2,1,0:T(8,128)(2,1)}, u32[]{:S(2)}) copy-start(bf16[1024,32,128]{2,1,0:T(8,128)(2,1)} %param.4) | copy-start | bytes 25165828
  82.0 3.4 %copy-start = (f32[16384,128]{1,0:T(8,128)S(1)}, f32[16384,128]{1,0:T(8,128)}, u32[]{:S(2)}) copy-start(f32[16384,128]{1,0:T(8,128)} %all-gather.3.cloned.1.call-done) | copy-start | bytes 25165828
  85.3 18.2 %copy-start.1 = (f32[16384,128]{1,0:T(8,128)S(1)}, f32[16384,128]{1,0:T(8,128)}, u32[]{:S(2)}) copy-start(f32[16384,128]{1,0:T(8,128)} %all-gather.3.cloned.1.call-done) | copy-start | bytes 25165828
  130.3 3.4 %copy-start.2 = (f32[16384,128]{1,0:T(8,128)S(1)}, f32[16384,128]{1,0:T(8,128)}, u32[]{:S(2)}) copy-start(f32[16384,128]{1,0:T(8,128)} %all-gather.3.cloned.1.call-done) | copy-start | bytes 25165828
  185.1 3.4 %copy-start.4 = (f32[2048,1024]{1,0:T(8,128)S(1)}, f32[2048,1024]{1,0:T(8,128)}, u32[]{:S(2)}) copy-start(f32[2048,1024]{1,0:T(8,128)} %all-gather.5.cloned.1.call-done) | copy-start | bytes 25165828
Sparse Core Ops, SparseCore 0:
  18.9 63.0 all-gather.2
  130.4 54.6 all-gather.4

commit v3 on v2

v3 whole, which is shorter than its diff:
```python
import math

import jax
import jax.numpy as jnp
from jax import lax
from jax.experimental import pallas as pl
from jax.experimental.pallas import tpu as pltpu
from jax.sharding import Mesh, PartitionSpec as P

NODES = 1024
NT = 512
F = 4
SHOT = ("xl", "z", "core")
NODE = ("y", "xh")
CHIPS = ("xl", "z")
PLANE_CHIPS = ("y", "xh", "xl")
PLANE = ("y", "xh", "xl", "core")
BF = jnp.bfloat16
F32 = jnp.float32
SMALL = pltpu.CompilerParams(vmem_limit_bytes=16 * 1024 * 1024)
LARGE = pltpu.CompilerParams(vmem_limit_bytes=32 * 1024 * 1024)
FULL = pltpu.CompilerParams(vmem_limit_bytes=58 * 1024 * 1024)


def local_table(freq_idx, first, count):
    sample = first + jnp.arange(count, dtype=jnp.int32)
    product = freq_idx[:, None] * sample[None, :] % NT
    angle = product.astype(F32) * (2.0 * math.pi / NT)
    stacked = jnp.stack([jnp.cos(angle), -jnp.sin(angle)], axis=1)
    return stacked.reshape(2 * F, count).astype(BF)


def struct(shape, dtype=F32):
    return jax.ShapeDtypeStruct(shape, dtype)


def cost(flops, moved):
    return pl.CostEstimate(flops=flops, bytes_accessed=moved, transcendentals=0)


def split(x):
    high = x.astype(BF)
    return high, (x - high.astype(F32)).astype(BF)


def stacked_split(x):
    return jnp.concatenate(split(x), axis=0)


def dot(a, b):
    return lax.dot_general(a, b, (((1,), (0,)), ((), ())), preferred_element_type=F32)


def whole(shape):
    return pl.BlockSpec(shape, lambda *_: (0,) * len(shape))


def exponent_of(peak):
    return jnp.floor(jnp.log(jnp.maximum(peak, 1e-30)) * (1.0 / math.log(2.0))) - 14.0


def code(x):
    return jnp.clip(jnp.floor(x + 0.5), -32767.0, 32767.0).astype(jnp.int32).astype(jnp.int16)


def peak_of(x):
    return jnp.max(jnp.abs(x), axis=(0, 1), keepdims=True)


def exponent_tile(rows, lanes):
    rows = [jnp.broadcast_to(r, (1, lanes)) for r in rows]
    rows.append(jnp.zeros((16 - len(rows), lanes), F32))
    return jnp.concatenate(rows, axis=0).astype(jnp.int32).astype(jnp.int16)


def lanes_sum(x):
    total = x[:, :128]
    for i in range(1, x.shape[1] // 128):
        total = total + x[:, i * 128 : (i + 1) * 128]
    return jnp.sum(total, axis=0, keepdims=True)


def total(rows):
    return jnp.sum(rows, axis=(0, 1), keepdims=True)


def transform_body(
    up_ref, table_ref, inverse_ref, mine_ref, other_ref, sums, exponents, held, arrived
):
    block = pl.program_id(0)
    me = lax.axis_index("core")

    def fetch(i):
        source = up_ref.at[i // 4, pl.ds(i % 2 * 2, 2), i // 2 % 2]
        return pltpu.make_async_copy(source, held.at[i], arrived.at[i])

    @pl.when(block == 0)
    def _():
        for i in range(8):
            fetch(i).start()

    fetch(block).wait()
    index = jnp.broadcast_to(inverse_ref[0:1, :], (64, 128))
    largest = jnp.zeros((64, 128), F32)
    for part in range(2):
        for group in range(4):
            row = group * 16
            x = [held[block, part, row + h * 8 : row + h * 8 + 8].reshape(256, 128) for h in range(2)]
            both = dot(table_ref[...], jnp.concatenate(x, axis=1))
            for h in range(2):
                y = jnp.take_along_axis(both[:, h * 128 : h * 128 + 128], index, axis=1)
                largest = jnp.maximum(largest, jnp.abs(y))
                at = part * 64 + row + h * 8
                for fc in range(8):
                    sums[fc, at : at + 8, :] = y[fc * 8 : fc * 8 + 8]
    exponent = exponent_of(peak_of(largest))
    scale = jnp.exp2(-exponent)
    exponents[pl.ds(block, 1), :] = jnp.broadcast_to(exponent, (1, 128))
    rows = pl.multiple_of(block * 64, 64)
    for fc in range(8):
        turned = sums[fc].T * scale
        at = pl.ds(rows + (fc % 2) * 32, 32)
        for x in range(2):
            first, second_ = (turned[x * 64 + c * 32 : x * 64 + c * 32 + 32] for c in range(2))
            mine_ref[x * 4 + fc // 2, at, :] = code(jnp.where(me == 0, first, second_))
            other_ref[x * 4 + fc // 2, at, :] = code(jnp.where(me == 0, second_, first))

    @pl.when(block == 7)
    def _():
        coded = exponent_tile([exponents[i : i + 1, :] for i in range(8)], 128)
        for dest in range(8):
            mine_ref[dest, 512:528, :] = coded
            other_ref[dest, 512:528, :] = coded


def transform(up_time, table, inverse):
    return pl.pallas_call(
        transform_body,
        grid=(8,),
        in_specs=[
            pl.BlockSpec(memory_space=pl.ANY),
            whole((64, 256)),
            whole((8, 128)),
        ],
        out_specs=[whole((8, 528, 128))] * 2,
        out_shape=[struct((8, 528, 128), jnp.int16)] * 2,
        scratch_shapes=[
            pltpu.VMEM((8, 128, 128), F32),
            pltpu.VMEM((8, 128), F32),
            pltpu.VMEM((8, 2, 64, 32, 128), BF),
            pltpu.SemaphoreType.DMA((8,)),
        ],
        compiler_params=FULL,
        cost_estimate=cost(600_000_000, 10_000_000),
        name="transform",
    )(up_time.reshape(2, 4, 2, 64, 32, 128), table, inverse)


def merge_body(mine_ref, other_ref, out_ref):
    scales = [jnp.exp2(r[0, 512:528, :].astype(F32)) for r in (mine_ref, other_ref)]
    exponents = []
    for block in range(8):
        rows = slice(block * 64, block * 64 + 64)
        sums, largest = [], jnp.zeros((64, 128), F32)
        for dest in range(8):
            mine = mine_ref[dest, rows, :].astype(F32) * scales[0][block : block + 1]
            sums.append(mine + other_ref[dest, rows, :].astype(F32) * scales[1][block : block + 1])
            largest = jnp.maximum(largest, jnp.abs(sums[-1]))
        exponents.append(exponent_of(peak_of(largest)))
        scale = jnp.exp2(-exponents[-1])
        for dest in range(8):
            out_ref[dest, rows, :] = code(sums[dest] * scale)
    coded = exponent_tile(exponents, 128)
    for dest in range(8):
        out_ref[dest, 512:528, :] = coded


def merge(pieces, other):
    return pl.pallas_call(
        merge_body,
        out_shape=struct((8, 528, 128), jnp.int16),
        compiler_params=SMALL,
        cost_estimate=cost(10_000_000, 3_000_000),
        name="merge",
    )(pieces, other)


def collect_body(in_ref, out_ref):
    scales = [jnp.exp2(in_ref[i, 512:528, :].astype(F32)) for i in range(8)]
    for block in range(8):
        summed = jnp.zeros((64, 128), F32)
        for i in range(8):
            piece = in_ref[i, block * 64 : block * 64 + 64, :].astype(F32)
            summed = summed + piece * scales[i][block : block + 1]
        out_ref[:, block * 128 : block * 128 + 128] = summed


def collect(received):
    return pl.pallas_call(
        collect_body,
        out_shape=struct((64, 1024)),
        compiler_params=SMALL,
        cost_estimate=cost(5_000_000, 2_000_000),
        name="collect",
    )(received)


def code_down_body(in_ref, out_ref):
    for f in range(F):
        field = in_ref[f].reshape(128, 128)
        exponent = exponent_of(peak_of(field))
        out_ref[f, 0:128, :] = code(field * jnp.exp2(-exponent))
        out_ref[f, 128:144, :] = exponent_tile([exponent], 128)


def code_down(downgoing):
    return pl.pallas_call(
        code_down_body,
        out_shape=struct((F, 144, 128), jnp.int16),
        compiler_params=SMALL,
        cost_estimate=cost(1_000_000, 500_000),
        name="code_down",
    )(downgoing)


def adjoint_step(down_ref, both):
    sums = []
    for c in range(2):
        first = dot(both, down_ref[0, c])
        sums.append(first[:64] + first[64:] + dot(both[:64], down_ref[1, c]))
    real = sums[0][:32] + sums[1][32:]
    imaginary = sums[0][32:] - sums[1][:32]
    return jnp.concatenate([real, imaginary], axis=0)


def forward_step(down_ref, both):
    sums = []
    for c in range(2):
        first = dot(down_ref[0, c], both) + dot(down_ref[1, c], both)
        sums.append((first[:, :64] + first[:, 64:]).T)
    real = sums[0][:32] - sums[1][32:]
    imaginary = sums[0][32:] + sums[1][:32]
    return jnp.concatenate([real, imaginary], axis=0)


def side_split(field):
    return jnp.concatenate(split(field.T), axis=1)


def pack(field, out_ref, first):
    turned = field.T
    for k in range(8):
        piece = turned[k * 32 : k * 32 + 32]
        out_ref[first + k, 0:16, :] = jnp.concatenate([piece[:16], piece[16:]], axis=1)


def unpack(in_ref, first):
    pieces = [in_ref[first + k, 0:16, :] for k in range(4)]
    rows = []
    for c in range(2):
        for half in range(2):
            at = half * 64 + c * 32
            rows.append(jnp.concatenate([p[:, at : at + 32] for p in pieces], axis=1))
    return jnp.concatenate(rows, axis=0)


def symmetric(field, in_ref, first):
    mirrored = jnp.concatenate([unpack(in_ref, first), unpack(in_ref, first + 4)], axis=1)
    return (field + mirrored) * 0.5


BY_NODES = (2, 2, 1024, 256)
BY_SHOTS = (2, 2, 256, 1024)


def decode_body(mine_ref, other_ref, down_ref):
    me = lax.axis_index("core")
    for source, core in ((mine_ref, me), (other_ref, 1 - me)):
        for n in range(2):
            for x in range(2):
                for z in range(4):
                    scale = jnp.exp2(source[n, x, z, 128:144, :].astype(F32))[0:1]
                    first = x * 512 + core * 256 + z * 64
                    rows = pl.ds(pl.multiple_of(first, 64), 64)
                    for c in range(2):
                        field = source[n, x, z, c * 64 : c * 64 + 64, :].astype(F32) * scale
                        high, low = split(field)
                        down_ref[0, c, rows, n * 128 : n * 128 + 128] = high
                        down_ref[1, c, rows, n * 128 : n * 128 + 128] = low


def decode(mine, other):
    block = pl.BlockSpec((2, 2, 4, 144, 128), lambda j: (j, 0, 0, 0, 0))
    return pl.pallas_call(
        decode_body,
        grid=(4,),
        in_specs=[block, block],
        out_specs=pl.BlockSpec(BY_NODES, lambda j: (0, 0, 0, j)),
        out_shape=struct((2, 2, 1024, 1024), BF),
        compiler_params=LARGE,
        cost_estimate=cost(20_000_000, 13_000_000),
        name="decode",
    )(mine.reshape(8, 2, 4, 144, 128), other.reshape(8, 2, 4, 144, 128))


def first_adjoint_body(data_ref, by_nodes_ref, field_ref, pieces_ref, both):
    @pl.when(pl.program_id(0) == 0)
    def _():
        both[...] = stacked_split(data_ref[...])

    field = adjoint_step(by_nodes_ref, both[...])
    field_ref[...] = field
    pack(field, pieces_ref, 0)


def first_adjoint(data, down):
    return pl.pallas_call(
        first_adjoint_body,
        grid=(4,),
        in_specs=[whole((64, 1024)), pl.BlockSpec(BY_NODES, lambda j: (0, 0, 0, j))],
        out_specs=[
            pl.BlockSpec((64, 256), lambda j: (0, j)),
            pl.BlockSpec((8, 16, 128), lambda j: (j, 0, 0)),
        ],
        out_shape=[struct((64, 1024)), struct((32, 16, 128))],
        scratch_shapes=[pltpu.VMEM((128, 1024), BF)],
        compiler_params=LARGE,
        cost_estimate=cost(800_000_000, 9_000_000),
        name="first_adjoint",
    )(data, down)


def second_body(
    field_ref, in_ref, by_shots_ref, by_nodes_ref, gradient_ref, image_ref, again_ref, out_ref,
    side, both, norm,
):
    phase, j = pl.program_id(0), pl.program_id(1)
    lanes = pl.ds(pl.multiple_of(j * 256, 256), 256)

    @pl.when((phase == 0) & (j == 0))
    def _():
        for i in range(4):
            at = slice(i * 256, i * 256 + 256)
            gradient = symmetric(field_ref[:, at], in_ref, i * 8)
            gradient_ref[:, at] = gradient
            side[at, :] = side_split(gradient)
        gradient = gradient_ref[...]
        norm[...] = jnp.zeros((8, 128), F32)
        norm[0:1, :] = lanes_sum(gradient * gradient)

    @pl.when(phase == 0)
    def _():
        image = forward_step(by_shots_ref, side[...])
        image_ref[:, lanes] = image
        both[:, lanes] = stacked_split(image)
        norm[1:2, :] += lanes_sum(image * image)

    @pl.when(phase == 1)
    def _():
        field = adjoint_step(by_nodes_ref, both[...])
        again_ref[:, lanes] = field
        pack(field, out_ref, j * 8)
        for k in range(8):
            out_ref[j * 8 + k, 16:24, :] = norm[...]


def second(field, received, down):
    return pl.pallas_call(
        second_body,
        grid=(2, 4),
        in_specs=[
            whole((64, 1024)),
            whole((32, 16, 128)),
            pl.BlockSpec(BY_SHOTS, lambda p, j: (0, 0, jnp.where(p == 0, j, 3), 0)),
            pl.BlockSpec(BY_NODES, lambda p, j: (0, 0, 0, jnp.where(p == 0, 0, j))),
        ],
        out_specs=[whole((64, 1024))] * 3 + [whole((32, 24, 128))],
        out_shape=[struct((64, 1024))] * 3 + [struct((32, 24, 128))],
        scratch_shapes=[
            pltpu.VMEM((1024, 128), BF),
            pltpu.VMEM((128, 1024), BF),
            pltpu.VMEM((8, 128), F32),
        ],
        compiler_params=LARGE,
        cost_estimate=cost(1_600_000_000, 18_000_000),
        name="second",
    )(field, received, down, down)


def first_step(in_ref):
    norm = total(jnp.sum(in_ref[:, 16:17, :], axis=0))
    curvature = total(jnp.sum(in_ref[:, 17:18, :], axis=0))
    return norm, curvature


def change_body(
    gradient_ref, field_ref, image_ref, in_ref, by_shots_ref, again_ref, change_ref, out_ref, side, sums
):
    j = pl.program_id(0)
    lanes = pl.ds(pl.multiple_of(j * 256, 256), 256)
    norm, curvature = first_step(in_ref)
    step = norm / curvature

    @pl.when(j == 0)
    def _():
        for i in range(4):
            at = slice(i * 256, i * 256 + 256)
            again = symmetric(field_ref[:, at], in_ref, i * 8)
            again_ref[:, at] = again
            side[at, :] = side_split(again)
        sums[...] = jnp.zeros((8, 128), F32)
        gradient = gradient_ref[...] - step * again_ref[...]
        sums[0:1, :] = lanes_sum(gradient * gradient)

    image = image_ref[:, lanes]
    change = image - step * forward_step(by_shots_ref, side[...])
    change_ref[:, lanes] = change
    sums[1:2, :] += lanes_sum(change * change)
    sums[2:3, :] += lanes_sum(change * image)

    @pl.when(j == 3)
    def _():
        for i in range(32):
            out_ref[i] = sums[...]


def changed(gradient, field, image, received, down):
    return pl.pallas_call(
        change_body,
        grid=(4,),
        in_specs=[
            whole((64, 1024)),
            whole((64, 1024)),
            whole((64, 1024)),
            whole((32, 24, 128)),
            pl.BlockSpec(BY_SHOTS, lambda j: (0, 0, j, 0)),
        ],
        out_specs=[whole((64, 1024)), whole((64, 1024)), whole((32, 8, 128))],
        out_shape=[struct((64, 1024)), struct((64, 1024)), struct((32, 8, 128))],
        scratch_shapes=[pltpu.VMEM((1024, 128), BF), pltpu.VMEM((8, 128), F32)],
        compiler_params=LARGE,
        cost_estimate=cost(800_000_000, 9_000_000),
        name="change",
    )(gradient, field, image, received, down)


def update_body(
    data_ref, gradient_ref, again_ref, image_ref, change_ref, in_ref, sums_ref, out_ref
):
    norm, curvature = first_step(in_ref)
    step = norm / curvature
    rows = jnp.sum(sums_ref[...], axis=0)
    new_norm, change_change, change_image = (total(rows[i : i + 1]) for i in range(3))
    beta = new_norm / norm
    new_step = new_norm / (change_change + 2.0 * beta * change_image + beta * beta * curvature)
    gradient, image = gradient_ref[...], image_ref[...]
    direction = (gradient - step * again_ref[...]) + beta * gradient
    result = step * gradient + new_step * direction
    left = data_ref[...] - step * image - new_step * (change_ref[...] + beta * image)
    exponents = [exponent_of(peak_of(result)), exponent_of(peak_of(left))]
    coded = code(result * jnp.exp2(-exponents[0]))
    turned = (left * jnp.exp2(-exponents[1])).T
    tile = exponent_tile(exponents, 128)
    for dest in range(8):
        for j in range(8):
            out_ref[dest, j * 64 : j * 64 + 64, :] = coded[:, j * 128 : j * 128 + 128]
        for core in range(2):
            at = (dest // 4 * 2 + core) * 256 + dest % 4 * 64
            piece = jnp.concatenate([turned[at : at + 32], turned[at + 32 : at + 64]], axis=1)
            out_ref[dest, 512 + core * 32 : 544 + core * 32, :] = code(piece)
        out_ref[dest, 576:592, :] = tile


def updated(data, gradient, again, image, change, received, sums):
    return pl.pallas_call(
        update_body,
        out_shape=struct((8, 592, 128), jnp.int16),
        compiler_params=SMALL,
        cost_estimate=cost(5_000_000, 3_000_000),
        name="update",
    )(data, gradient, again, image, change, received, sums)


def finish_body(mine_ref, other_ref, reflectivity_ref, residual_ref, held, arrived):
    f = pl.program_id(0)
    me = lax.axis_index("core")

    def fetch(i, x, k):
        source = (mine_ref, other_ref)[k].at[x, i]
        slot = me if k == 0 else 1 - me
        return pltpu.make_async_copy(source, held.at[i, x, slot], arrived.at[i, x, k])

    @pl.when(f == 0)
    def _():
        for i in range(F):
            for x in range(2):
                for k in range(2):
                    fetch(i, x, k).start()

    for x in range(2):
        for k in range(2):
            fetch(f, x, k).wait()

    scales = []
    for k in range(4):
        scales.append(jnp.exp2(held[f, k // 2, k % 2, 576:592, :].astype(F32)))
    for c in range(2):
        for j in range(8):
            at = slice(j * 64 + c * 32, j * 64 + c * 32 + 32)
            parts = [held[f, k // 2, k % 2, at, :].astype(F32) * scales[k][0:1] for k in range(4)]
            whole_rows = jnp.concatenate(parts, axis=0)
            reflectivity_ref[0, c, j * 128 : j * 128 + 128, :] = whole_rows.T
    first = pl.multiple_of(512 + me * 32, 32)
    pieces = [
        held[f, k // 2, k % 2, pl.ds(first, 32), :].astype(F32) * scales[k][1:2] for k in range(4)
    ]
    for c in range(2):
        for half in range(2):
            at = half * 64 + c * 32
            row = jnp.concatenate([p[:, at : at + 32] for p in pieces], axis=1)
            residual_ref[0, c, half * 32 : half * 32 + 32, :] = row


def finish(mine, other):
    return pl.pallas_call(
        finish_body,
        grid=(F,),
        in_specs=[pl.BlockSpec(memory_space=pl.ANY)] * 2,
        out_specs=[
            pl.BlockSpec((1, 2, 1024, 128), lambda f: (f, 0, 0, 0)),
            pl.BlockSpec((1, 2, 64, 128), lambda f: (f, 0, 0, 0)),
        ],
        out_shape=[struct((F, 2, 1024, 128)), struct((F, 2, 64, 128))],
        scratch_shapes=[
            pltpu.VMEM((F, 2, 2, 592, 128), jnp.int16),
            pltpu.SemaphoreType.DMA((F, 2, 2)),
        ],
        compiler_params=LARGE,
        cost_estimate=cost(10_000_000, 7_000_000),
        name="finish",
    )(mine.reshape(2, F, 592, 128), other.reshape(2, F, 592, 128))


def swap_cores(x):
    return lax.ppermute(x, "core", [(0, 1), (1, 0)])


def shards(up_time, downgoing, freq_idx, node_map):
    own = lax.all_to_all(code_down(downgoing), "z", 0, 0, tiled=True)
    mine = lax.all_gather(own.reshape(576, 128), PLANE_CHIPS, axis=0, tiled=True)
    down = decode(mine, swap_cores(mine))

    count = up_time.shape[1]
    table = local_table(freq_idx, lax.axis_index(SHOT) * count, count)
    table = table[:, None, None, :] * jnp.eye(8, dtype=BF)[None, :, :, None]
    slots = jnp.arange(128, dtype=jnp.int32)
    inverse = jnp.sum(jnp.where(node_map[:, None] == slots[None, :], slots[:, None], 0), axis=0)
    inverse = jnp.broadcast_to(inverse[None, :], (8, 128))
    pieces, others = transform(up_time, table.reshape(64, 256), inverse)
    pieces = merge(pieces, swap_cores(others))
    data = collect(lax.all_to_all(pieces, CHIPS, 0, 0, tiled=True))

    field, pieces = first_adjoint(data, down)
    received = lax.all_to_all(pieces, PLANE, 0, 0, tiled=True)
    gradient, image, field, pieces = second(field, received, down)
    received = lax.all_to_all(pieces, PLANE, 0, 0, tiled=True)
    again, change, sums = changed(gradient, field, image, received, down)
    sums = lax.all_to_all(sums, PLANE, 0, 0, tiled=True)
    pieces = updated(data, gradient, again, image, change, received, sums)
    mine = lax.all_to_all(pieces, CHIPS, 0, 0, tiled=True)
    return tuple(finish(mine, swap_cores(mine)))


def solution(mesh):
    fine = Mesh(mesh.devices.reshape(2, 4, 2, 4, 2), SHOT + NODE)
    return jax.shard_map(
        shards,
        mesh=fine,
        in_specs=(P(None, SHOT, NODE), P(None, None, SHOT, NODE), P(), P(NODE)),
        out_specs=(P(None, None, None, NODE), P(None, None, SHOT, NODE)),
        check_vma=False,
    )
```

time: 201 us -> 173 us (0.86)
  starting transfers between devices: 0.08 us -> 14.9 us
  between operations: 14.1 us -> 0.74 us
  blocking collectives: 114 us -> 101 us
  local copies, waits for them, and re-layouts: 13.7 us -> 3.54 us
  waiting for transfers between devices: 18.2 us -> 9.53 us
  Pallas kernels: 38.6 us -> 41.5 us
    all_to_all x3 -> x2, blocking collectives: 71.9 us -> 37.2 us  [the longest x1 18.9 us: shards(): mine = lax.all_to_all(pieces, CHIPS, 0, 0, tiled=True)]
    all_gather x0 -> x1, blocking collectives: none -> 23.7 us  [shards(): lax.all_gather(own.reshape(576, 128), PLANE_CHIPS, axis=0, tiled=True)]
    all_gather x2 -> x0, waiting for transfers between devices: 18.2 us -> none  [the longest x1 11.3 us: shards(): pairs = lax.all_gather(pair, SHOT, axis=0, tiled=True)]
    unnamed x10 -> x6, local copies, waits for them, and re-layouts: 13.5 us -> 2.18 us
    ppermute x0 -> x3, starting transfers between devices: none -> 9.09 us  [swap_cores(): return lax.ppermute(x, 'core', [(0, 1), (1, 0)])]
    all_to_all x0 -> x1, starting transfers between devices: none -> 5.86 us  [shards(): own = lax.all_to_all(code_down(downgoing), 'z', 0, 0, tiled=True)]
    pallas_call x6 -> x7, Pallas kernels: 23.2 us -> 28.8 us  [the longest x1 9.25 us: transform(): pl.pallas_call(transform_body, grid=(8,), in_specs=[pl.BlockSpec(memory_s...]
    ppermute x0 -> x3, waiting for transfers between devices: none -> 5.43 us  [swap_cores(): return lax.ppermute(x, 'core', [(0, 1), (1, 0)])]
  transfers between devices with their start and end apart: 2 -> 4, of which waited for: 2 -> 3; matrix products, arithmetic and copies ran while one was open for 1% -> 1% of each run, Pallas kernels for 9% -> 6%
where the time goes in v3:
time: 173 us; the launch traced here: 172 us
  blocking collectives  101 us (58%)
  Pallas kernels  41.5 us (24%)
  starting transfers between devices  14.9 us (9%)
  waiting for transfers between devices  9.53 us (6%)
  local copies, waits for them, and re-layouts  3.54 us (2%)
    all_to_all x2, blocking collectives, shards(): received = lax.all_to_all(pieces, PLANE, 0, 0, tiled=True)  28.9 us
    all_gather x1, blocking collectives, shards(): lax.all_gather(own.reshape(576, 128), PLANE_CHIPS, axis=0, tiled=True)  23.7 us
    all_to_all x1, blocking collectives, shards(): mine = lax.all_to_all(pieces, CHIPS, 0, 0, tiled=True)  18.9 us
    all_to_all x1, blocking collectives, shards(): data = collect(lax.all_to_all(pieces, CHIPS, 0, 0, tiled=True))  18.4 us
    all_to_all x1, blocking collectives, shards(): sums = lax.all_to_all(sums, PLANE, 0, 0, tiled=True)  11.2 us
    pallas_call x1, Pallas kernels, transform(): pl.pallas_call(transform_body, grid=(8,), in_specs=[pl.BlockSpec(memory_s...  9.25 us
    ppermute x3, starting transfers between devices, swap_cores(): return lax.ppermute(x, 'core', [(0, 1), (1, 0)])  9.09 us
    pallas_call x1, Pallas kernels, second(): pl.pallas_call(second_body, grid=(2, 4), in_specs=[whole((64, 1024)), who...  8.75 us
  transfers between devices with their start and end apart: 4, of which 3 were waited for; matrix products, arithmetic and copies ran while one was open for 1% of the time, Pallas kernels for 6%

profile of v3, /device:TPU:1, one launch (start us, length us, event | category | flops | bytes accessed | tf_op | source)
XLA Modules:
  0.0 172.2 jit_solution(17222689086341302369)
XLA Ops:
  0.6 0.0 copy-start.1
  0.6 0.9 copy-done.1
  1.6 0.9 code_down.1
  2.4 5.9 %all-to-all-start.1 = ((s16[4,144,128]{2,1,0:T(8,128)(2,1)}), s16[4,144,128]{2,1,0:T(8,128)(2,1)S(1)}, u32[]{:S(2)}, u32[]{:S(2)}) async-start(s16[4,144,128]{2,1,0:T(8,128)(2,1)} %code_down.1), calls=%async_computation.1 | async-start | bytes 294912 | tf_op jit(solution)/shard_map/all_to_all | solution.py:549
  8.3 0.8 cosine_convert_fusion
  9.1 4.1 %all-to-all-done.1 = s16[4,144,128]{2,1,0:T(8,128)(2,1)S(1)} async-done(((s16[4,144,128]{2,1,0:T(8,128)(2,1)}), s16[4,144,128]{2,1,0:T(8,128)(2,1)S(1)}, u32[]{:S(2)}, u32[]{:S(2)}) %all-to-all-start.1) | async-done | bytes 147488 | tf_op jit(solution)/shard_map/all_to_all | solution.py:549
  13.2 0.0 copy-start.2
  13.2 23.7 %all-gather.1 = s16[9216,128]{1,0:T(8,128)(2,1)S(1)} all-gather(s16[576,128]{1,0:T(8,128)(2,1)S(1)} %bitcast.13), channel_id=1, replica_groups=mesh['xl'=2,'z'=4,'core'=2,'y'=4,'xh'=2] {'y','xh','xl'}, dimensions={0}, use_global_device_ids=true | all-gather | bytes 2506752 | tf_op jit(solution)/shard_map/all_gather | solution.py:550
  36.9 7.0 %collective-permute-start.1 = (s16[9216,128]{1,0:T(8,128)(2,1)S(1)}, s16[9216,128]{1,0:T(8,128)(2,1)}, u32[]{:S(2)}, u32[]{:S(2)}) collective-permute-start(s16[9216,128]{1,0:T(8,128)(2,1)S(1)} %all-gather.1), channel_id=1, source_target_pairs={{0,8},{8,0},{1,9},{9,1},{2,10},{10,2},{3,11},{11,3},{4,12},{12,4},... | collective-permute-start | bytes 7077896 | tf_op jit(solution)/shard_map/ppermute | solution.py:545
  43.9 0.1 broadcast_multiply_fusion
  44.0 0.8 mul.78.table_ref
  44.8 0.0 copy-done.2
  44.8 0.1 select_reduce_fusion
  44.9 0.6 broadcast_in_dim.16.inverse_ref
  45.5 9.2 %transform.1 = (s16[8,528,128]{2,1,0:T(8,128)(2,1)}, s16[8,528,128]{2,1,0:T(8,128)(2,1)}) custom-call(bf16[2,4,2,64,32,128]{5,4,3,2,1,0:T(8,128)(2,1)} %bitcast.12, bf16[64,256]{1,0:T(8,128)(2,1)} %mul.78.table_ref, s32[8,128]{1,0:T(8,128)} %broadcast_in_dim.16.inverse_ref), custom_call_target="tpu_custom_call" | custom-call | flops 600000000 | bytes 10000000 | tf_op jit(solution)/shard_map/transform/pallas_call | solution.py:137
  54.7 0.1 collective-permute-start
  54.8 2.9 %collective-permute-done.other_ref = s16[8,528,128]{2,1,0:T(8,128)(2,1)S(1)} collective-permute-done((s16[8,528,128]{2,1,0:T(8,128)(2,1)}, s16[8,528,128]{2,1,0:T(8,128)(2,1)S(1)}, u32[]{:S(2)}, u32[]{:S(2)}) %collective-permute-start) | collective-permute-done | bytes 1081376 | tf_op jit(solution)/shard_map/ppermute | solution.py:545
  57.7 0.0 copy-start
  57.7 1.2 copy-done
  58.9 1.2 merge.1
  60.2 18.4 %all_to_all.30.in_ref = s16[8,528,128]{2,1,0:T(8,128)(2,1)S(1)} all-to-all(s16[8,528,128]{2,1,0:T(8,128)(2,1)S(1)} %merge.1), channel_id=1, replica_groups=mesh['xl'=2,'z'=4,'core'=2,'y'=4,'xh'=2] {'xl','z'}, dimensions={0} | all-to-all | bytes 2162688 | tf_op jit(solution)/shard_map/all_to_all | solution.py:561
  78.5 0.3 collect.1.data_ref
  78.8 0.0 collective-permute-done.1
  78.8 4.7 %decode.1.by_nodes_ref.by_shots_ref = bf16[2,2,1024,1024]{3,2,1,0:T(8,128)(2,1)S(1)} custom-call(s16[8,2,4,144,128]{4,3,2,1,0:T(8,128)(2,1)S(1)} %bitcast.9, s16[8,2,4,144,128]{4,3,2,1,0:T(8,128)(2,1)} %bitcast.4.other_ref), custom_call_target="tpu_custom_call" | custom-call | flops 20000000 | bytes 13000000 | tf_op jit(solution)/shard_map/decode/pallas_call | solution.py:294
  83.5 3.7 %first_adjoint.1 = (f32[64,1024]{1,0:T(8,128)S(1)}, f32[32,16,128]{2,1,0:T(8,128)S(1)}) custom-call(f32[64,1024]{1,0:T(8,128)S(1)} %collect.1.data_ref, bf16[2,2,1024,1024]{3,2,1,0:T(8,128)(2,1)S(1)} %decode.1.by_nodes_ref.by_shots_ref), custom_call_target="tpu_custom_call" | custom-call | flops 800000000 | bytes 9000000 | tf_op jit(solution)/shard_map/first_adjoint/pallas_call | solution.py:317
  87.2 15.2 %all_to_all.31.in_ref = f32[32,16,128]{2,1,0:T(8,128)S(1)} all-to-all(f32[32,16,128]{2,1,0:T(8,128)S(1)} %get-tuple-element.16), channel_id=1, replica_groups=mesh['xl'=2,'z'=4,'core'=2,'y'=4,'xh'=2] {'y','xh','xl','core'}, dimensions={0} | all-to-all | bytes 524288 | tf_op jit(solution)/shard_map/all_to_all | solution.py:564
  102.4 8.8 %second.1 = (f32[64,1024]{1,0:T(8,128)S(1)}, f32[64,1024]{1,0:T(8,128)S(1)}, f32[64,1024]{1,0:T(8,128)S(1)}, f32[32,24,128]{2,1,0:T(8,128)S(1)}) custom-call(f32[64,1024]{1,0:T(8,128)S(1)} %get-tuple-element.15.field_ref, f32[32,16,128]{2,1,0:T(8,128)S(1)} %all_to_all.31.in_ref, bf16[2,2,1024,1024]{3,2,1,0:T(8,128)(2,1)S(1)} %decode.1.by_nodes_ref.by_shots_ref, ...), custom_call_target="tpu_custom_call" | custom-call | flops 1600000000 | bytes 18000000 | tf_op jit(solution)/shard_map/second/pallas_call | solution.py:368
  111.1 13.7 %all_to_all.32.in_ref = f32[32,24,128]{2,1,0:T(8,128)S(1)} all-to-all(f32[32,24,128]{2,1,0:T(8,128)S(1)} %get-tuple-element.20), channel_id=1, replica_groups=mesh['xl'=2,'z'=4,'core'=2,'y'=4,'xh'=2] {'y','xh','xl','core'}, dimensions={0} | all-to-all | bytes 786432 | tf_op jit(solution)/shard_map/all_to_all | solution.py:566
  124.9 5.6 %change.1 = (f32[64,1024]{1,0:T(8,128)S(1)}, f32[64,1024]{1,0:T(8,128)S(1)}, f32[32,8,128]{2,1,0:T(8,128)S(1)}) custom-call(f32[64,1024]{1,0:T(8,128)S(1)} %get-tuple-element.17.gradient_ref, f32[64,1024]{1,0:T(8,128)S(1)} %get-tuple-element.18.field_ref, f32[64,1024]{1,0:T(8,128)S(1)} %get-tuple-element.19.image_ref, f32[32,24,128]{2,1,0:T(8,128)S(1)} %all_to_all.32.in_ref, ...), custom_call_target="tpu_custom_call" | custom-call | flops 800000000 | bytes 9000000 | tf_op jit(solution)/shard_map/change/pallas_call | solution.py:428
  130.4 11.2 %all_to_all.33.sums_ref = f32[32,8,128]{2,1,0:T(8,128)S(1)} all-to-all(f32[32,8,128]{2,1,0:T(8,128)S(1)} %get-tuple-element.23), channel_id=1, replica_groups=mesh['xl'=2,'z'=4,'core'=2,'y'=4,'xh'=2] {'y','xh','xl','core'}, dimensions={0} | all-to-all | bytes 262144 | tf_op jit(solution)/shard_map/all_to_all | solution.py:568
  141.6 0.9 update.1
  142.5 18.9 %all_to_all.34 = s16[8,592,128]{2,1,0:T(8,128)(2,1)S(1)} all-to-all(s16[8,592,128]{2,1,0:T(8,128)(2,1)S(1)} %update.1), channel_id=1, replica_groups=mesh['xl'=2,'z'=4,'core'=2,'y'=4,'xh'=2] {'xl','z'}, dimensions={0} | all-to-all | bytes 2424832 | tf_op jit(solution)/shard_map/all_to_all | solution.py:570
  161.4 2.0 %collective-permute-start.2 = (s16[8,592,128]{2,1,0:T(8,128)(2,1)S(1)}, s16[8,592,128]{2,1,0:T(8,128)(2,1)S(1)}, u32[]{:S(2)}, u32[]{:S(2)}) collective-permute-start(s16[8,592,128]{2,1,0:T(8,128)(2,1)S(1)} %all_to_all.34), channel_id=1, source_target_pairs={{0,8},{8,0},{1,9},{9,1},{2,10},{10,2},{3,11},{11,3},{4,12},{12,4},... | collective-permute-start | bytes 3637256 | tf_op jit(solution)/shard_map/ppermute | solution.py:545
  163.3 2.5 %collective-permute-done.2 = s16[8,592,128]{2,1,0:T(8,128)(2,1)S(1)} collective-permute-done((s16[8,592,128]{2,1,0:T(8,128)(2,1)S(1)}, s16[8,592,128]{2,1,0:T(8,128)(2,1)S(1)}, u32[]{:S(2)}, u32[]{:S(2)}) %collective-permute-start.2) | collective-permute-done | bytes 1212448 | tf_op jit(solution)/shard_map/ppermute | solution.py:545
  165.9 6.3 %finish.1 = (f32[4,2,1024,128]{3,2,1,0:T(8,128)}, f32[4,2,64,128]{3,2,1,0:T(8,128)}) custom-call(s16[2,4,592,128]{3,2,1,0:T(8,128)(2,1)S(1)} %bitcast.10, s16[2,4,592,128]{3,2,1,0:T(8,128)(2,1)S(1)} %bitcast.11), custom_call_target="tpu_custom_call" | custom-call | flops 10000000 | bytes 7000000 | tf_op jit(solution)/shard_map/finish/pallas_call | solution.py:525
  (4 shorter events, 0.0 us)
Async XLA Ops:
  0.6 1.0 copy-start.1
  2.4 10.8 %all-to-all-start.1 = ((s16[4,144,128]{2,1,0:T(8,128)(2,1)}), s16[4,144,128]{2,1,0:T(8,128)(2,1)S(1)}, u32[]{:S(2)}, u32[]{:S(2)}) async-start(s16[4,144,128]{2,1,0:T(8,128)(2,1)} %code_down.1), calls=%async_computation.1 | async-start | bytes 294912 | tf_op jit(solution)/shard_map/all_to_all | solution.py:549
  13.2 31.5 %copy-start.2 = (s32[128]{0:T(128)S(1)}, s32[128]{0:T(128)}, u32[]{:S(2)}) copy-start(s32[128]{0:T(128)} %param.7) | copy-start | bytes 1540
  36.9 41.9 %collective-permute-start.1 = (s16[9216,128]{1,0:T(8,128)(2,1)S(1)}, s16[9216,128]{1,0:T(8,128)(2,1)}, u32[]{:S(2)}, u32[]{:S(2)}) collective-permute-start(s16[9216,128]{1,0:T(8,128)(2,1)S(1)} %all-gather.1), channel_id=1, source_target_pairs={{0,8},{8,0},{1,9},{9,1},{2,10},{10,2},{3,11},{11,3},{4,12},{12,4},... | collective-permute-start | bytes 7077896 | tf_op jit(solution)/shard_map/ppermute | solution.py:545
  54.7 3.0 %collective-permute-start = (s16[8,528,128]{2,1,0:T(8,128)(2,1)}, s16[8,528,128]{2,1,0:T(8,128)(2,1)S(1)}, u32[]{:S(2)}, u32[]{:S(2)}) collective-permute-start(s16[8,528,128]{2,1,0:T(8,128)(2,1)} %get-tuple-element.14), channel_id=1, source_target_pairs={{0,8},{8,0},{1,9},{9,1},{2,10},{10,2},{3,11},{11,3},{4,12},{12,4},... | collective-permute-start | bytes 3244040 | tf_op jit(solution)/shard_map/ppermute | solution.py:545
  57.7 1.2 copy-start
  161.4 4.5 %collective-permute-start.2 = (s16[8,592,128]{2,1,0:T(8,128)(2,1)S(1)}, s16[8,592,128]{2,1,0:T(8,128)(2,1)S(1)}, u32[]{:S(2)}, u32[]{:S(2)}) collective-permute-start(s16[8,592,128]{2,1,0:T(8,128)(2,1)S(1)} %all_to_all.34), channel_id=1, source_target_pairs={{0,8},{8,0},{1,9},{9,1},{2,10},{10,2},{3,11},{11,3},{4,12},{12,4},... | collective-permute-start | bytes 3637256 | tf_op jit(solution)/shard_map/ppermute | solution.py:545

commit v4 on v3

--- a/solution.py
+++ b/solution.py
@@ -18,7 +18,6 @@
 BF = jnp.bfloat16
 F32 = jnp.float32
 SMALL = pltpu.CompilerParams(vmem_limit_bytes=16 * 1024 * 1024)
-LARGE = pltpu.CompilerParams(vmem_limit_bytes=32 * 1024 * 1024)
 FULL = pltpu.CompilerParams(vmem_limit_bytes=58 * 1024 * 1024)
 
 
@@ -209,34 +208,37 @@
     for f in range(F):
         field = in_ref[f].reshape(128, 128)
         exponent = exponent_of(peak_of(field))
-        out_ref[f, 0:128, :] = code(field * jnp.exp2(-exponent))
-        out_ref[f, 128:144, :] = exponent_tile([exponent], 128)
+        coded = code(field * jnp.exp2(-exponent))
+        tile = exponent_tile([exponent], 128)
+        for i in range(16):
+            out_ref[f * 16 + i, 0:128, :] = coded
+            out_ref[f * 16 + i, 128:144, :] = tile
 
 
 def code_down(downgoing):
     return pl.pallas_call(
         code_down_body,
-        out_shape=struct((F, 144, 128), jnp.int16),
-        compiler_params=SMALL,
-        cost_estimate=cost(1_000_000, 500_000),
+        out_shape=struct((64, 144, 128), jnp.int16),
+        compiler_params=FULL,
+        cost_estimate=cost(1_000_000, 3_000_000),
         name="code_down",
     )(downgoing)
 
 
-def adjoint_step(down_ref, both):
+def adjoint_step(down_ref, both, nodes=slice(None)):
     sums = []
     for c in range(2):
-        first = dot(both, down_ref[0, c])
-        sums.append(first[:64] + first[64:] + dot(both[:64], down_ref[1, c]))
+        first = dot(both, down_ref[0, c, :, nodes])
+        sums.append(first[:64] + first[64:] + dot(both[:64], down_ref[1, c, :, nodes]))
     real = sums[0][:32] + sums[1][32:]
     imaginary = sums[0][32:] - sums[1][:32]
     return jnp.concatenate([real, imaginary], axis=0)
 
 
-def forward_step(down_ref, both):
+def forward_step(down_ref, both, shots):
     sums = []
     for c in range(2):
-        first = dot(down_ref[0, c], both) + dot(down_ref[1, c], both)
+        first = dot(down_ref[0, c, shots, :], both) + dot(down_ref[1, c, shots, :], both)
         sums.append((first[:, :64] + first[:, 64:]).T)
     real = sums[0][:32] - sums[1][32:]
     imaginary = sums[0][32:] + sums[1][:32]
@@ -269,122 +271,91 @@
     return (field + mirrored) * 0.5
 
 
-BY_NODES = (2, 2, 1024, 256)
-BY_SHOTS = (2, 2, 256, 1024)
+HELD = pl.BlockSpec(memory_space=pltpu.VMEM)
 
 
 def decode_body(mine_ref, other_ref, down_ref):
     me = lax.axis_index("core")
-    for source, core in ((mine_ref, me), (other_ref, 1 - me)):
-        for n in range(2):
+    for n in range(8):
+        lanes = slice(n * 128, n * 128 + 128)
+        for source, core in ((mine_ref, me), (other_ref, 1 - me)):
             for x in range(2):
                 for z in range(4):
-                    scale = jnp.exp2(source[n, x, z, 128:144, :].astype(F32))[0:1]
+                    scale = jnp.exp2(source[z, n, x, 128:144, :].astype(F32))[0:1]
                     first = x * 512 + core * 256 + z * 64
                     rows = pl.ds(pl.multiple_of(first, 64), 64)
                     for c in range(2):
-                        field = source[n, x, z, c * 64 : c * 64 + 64, :].astype(F32) * scale
+                        field = source[z, n, x, c * 64 : c * 64 + 64, :].astype(F32) * scale
                         high, low = split(field)
-                        down_ref[0, c, rows, n * 128 : n * 128 + 128] = high
-                        down_ref[1, c, rows, n * 128 : n * 128 + 128] = low
+                        down_ref[0, c, rows, lanes] = high
+                        down_ref[1, c, rows, lanes] = low
 
 
 def decode(mine, other):
-    block = pl.BlockSpec((2, 2, 4, 144, 128), lambda j: (j, 0, 0, 0, 0))
     return pl.pallas_call(
         decode_body,
-        grid=(4,),
-        in_specs=[block, block],
-        out_specs=pl.BlockSpec(BY_NODES, lambda j: (0, 0, 0, j)),
+        in_specs=[HELD] * 2,
+        out_specs=HELD,
         out_shape=struct((2, 2, 1024, 1024), BF),
-        compiler_params=LARGE,
+        compiler_params=SMALL,
         cost_estimate=cost(20_000_000, 13_000_000),
         name="decode",
-    )(mine.reshape(8, 2, 4, 144, 128), other.reshape(8, 2, 4, 144, 128))
-
-
-def first_adjoint_body(data_ref, by_nodes_ref, field_ref, pieces_ref, both):
-    @pl.when(pl.program_id(0) == 0)
-    def _():
-        both[...] = stacked_split(data_ref[...])
-
-    field = adjoint_step(by_nodes_ref, both[...])
-    field_ref[...] = field
-    pack(field, pieces_ref, 0)
+    )(mine.reshape(4, 8, 2, 144, 128), other.reshape(4, 8, 2, 144, 128))
+
+
+def first_adjoint_body(data_ref, down_ref, field_ref, pieces_ref):
+    both = stacked_split(data_ref[...])
+    for i in range(4):
+        at = slice(i * 256, i * 256 + 256)
+        field = adjoint_step(down_ref, both, at)
+        field_ref[:, at] = field
+        pack(field, pieces_ref, i * 8)
 
 
 def first_adjoint(data, down):
     return pl.pallas_call(
         first_adjoint_body,
-        grid=(4,),
-        in_specs=[whole((64, 1024)), pl.BlockSpec(BY_NODES, lambda j: (0, 0, 0, j))],
-        out_specs=[
-            pl.BlockSpec((64, 256), lambda j: (0, j)),
-            pl.BlockSpec((8, 16, 128), lambda j: (j, 0, 0)),
-        ],
+        in_specs=[HELD] * 2,
+        out_specs=[HELD] * 2,
         out_shape=[struct((64, 1024)), struct((32, 16, 128))],
-        scratch_shapes=[pltpu.VMEM((128, 1024), BF)],
-        compiler_params=LARGE,
+        compiler_params=SMALL,
         cost_estimate=cost(800_000_000, 9_000_000),
         name="first_adjoint",
     )(data, down)
 
 
-def second_body(
-    field_ref, in_ref, by_shots_ref, by_nodes_ref, gradient_ref, image_ref, again_ref, out_ref,
-    side, both, norm,
-):
-    phase, j = pl.program_id(0), pl.program_id(1)
-    lanes = pl.ds(pl.multiple_of(j * 256, 256), 256)
-
-    @pl.when((phase == 0) & (j == 0))
-    def _():
-        for i in range(4):
-            at = slice(i * 256, i * 256 + 256)
-            gradient = symmetric(field_ref[:, at], in_ref, i * 8)
-            gradient_ref[:, at] = gradient
-            side[at, :] = side_split(gradient)
-        gradient = gradient_ref[...]
-        norm[...] = jnp.zeros((8, 128), F32)
-        norm[0:1, :] = lanes_sum(gradient * gradient)
-
-    @pl.when(phase == 0)
-    def _():
-        image = forward_step(by_shots_ref, side[...])
-        image_ref[:, lanes] = image
-        both[:, lanes] = stacked_split(image)
-        norm[1:2, :] += lanes_sum(image * image)
-
-    @pl.when(phase == 1)
-    def _():
-        field = adjoint_step(by_nodes_ref, both[...])
-        again_ref[:, lanes] = field
-        pack(field, out_ref, j * 8)
-        for k in range(8):
-            out_ref[j * 8 + k, 16:24, :] = norm[...]
+def second_body(field_ref, in_ref, down_ref, gradient_ref, image_ref, again_ref, out_ref, side, both):
+    blocks = [slice(i * 256, i * 256 + 256) for i in range(4)]
+    for i, at in enumerate(blocks):
+        gradient = symmetric(field_ref[:, at], in_ref, i * 8)
+        gradient_ref[:, at] = gradient
+        side[at, :] = side_split(gradient)
+    for at in blocks:
+        image = forward_step(down_ref, side[...], at)
+        image_ref[:, at] = image
+        both[:, at] = stacked_split(image)
+    gradient, image = gradient_ref[...], image_ref[...]
+    rows = [lanes_sum(gradient * gradient), lanes_sum(image * image), jnp.zeros((6, 128), F32)]
+    norm = jnp.concatenate(rows, axis=0)
+    for i, at in enumerate(blocks):
+        field = adjoint_step(down_ref, both[...], at)
+        again_ref[:, at] = field
+        pack(field, out_ref, i * 8)
+    for k in range(32):
+        out_ref[k, 16:24, :] = norm
 
 
 def second(field, received, down):
     return pl.pallas_call(
         second_body,
-        grid=(2, 4),
-        in_specs=[
-            whole((64, 1024)),
-            whole((32, 16, 128)),
-            pl.BlockSpec(BY_SHOTS, lambda p, j: (0, 0, jnp.where(p == 0, j, 3), 0)),
-            pl.BlockSpec(BY_NODES, lambda p, j: (0, 0, 0, jnp.where(p == 0, 0, j))),
-        ],
-        out_specs=[whole((64, 1024))] * 3 + [whole((32, 24, 128))],
+        in_specs=[HELD] * 3,
+        out_specs=[HELD] * 4,
         out_shape=[struct((64, 1024))] * 3 + [struct((32, 24, 128))],
-        scratch_shapes=[
-            pltpu.VMEM((1024, 128), BF),
-            pltpu.VMEM((128, 1024), BF),
-            pltpu.VMEM((8, 128), F32),
-        ],
-        compiler_params=LARGE,
+        scratch_shapes=[pltpu.VMEM((1024, 128), BF), pltpu.VMEM((128, 1024), BF)],
+        compiler_params=SMALL,
         cost_estimate=cost(1_600_000_000, 18_000_000),
         name="second",
-    )(field, received, down, down)
+    )(field, received, down)
 
 
 def first_step(in_ref):
@@ -394,54 +365,42 @@
 
 
 def change_body(
-    gradient_ref, field_ref, image_ref, in_ref, by_shots_ref, again_ref, change_ref, out_ref, side, sums
+    gradient_ref, field_ref, image_ref, in_ref, down_ref, again_ref, change_ref, out_ref, side
 ):
-    j = pl.program_id(0)
-    lanes = pl.ds(pl.multiple_of(j * 256, 256), 256)
+    blocks = [slice(i * 256, i * 256 + 256) for i in range(4)]
     norm, curvature = first_step(in_ref)
     step = norm / curvature
-
-    @pl.when(j == 0)
-    def _():
-        for i in range(4):
-            at = slice(i * 256, i * 256 + 256)
-            again = symmetric(field_ref[:, at], in_ref, i * 8)
-            again_ref[:, at] = again
-            side[at, :] = side_split(again)
-        sums[...] = jnp.zeros((8, 128), F32)
-        gradient = gradient_ref[...] - step * again_ref[...]
-        sums[0:1, :] = lanes_sum(gradient * gradient)
-
-    image = image_ref[:, lanes]
-    change = image - step * forward_step(by_shots_ref, side[...])
-    change_ref[:, lanes] = change
-    sums[1:2, :] += lanes_sum(change * change)
-    sums[2:3, :] += lanes_sum(change * image)
-
-    @pl.when(j == 3)
-    def _():
-        for i in range(32):
-            out_ref[i] = sums[...]
+    for i, at in enumerate(blocks):
+        again = symmetric(field_ref[:, at], in_ref, i * 8)
+        again_ref[:, at] = again
+        side[at, :] = side_split(again)
+    for at in blocks:
+        change_ref[:, at] = image_ref[:, at] - step * forward_step(down_ref, side[...], at)
+    gradient = gradient_ref[...] - step * again_ref[...]
+    change = change_ref[...]
+    rows = [gradient * gradient, change * change, change * image_ref[...]]
+    rows = [lanes_sum(row) for row in rows] + [jnp.zeros((5, 128), F32)]
+    sums = jnp.concatenate(rows, axis=0)
+    for i in range(32):
+        out_ref[i] = sums
 
 
 def changed(gradient, field, image, received, down):
     return pl.pallas_call(
         change_body,
-        grid=(4,),
-        in_specs=[
-            whole((64, 1024)),
-            whole((64, 1024)),
-            whole((64, 1024)),
-            whole((32, 24, 128)),
-            pl.BlockSpec(BY_SHOTS, lambda j: (0, 0, j, 0)),
-        ],
-        out_specs=[whole((64, 1024)), whole((64, 1024)), whole((32, 8, 128))],
+        in_specs=[HELD] * 5,
+        out_specs=[HELD] * 3,
         out_shape=[struct((64, 1024)), struct((64, 1024)), struct((32, 8, 128))],
-        scratch_shapes=[pltpu.VMEM((1024, 128), BF), pltpu.VMEM((8, 128), F32)],
-        compiler_params=LARGE,
+        scratch_shapes=[pltpu.VMEM((1024, 128), BF)],
+        compiler_params=SMALL,
         cost_estimate=cost(800_000_000, 9_000_000),
         name="change",
     )(gradient, field, image, received, down)
+
+
+def side_by_side(field):
+    turned = field.T
+    return jnp.concatenate([turned[:512], turned[512:]], axis=1)
 
 
 def update_body(
@@ -458,12 +417,12 @@
     result = step * gradient + new_step * direction
     left = data_ref[...] - step * image - new_step * (change_ref[...] + beta * image)
     exponents = [exponent_of(peak_of(result)), exponent_of(peak_of(left))]
-    coded = code(result * jnp.exp2(-exponents[0]))
+    own = lax.axis_index("xl") * 2 + lax.axis_index("core")
+    coded = code(pltpu.roll(side_by_side(result * jnp.exp2(-exponents[0])), own * 32, 1))
     turned = (left * jnp.exp2(-exponents[1])).T
     tile = exponent_tile(exponents, 128)
     for dest in range(8):
-        for j in range(8):
-            out_ref[dest, j * 64 : j * 64 + 64, :] = coded[:, j * 128 : j * 128 + 128]
+        out_ref[dest, 0:512, :] = coded
         for core in range(2):
             at = (dest // 4 * 2 + core) * 256 + dest % 4 * 64
             piece = jnp.concatenate([turned[at : at + 32], turned[at + 32 : at + 64]], axis=1)
@@ -481,39 +440,25 @@
     )(data, gradient, again, image, change, received, sums)
 
 
-def finish_body(mine_ref, other_ref, reflectivity_ref, residual_ref, held, arrived):
-    f = pl.program_id(0)
-    me = lax.axis_index("core")
-
-    def fetch(i, x, k):
-        source = (mine_ref, other_ref)[k].at[x, i]
-        slot = me if k == 0 else 1 - me
-        return pltpu.make_async_copy(source, held.at[i, x, slot], arrived.at[i, x, k])
-
-    @pl.when(f == 0)
-    def _():
-        for i in range(F):
-            for x in range(2):
-                for k in range(2):
-                    fetch(i, x, k).start()
-
-    for x in range(2):
-        for k in range(2):
-            fetch(f, x, k).wait()
-
-    scales = []
-    for k in range(4):
-        scales.append(jnp.exp2(held[f, k // 2, k % 2, 576:592, :].astype(F32)))
-    for c in range(2):
-        for j in range(8):
-            at = slice(j * 64 + c * 32, j * 64 + c * 32 + 32)
-            parts = [held[f, k // 2, k % 2, at, :].astype(F32) * scales[k][0:1] for k in range(4)]
-            whole_rows = jnp.concatenate(parts, axis=0)
-            reflectivity_ref[0, c, j * 128 : j * 128 + 128, :] = whole_rows.T
-    first = pl.multiple_of(512 + me * 32, 32)
-    pieces = [
-        held[f, k // 2, k % 2, pl.ds(first, 32), :].astype(F32) * scales[k][1:2] for k in range(4)
-    ]
+def place(f, first_ref, second_ref, core, reflectivity_ref, residual_ref):
+    refs = [ref.at[x, f] for x in range(2) for ref in (first_ref, second_ref)]
+    scales = [jnp.exp2(ref[576:592, :].astype(F32)) for ref in refs]
+    owner = lax.broadcasted_iota(jnp.int32, (64, 128), 1) // 32
+    spread = scales[3][0:1]
+    for k in range(3):
+        spread = jnp.where(owner[0:1] == k, scales[k][0:1], spread)
+    for j in range(8):
+        parts = [ref[j * 64 : j * 64 + 64, :].astype(F32) for ref in refs]
+        for q in range(4):
+            mixed = parts[(3 - q) % 4]
+            for b in range(3):
+                mixed = jnp.where(owner == b, parts[(b - q) % 4], mixed)
+            if q:
+                mixed = pltpu.roll(mixed, 128 - 32 * q, 1)
+            first = q // 2 * 512 + j * 64
+            reflectivity_ref[0, q % 2, first : first + 64, :] = mixed * spread
+    rows = slice(512 + core * 32, 544 + core * 32)
+    pieces = [ref[rows, :].astype(F32) * scale[1:2] for ref, scale in zip(refs, scales)]
     for c in range(2):
         for half in range(2):
             at = half * 64 + c * 32
@@ -521,21 +466,30 @@
             residual_ref[0, c, half * 32 : half * 32 + 32, :] = row
 
 
+def finish_body(mine_ref, other_ref, reflectivity_ref, residual_ref):
+    f = pl.program_id(0)
+    me = lax.axis_index("core")
+
+    @pl.when(me == 0)
+    def _():
+        place(f, mine_ref, other_ref, 0, reflectivity_ref, residual_ref)
+
+    @pl.when(me == 1)
+    def _():
+        place(f, other_ref, mine_ref, 1, reflectivity_ref, residual_ref)
+
+
 def finish(mine, other):
     return pl.pallas_call(
         finish_body,
         grid=(F,),
-        in_specs=[pl.BlockSpec(memory_space=pl.ANY)] * 2,
+        in_specs=[HELD] * 2,
         out_specs=[
             pl.BlockSpec((1, 2, 1024, 128), lambda f: (f, 0, 0, 0)),
             pl.BlockSpec((1, 2, 64, 128), lambda f: (f, 0, 0, 0)),
         ],
         out_shape=[struct((F, 2, 1024, 128)), struct((F, 2, 64, 128))],
-        scratch_shapes=[
-            pltpu.VMEM((F, 2, 2, 592, 128), jnp.int16),
-            pltpu.SemaphoreType.DMA((F, 2, 2)),
-        ],
-        compiler_params=LARGE,
+        compiler_params=SMALL,
         cost_estimate=cost(10_000_000, 7_000_000),
         name="finish",
     )(mine.reshape(2, F, 592, 128), other.reshape(2, F, 592, 128))
@@ -546,10 +500,7 @@
 
 
 def shards(up_time, downgoing, freq_idx, node_map):
-    own = lax.all_to_all(code_down(downgoing), "z", 0, 0, tiled=True)
-    mine = lax.all_gather(own.reshape(576, 128), PLANE_CHIPS, axis=0, tiled=True)
-    down = decode(mine, swap_cores(mine))
-
+    mine = lax.all_to_all(code_down(downgoing), ("z",) + PLANE_CHIPS, 0, 0, tiled=True)
     count = up_time.shape[1]
     table = local_table(freq_idx, lax.axis_index(SHOT) * count, count)
     table = table[:, None, None, :] * jnp.eye(8, dtype=BF)[None, :, :, None]
@@ -558,7 +509,10 @@
     inverse = jnp.broadcast_to(inverse[None, :], (8, 128))
     pieces, others = transform(up_time, table.reshape(64, 256), inverse)
     pieces = merge(pieces, swap_cores(others))
-    data = collect(lax.all_to_all(pieces, CHIPS, 0, 0, tiled=True))
+    mine, pieces = lax.optimization_barrier((mine, pieces))
+    down = decode(mine, swap_cores(mine))
+    received = lax.all_to_all(pieces, CHIPS, 0, 0, tiled=True)
+    data = collect(received)
 
     field, pieces = first_adjoint(data, down)
     received = lax.all_to_all(pieces, PLANE, 0, 0, tiled=True)

time: 173 us -> 147 us (0.85)
  blocking collectives: 101 us -> 76.5 us
  Pallas kernels: 41.5 us -> 29.6 us
  waiting for transfers between devices: 9.53 us -> 19.2 us
  starting transfers between devices: 14.9 us -> 17.7 us
    all_gather x1 -> x0, blocking collectives: 23.7 us -> none  [shards(): lax.all_gather(own.reshape(576, 128), PLANE_CHIPS, axis=0, tiled=True)]
    pallas_call x6, Pallas kernels: 29.9 us -> 17.8 us  [the longest x1 4.61 us: second(): pl.pallas_call(second_body, in_specs=[HELD] * 3, out_specs=[HELD] * 4, ou...]
    all_to_all x1, waiting for transfers between devices: 4.1 us -> 14.1 us  [shards(): lax.all_to_all(code_down(downgoing), ('z',) + PLANE_CHIPS, 0, 0, tiled=True)]
    all_to_all x1, starting transfers between devices: 5.86 us -> 12.1 us  [shards(): lax.all_to_all(code_down(downgoing), ('z',) + PLANE_CHIPS, 0, 0, tiled=True)]
    ppermute x3, starting transfers between devices: 9.09 us -> 5.62 us  [swap_cores(): return lax.ppermute(x, 'core', [(0, 1), (1, 0)])]
  transfers between devices with their start and end apart: 4 -> 4, of which waited for: 3 -> 3; matrix products, arithmetic and copies ran while one was open for 1% -> 1% of each run, Pallas kernels for 6% -> 7%
where the time goes in v4:
time: 147 us
  blocking collectives  76.5 us (52%)
  Pallas kernels  29.6 us (20%)
  waiting for transfers between devices  19.2 us (13%)
  starting transfers between devices  17.7 us (12%)
  local copies, waits for them, and re-layouts  2.6 us (2%)
    all_to_all x2, blocking collectives, shards(): received = lax.all_to_all(pieces, PLANE, 0, 0, tiled=True)  28 us
    all_to_all x1, blocking collectives, shards(): mine = lax.all_to_all(pieces, CHIPS, 0, 0, tiled=True)  18.9 us
    all_to_all x1, blocking collectives, shards(): received = lax.all_to_all(pieces, CHIPS, 0, 0, tiled=True)  18.4 us
    all_to_all x1, waiting for transfers between devices, shards(): lax.all_to_all(code_down(downgoing), ('z',) + PLANE_CHIPS, 0, 0, tiled=True)  14.1 us
    all_to_all x1, starting transfers between devices, shards(): lax.all_to_all(code_down(downgoing), ('z',) + PLANE_CHIPS, 0, 0, tiled=True)  12.1 us
    all_to_all x1, blocking collectives, shards(): sums = lax.all_to_all(sums, PLANE, 0, 0, tiled=True)  11.2 us
    pallas_call x1, Pallas kernels, transform(): pl.pallas_call(transform_body, grid=(8,), in_specs=[pl.BlockSpec(memory_s...  9.25 us
    ppermute x3, starting transfers between devices, swap_cores(): return lax.ppermute(x, 'core', [(0, 1), (1, 0)])  5.62 us
  transfers between devices with their start and end apart: 4, of which 3 were waited for; matrix products, arithmetic and copies ran while one was open for 1% of the time, Pallas kernels for 7%

profile of v4, /device:TPU:1, one launch (start us, length us, event | category | flops | bytes accessed | tf_op | source)
XLA Modules:
  0.0 146.6 jit_solution(15370235433557020778)
XLA Ops:
  0.6 2.8 %code_down.1 = s16[64,144,128]{2,1,0:T(8,128)(2,1)} custom-call(f32[4,2,64,128]{3,2,1,0:T(8,128)} %in_ref.1), custom_call_target="tpu_custom_call" | custom-call | flops 1000000 | bytes 3000000 | tf_op jit(solution)/shard_map/code_down/pallas_call | solution.py:219
  3.4 0.0 copy-start.1
  3.4 0.0 copy-start.2
  3.4 12.1 %all-to-all-start = ((s16[64,144,128]{2,1,0:T(8,128)(2,1)}), s16[64,144,128]{2,1,0:T(8,128)(2,1)S(1)}, u32[]{:S(2)}, u32[]{:S(2)}) async-start(s16[64,144,128]{2,1,0:T(8,128)(2,1)} %code_down.1), calls=%async_computation | async-start | bytes 4718592 | tf_op jit(solution)/shard_map/all_to_all | solution.py:503
  15.5 0.0 copy-done.1
  15.6 0.1 cosine_convert_fusion
  15.7 0.1 broadcast_multiply_fusion
  15.8 0.8 mul.78.table_ref
  16.6 0.0 copy-done.2
  16.6 0.1 select_reduce_fusion
  16.7 0.6 broadcast_in_dim.16.inverse_ref
  17.3 9.3 %transform.1 = (s16[8,528,128]{2,1,0:T(8,128)(2,1)}, s16[8,528,128]{2,1,0:T(8,128)(2,1)}) custom-call(bf16[2,4,2,64,32,128]{5,4,3,2,1,0:T(8,128)(2,1)} %bitcast.12, bf16[64,256]{1,0:T(8,128)(2,1)} %mul.78.table_ref, s32[8,128]{1,0:T(8,128)} %broadcast_in_dim.16.inverse_ref), custom_call_target="tpu_custom_call" | custom-call | flops 600000000 | bytes 10000000 | tf_op jit(solution)/shard_map/transform/pallas_call | solution.py:136
  26.5 1.0 collective-permute-start
  27.6 2.5 %collective-permute-done.other_ref = s16[8,528,128]{2,1,0:T(8,128)(2,1)S(1)} collective-permute-done((s16[8,528,128]{2,1,0:T(8,128)(2,1)}, s16[8,528,128]{2,1,0:T(8,128)(2,1)S(1)}, u32[]{:S(2)}, u32[]{:S(2)}) %collective-permute-start) | collective-permute-done | bytes 1081376 | tf_op jit(solution)/shard_map/ppermute | solution.py:499
  30.1 0.0 copy-start
  30.1 1.2 copy-done
  31.3 1.2 merge.1
  32.6 14.1 %all-to-all-done = s16[64,144,128]{2,1,0:T(8,128)(2,1)S(1)} async-done(((s16[64,144,128]{2,1,0:T(8,128)(2,1)}), s16[64,144,128]{2,1,0:T(8,128)(2,1)S(1)}, u32[]{:S(2)}, u32[]{:S(2)}) %all-to-all-start) | async-done | bytes 2359328 | tf_op jit(solution)/shard_map/all_to_all | solution.py:503
  46.7 2.6 %collective-permute-start.1 = (s16[64,144,128]{2,1,0:T(8,128)(2,1)S(1)}, s16[64,144,128]{2,1,0:T(8,128)(2,1)S(1)}, u32[]{:S(2)}, u32[]{:S(2)}) collective-permute-start(s16[64,144,128]{2,1,0:T(8,128)(2,1)S(1)} %all-to-all-done), channel_id=1, source_target_pairs={{0,8},{8,0},{1,9},{9,1},{2,10},{10,2},{3,11},{11,3},{4,12},{12,4},... | collective-permute-start | bytes 7077896 | tf_op jit(solution)/shard_map/ppermute | solution.py:499
  49.3 18.4 %all_to_all.30.in_ref = s16[8,528,128]{2,1,0:T(8,128)(2,1)S(1)} all-to-all(s16[8,528,128]{2,1,0:T(8,128)(2,1)S(1)} %merge.1), channel_id=1, replica_groups=mesh['xl'=2,'z'=4,'core'=2,'y'=4,'xh'=2] {'xl','z'}, dimensions={0} | all-to-all | bytes 2162688 | tf_op jit(solution)/shard_map/all_to_all | solution.py:514
  67.7 0.3 collect.1.data_ref
  68.0 0.0 collective-permute-done.1
  68.0 2.7 %decode.1.down_ref = bf16[2,2,1024,1024]{3,2,1,0:T(8,128)(2,1)S(1)} custom-call(s16[4,8,2,144,128]{4,3,2,1,0:T(8,128)(2,1)S(1)} %bitcast.8, s16[4,8,2,144,128]{4,3,2,1,0:T(8,128)(2,1)S(1)} %bitcast.10), custom_call_target="tpu_custom_call" | custom-call | flops 20000000 | bytes 13000000 | tf_op jit(solution)/shard_map/decode/pallas_call | solution.py:295
  70.7 1.7 %first_adjoint.1 = (f32[64,1024]{1,0:T(8,128)S(1)}, f32[32,16,128]{2,1,0:T(8,128)S(1)}) custom-call(f32[64,1024]{1,0:T(8,128)S(1)} %collect.1.data_ref, bf16[2,2,1024,1024]{3,2,1,0:T(8,128)(2,1)S(1)} %decode.1.down_ref), custom_call_target="tpu_custom_call" | custom-call | flops 800000000 | bytes 9000000 | tf_op jit(solution)/shard_map/first_adjoint/pallas_call | solution.py:316
  72.4 14.2 %all_to_all.31.in_ref = f32[32,16,128]{2,1,0:T(8,128)S(1)} all-to-all(f32[32,16,128]{2,1,0:T(8,128)S(1)} %get-tuple-element.20), channel_id=1, replica_groups=mesh['xl'=2,'z'=4,'core'=2,'y'=4,'xh'=2] {'y','xh','xl','core'}, dimensions={0} | all-to-all | bytes 524288 | tf_op jit(solution)/shard_map/all_to_all | solution.py:518
  86.6 4.6 %second.1 = (f32[64,1024]{1,0:T(8,128)S(1)}, f32[64,1024]{1,0:T(8,128)S(1)}, f32[64,1024]{1,0:T(8,128)S(1)}, f32[32,24,128]{2,1,0:T(8,128)S(1)}) custom-call(f32[64,1024]{1,0:T(8,128)S(1)} %get-tuple-element.19.field_ref, f32[32,16,128]{2,1,0:T(8,128)S(1)} %all_to_all.31.in_ref, bf16[2,2,1024,1024]{3,2,1,0:T(8,128)(2,1)S(1)} %decode.1.down_ref), custom_call_target="tpu_custom_call" | custom-call | flops 1600000000 | bytes 18000000 | tf_op jit(solution)/shard_map/second/pallas_call | solution.py:349
  91.2 13.7 %all_to_all.32.in_ref = f32[32,24,128]{2,1,0:T(8,128)S(1)} all-to-all(f32[32,24,128]{2,1,0:T(8,128)S(1)} %get-tuple-element.24), channel_id=1, replica_groups=mesh['xl'=2,'z'=4,'core'=2,'y'=4,'xh'=2] {'y','xh','xl','core'}, dimensions={0} | all-to-all | bytes 786432 | tf_op jit(solution)/shard_map/all_to_all | solution.py:520
  105.0 3.1 %change.1 = (f32[64,1024]{1,0:T(8,128)S(1)}, f32[64,1024]{1,0:T(8,128)S(1)}, f32[32,8,128]{2,1,0:T(8,128)S(1)}) custom-call(f32[64,1024]{1,0:T(8,128)S(1)} %get-tuple-element.21.gradient_ref, f32[64,1024]{1,0:T(8,128)S(1)} %get-tuple-element.22.field_ref, f32[64,1024]{1,0:T(8,128)S(1)} %get-tuple-element.23.image_ref, f32[32,24,128]{2,1,0:T(8,128)S(1)} %all_to_all.32.in_ref, ...), custom_call_target="tpu_custom_call" | custom-call | flops 800000000 | bytes 9000000 | tf_op jit(solution)/shard_map/change/pallas_call | solution.py:389
  108.0 11.2 %all_to_all.33.sums_ref = f32[32,8,128]{2,1,0:T(8,128)S(1)} all-to-all(f32[32,8,128]{2,1,0:T(8,128)S(1)} %get-tuple-element.27), channel_id=1, replica_groups=mesh['xl'=2,'z'=4,'core'=2,'y'=4,'xh'=2] {'y','xh','xl','core'}, dimensions={0} | all-to-all | bytes 262144 | tf_op jit(solution)/shard_map/all_to_all | solution.py:522
  119.3 1.0 update.1
  120.3 18.9 %all_to_all.34 = s16[8,592,128]{2,1,0:T(8,128)(2,1)S(1)} all-to-all(s16[8,592,128]{2,1,0:T(8,128)(2,1)S(1)} %update.1), channel_id=1, replica_groups=mesh['xl'=2,'z'=4,'core'=2,'y'=4,'xh'=2] {'xl','z'}, dimensions={0} | all-to-all | bytes 2424832 | tf_op jit(solution)/shard_map/all_to_all | solution.py:524
  139.2 2.0 %collective-permute-start.2 = (s16[8,592,128]{2,1,0:T(8,128)(2,1)S(1)}, s16[8,592,128]{2,1,0:T(8,128)(2,1)S(1)}, u32[]{:S(2)}, u32[]{:S(2)}) collective-permute-start(s16[8,592,128]{2,1,0:T(8,128)(2,1)S(1)} %all_to_all.34), channel_id=1, source_target_pairs={{0,8},{8,0},{1,9},{9,1},{2,10},{10,2},{3,11},{11,3},{4,12},{12,4},... | collective-permute-start | bytes 3637256 | tf_op jit(solution)/shard_map/ppermute | solution.py:499
  141.1 2.5 %collective-permute-done.2 = s16[8,592,128]{2,1,0:T(8,128)(2,1)S(1)} collective-permute-done((s16[8,592,128]{2,1,0:T(8,128)(2,1)S(1)}, s16[8,592,128]{2,1,0:T(8,128)(2,1)S(1)}, u32[]{:S(2)}, u32[]{:S(2)}) %collective-permute-start.2) | collective-permute-done | bytes 1212448 | tf_op jit(solution)/shard_map/ppermute | solution.py:499
  143.6 3.0 %finish.1 = (f32[4,2,1024,128]{3,2,1,0:T(8,128)}, f32[4,2,64,128]{3,2,1,0:T(8,128)}) custom-call(s16[2,4,592,128]{3,2,1,0:T(8,128)(2,1)S(1)} %bitcast.9, s16[2,4,592,128]{3,2,1,0:T(8,128)(2,1)S(1)} %bitcast.11), custom_call_target="tpu_custom_call" | custom-call | flops 10000000 | bytes 7000000 | tf_op jit(solution)/shard_map/finish/pallas_call | solution.py:483
  (4 shorter events, 0.0 us)
Async XLA Ops:
  3.4 12.1 %copy-start.1 = (s32[4]{0:T(128)S(1)}, s32[4]{0:T(128)}, u32[]{:S(2)}) copy-start(s32[4]{0:T(128)} %param.6) | copy-start | bytes 52
  3.4 13.1 %copy-start.2 = (s32[128]{0:T(128)S(1)}, s32[128]{0:T(128)}, u32[]{:S(2)}) copy-start(s32[128]{0:T(128)} %param.7) | copy-start | bytes 1540
  3.4 43.2 %all-to-all-start = ((s16[64,144,128]{2,1,0:T(8,128)(2,1)}), s16[64,144,128]{2,1,0:T(8,128)(2,1)S(1)}, u32[]{:S(2)}, u32[]{:S(2)}) async-start(s16[64,144,128]{2,1,0:T(8,128)(2,1)} %code_down.1), calls=%async_computation | async-start | bytes 4718592 | tf_op jit(solution)/shard_map/all_to_all | solution.py:503
  26.5 3.6 %collective-permute-start = (s16[8,528,128]{2,1,0:T(8,128)(2,1)}, s16[8,528,128]{2,1,0:T(8,128)(2,1)S(1)}, u32[]{:S(2)}, u32[]{:S(2)}) collective-permute-start(s16[8,528,128]{2,1,0:T(8,128)(2,1)} %get-tuple-element.16), channel_id=1, source_target_pairs={{0,8},{8,0},{1,9},{9,1},{2,10},{10,2},{3,11},{11,3},{4,12},{12,4},... | collective-permute-start | bytes 3244040 | tf_op jit(solution)/shard_map/ppermute | solution.py:499
  30.1 1.2 copy-start
  46.7 21.3 %collective-permute-start.1 = (s16[64,144,128]{2,1,0:T(8,128)(2,1)S(1)}, s16[64,144,128]{2,1,0:T(8,128)(2,1)S(1)}, u32[]{:S(2)}, u32[]{:S(2)}) collective-permute-start(s16[64,144,128]{2,1,0:T(8,128)(2,1)S(1)} %all-to-all-done), channel_id=1, source_target_pairs={{0,8},{8,0},{1,9},{9,1},{2,10},{10,2},{3,11},{11,3},{4,12},{12,4},... | collective-permute-start | bytes 7077896 | tf_op jit(solution)/shard_map/ppermute | solution.py:499
  139.2 4.5 %collective-permute-start.2 = (s16[8,592,128]{2,1,0:T(8,128)(2,1)S(1)}, s16[8,592,128]{2,1,0:T(8,128)(2,1)S(1)}, u32[]{:S(2)}, u32[]{:S(2)}) collective-permute-start(s16[8,592,128]{2,1,0:T(8,128)(2,1)S(1)} %all_to_all.34), channel_id=1, source_target_pairs={{0,8},{8,0},{1,9},{9,1},{2,10},{10,2},{3,11},{11,3},{4,12},{12,4},... | collective-permute-start | bytes 3637256 | tf_op jit(solution)/shard_map/ppermute | solution.py:499

commit v5 on v4

--- a/solution.py
+++ b/solution.py
@@ -13,10 +13,12 @@
 SHOT = ("xl", "z", "core")
 NODE = ("y", "xh")
 CHIPS = ("xl", "z")
+ORDER = (6, 7, 5, 2, 3, 1, 4)
 PLANE_CHIPS = ("y", "xh", "xl")
 PLANE = ("y", "xh", "xl", "core")
 BF = jnp.bfloat16
 F32 = jnp.float32
+HELD = pl.BlockSpec(memory_space=pltpu.VMEM)
 SMALL = pltpu.CompilerParams(vmem_limit_bytes=16 * 1024 * 1024)
 FULL = pltpu.CompilerParams(vmem_limit_bytes=58 * 1024 * 1024)
 
@@ -83,114 +85,99 @@
     return jnp.sum(rows, axis=(0, 1), keepdims=True)
 
 
-def transform_body(
-    up_ref, table_ref, inverse_ref, mine_ref, other_ref, sums, exponents, held, arrived
-):
-    block = pl.program_id(0)
+def transform_body(up_ref, table_ref, inverse_ref, mine_ref, other_ref, sums, exponents):
     me = lax.axis_index("core")
-
-    def fetch(i):
-        source = up_ref.at[i // 4, pl.ds(i % 2 * 2, 2), i // 2 % 2]
-        return pltpu.make_async_copy(source, held.at[i], arrived.at[i])
-
-    @pl.when(block == 0)
-    def _():
-        for i in range(8):
-            fetch(i).start()
-
-    fetch(block).wait()
-    index = jnp.broadcast_to(inverse_ref[0:1, :], (64, 128))
-    largest = jnp.zeros((64, 128), F32)
-    for part in range(2):
-        for group in range(4):
-            row = group * 16
-            x = [held[block, part, row + h * 8 : row + h * 8 + 8].reshape(256, 128) for h in range(2)]
-            both = dot(table_ref[...], jnp.concatenate(x, axis=1))
+    index = jnp.broadcast_to(inverse_ref[...], (64, 128))
+    table = jnp.concatenate([table_ref[...].astype(F32)] * 8, axis=1)
+    table = jnp.broadcast_to(table[:, None, :], (8, 8, 256)).reshape(64, 256)
+    shot = lax.broadcasted_iota(jnp.int32, (64, 256), 0) % 8
+    table = jnp.where(shot == lax.broadcasted_iota(jnp.int32, (64, 256), 1) // 32, table, 0.0).astype(BF)
+
+    def step(block, carry):
+        chip, core, first = block // 4, block // 2 % 2, block % 2 * 2
+        largest = jnp.zeros((64, 128), F32)
+        for pair in range(8):
+            part, row = first + pair // 4, pair % 4 * 16
+            x = [up_ref[chip, part, core, row + h * 8 : row + h * 8 + 8].reshape(256, 128) for h in range(2)]
+            both = dot(table, jnp.concatenate(x, axis=1))
             for h in range(2):
                 y = jnp.take_along_axis(both[:, h * 128 : h * 128 + 128], index, axis=1)
                 largest = jnp.maximum(largest, jnp.abs(y))
-                at = part * 64 + row + h * 8
+                at = pair // 4 * 64 + row + h * 8
                 for fc in range(8):
                     sums[fc, at : at + 8, :] = y[fc * 8 : fc * 8 + 8]
-    exponent = exponent_of(peak_of(largest))
-    scale = jnp.exp2(-exponent)
-    exponents[pl.ds(block, 1), :] = jnp.broadcast_to(exponent, (1, 128))
-    rows = pl.multiple_of(block * 64, 64)
-    for fc in range(8):
-        turned = sums[fc].T * scale
-        at = pl.ds(rows + (fc % 2) * 32, 32)
-        for x in range(2):
-            first, second_ = (turned[x * 64 + c * 32 : x * 64 + c * 32 + 32] for c in range(2))
-            mine_ref[x * 4 + fc // 2, at, :] = code(jnp.where(me == 0, first, second_))
-            other_ref[x * 4 + fc // 2, at, :] = code(jnp.where(me == 0, second_, first))
-
-    @pl.when(block == 7)
-    def _():
-        coded = exponent_tile([exponents[i : i + 1, :] for i in range(8)], 128)
-        for dest in range(8):
-            mine_ref[dest, 512:528, :] = coded
-            other_ref[dest, 512:528, :] = coded
+        exponent = exponent_of(peak_of(largest))
+        scale = jnp.exp2(-exponent)
+        exponents[pl.ds(block, 1), :] = jnp.broadcast_to(exponent, (1, 128))
+        rows = pl.multiple_of(block * 64, 64)
+        for fc in range(8):
+            turned = sums[fc].T * scale
+            at = pl.ds(rows + (fc % 2) * 32, 32)
+            for x in range(2):
+                lower, upper = (turned[x * 64 + c * 32 : x * 64 + c * 32 + 32] for c in range(2))
+                mine_ref[x * 4 + fc // 2, at, :] = code(jnp.where(me == 0, lower, upper))
+                other_ref[x * 4 + fc // 2, at, :] = code(jnp.where(me == 0, upper, lower))
+        return carry
+
+    lax.fori_loop(0, 8, step, 0)
+    coded = exponent_tile([exponents[i : i + 1, :] for i in range(8)], 128)
+    for dest in range(8):
+        mine_ref[dest, 512:528, :] = coded
+        other_ref[dest, 512:528, :] = coded
 
 
 def transform(up_time, table, inverse):
     return pl.pallas_call(
         transform_body,
-        grid=(8,),
-        in_specs=[
-            pl.BlockSpec(memory_space=pl.ANY),
-            whole((64, 256)),
-            whole((8, 128)),
-        ],
-        out_specs=[whole((8, 528, 128))] * 2,
+        in_specs=[HELD] * 3,
+        out_specs=[HELD] * 2,
         out_shape=[struct((8, 528, 128), jnp.int16)] * 2,
-        scratch_shapes=[
-            pltpu.VMEM((8, 128, 128), F32),
-            pltpu.VMEM((8, 128), F32),
-            pltpu.VMEM((8, 2, 64, 32, 128), BF),
-            pltpu.SemaphoreType.DMA((8,)),
-        ],
-        compiler_params=FULL,
+        scratch_shapes=[pltpu.VMEM((8, 128, 128), F32), pltpu.VMEM((8, 128), F32)],
+        compiler_params=SMALL,
         cost_estimate=cost(600_000_000, 10_000_000),
         name="transform",
     )(up_time.reshape(2, 4, 2, 64, 32, 128), table, inverse)
 
 
-def merge_body(mine_ref, other_ref, out_ref):
+def merge_body(mine_ref, other_ref, *out_refs):
+    chip = lax.axis_index("xl") * 4 + lax.axis_index("z")
     scales = [jnp.exp2(r[0, 512:528, :].astype(F32)) for r in (mine_ref, other_ref)]
     exponents = []
     for block in range(8):
         rows = slice(block * 64, block * 64 + 64)
         sums, largest = [], jnp.zeros((64, 128), F32)
-        for dest in range(8):
+        for i in range(8):
+            dest = chip ^ i
             mine = mine_ref[dest, rows, :].astype(F32) * scales[0][block : block + 1]
             sums.append(mine + other_ref[dest, rows, :].astype(F32) * scales[1][block : block + 1])
             largest = jnp.maximum(largest, jnp.abs(sums[-1]))
         exponents.append(exponent_of(peak_of(largest)))
         scale = jnp.exp2(-exponents[-1])
-        for dest in range(8):
-            out_ref[dest, rows, :] = code(sums[dest] * scale)
+        for i in range(8):
+            out_refs[i][rows, :] = code(sums[i] * scale)
     coded = exponent_tile(exponents, 128)
-    for dest in range(8):
-        out_ref[dest, 512:528, :] = coded
+    for out_ref in out_refs:
+        out_ref[512:528, :] = coded
 
 
 def merge(pieces, other):
     return pl.pallas_call(
         merge_body,
-        out_shape=struct((8, 528, 128), jnp.int16),
+        out_shape=[struct((528, 128), jnp.int16)] * 8,
         compiler_params=SMALL,
         cost_estimate=cost(10_000_000, 3_000_000),
         name="merge",
     )(pieces, other)
 
 
-def collect_body(in_ref, out_ref):
-    scales = [jnp.exp2(in_ref[i, 512:528, :].astype(F32)) for i in range(8)]
+def collect_body(*refs):
+    in_refs, out_ref = refs[:-1], refs[-1]
+    scales = [jnp.exp2(ref[512:528, :].astype(F32)) for ref in in_refs]
     for block in range(8):
         summed = jnp.zeros((64, 128), F32)
-        for i in range(8):
-            piece = in_ref[i, block * 64 : block * 64 + 64, :].astype(F32)
-            summed = summed + piece * scales[i][block : block + 1]
+        for ref, scale in zip(in_refs, scales):
+            piece = ref[block * 64 : block * 64 + 64, :].astype(F32)
+            summed = summed + piece * scale[block : block + 1]
         out_ref[:, block * 128 : block * 128 + 128] = summed
 
 
@@ -201,7 +188,7 @@
         compiler_params=SMALL,
         cost_estimate=cost(5_000_000, 2_000_000),
         name="collect",
-    )(received)
+    )(*received)
 
 
 def code_down_body(in_ref, out_ref):
@@ -269,9 +256,6 @@
 def symmetric(field, in_ref, first):
     mirrored = jnp.concatenate([unpack(in_ref, first), unpack(in_ref, first + 4)], axis=1)
     return (field + mirrored) * 0.5
-
-
-HELD = pl.BlockSpec(memory_space=pltpu.VMEM)
 
 
 def decode_body(mine_ref, other_ref, down_ref):
@@ -503,16 +487,15 @@
     mine = lax.all_to_all(code_down(downgoing), ("z",) + PLANE_CHIPS, 0, 0, tiled=True)
     count = up_time.shape[1]
     table = local_table(freq_idx, lax.axis_index(SHOT) * count, count)
-    table = table[:, None, None, :] * jnp.eye(8, dtype=BF)[None, :, :, None]
     slots = jnp.arange(128, dtype=jnp.int32)
     inverse = jnp.sum(jnp.where(node_map[:, None] == slots[None, :], slots[:, None], 0), axis=0)
-    inverse = jnp.broadcast_to(inverse[None, :], (8, 128))
-    pieces, others = transform(up_time, table.reshape(64, 256), inverse)
+    pieces, others = transform(up_time, table, inverse[None, :])
     pieces = merge(pieces, swap_cores(others))
-    mine, pieces = lax.optimization_barrier((mine, pieces))
+    received = [lax.ppermute(pieces[i], CHIPS, [(k, k ^ i) for k in range(8)]) for i in ORDER]
+    mine, received[:4] = lax.optimization_barrier((mine, received[:4]))
     down = decode(mine, swap_cores(mine))
-    received = lax.all_to_all(pieces, CHIPS, 0, 0, tiled=True)
-    data = collect(received)
+    received[4:], down = lax.optimization_barrier((received[4:], down))
+    data = collect([pieces[0], *received])
 
     field, pieces = first_adjoint(data, down)
     received = lax.all_to_all(pieces, PLANE, 0, 0, tiled=True)

time: 147 us -> 142 us (0.966)
  blocking collectives: 76.5 us -> 59 us
  waiting for transfers between devices: 19.2 us -> 27 us
  starting transfers between devices: 17.7 us -> 25 us
  Pallas kernels: 29.6 us -> 26.2 us
    ppermute x0 -> x7, waiting for transfers between devices: none -> 18.8 us  [shards(): lax.ppermute(pieces[i], CHIPS, [(k, k ^ i) for k in range(8)])]
    all_to_all x1 -> x0, blocking collectives: 18.4 us -> none  [shards(): received = lax.all_to_all(pieces, CHIPS, 0, 0, tiled=True)]
    all_to_all x1, waiting for transfers between devices: 14.1 us -> 0.01 us  [shards(): lax.all_to_all(code_down(downgoing), ('z',) + PLANE_CHIPS, 0, 0, tiled=True)]
    ppermute x0 -> x7, starting transfers between devices: none -> 9.41 us  [shards(): lax.ppermute(pieces[i], CHIPS, [(k, k ^ i) for k in range(8)])]
    pallas_call x2, Pallas kernels: 10.5 us -> 7.03 us  [the longest x1 5.81 us: transform(): pl.pallas_call(transform_body, in_specs=[HELD] * 3, out_specs=[HELD] * 2,...]
    ppermute x3, waiting for transfers between devices: 5.07 us -> 8.25 us  [swap_cores(): return lax.ppermute(x, 'core', [(0, 1), (1, 0)])]
    unnamed x6, local copies, waits for them, and re-layouts: 1.24 us -> 3.39 us
    ppermute x3, starting transfers between devices: 5.62 us -> 3.49 us  [swap_cores(): return lax.ppermute(x, 'core', [(0, 1), (1, 0)])]
  transfers between devices with their start and end apart: 4 -> 11, of which waited for: 3 -> 7; matrix products, arithmetic and copies ran while one was open for 1% -> 0% of each run, Pallas kernels for 7% -> 7%
where the time goes in v5:
time: 142 us
  blocking collectives  59 us (42%)
  waiting for transfers between devices  27 us (19%)
  Pallas kernels  26.2 us (18%)
  starting transfers between devices  25 us (18%)
  local copies, waits for them, and re-layouts  3.39 us (2%)
    all_to_all x2, blocking collectives, shards(): received = lax.all_to_all(pieces, PLANE, 0, 0, tiled=True)  28.2 us
    all_to_all x1, blocking collectives, shards(): mine = lax.all_to_all(pieces, CHIPS, 0, 0, tiled=True)  19.7 us
    ppermute x7, waiting for transfers between devices, shards(): lax.ppermute(pieces[i], CHIPS, [(k, k ^ i) for k in range(8)])  18.8 us
    all_to_all x1, starting transfers between devices, shards(): lax.all_to_all(code_down(downgoing), ('z',) + PLANE_CHIPS, 0, 0, tiled=True)  12.1 us
    all_to_all x1, blocking collectives, shards(): sums = lax.all_to_all(sums, PLANE, 0, 0, tiled=True)  11.2 us
    ppermute x7, starting transfers between devices, shards(): lax.ppermute(pieces[i], CHIPS, [(k, k ^ i) for k in range(8)])  9.41 us
    ppermute x3, waiting for transfers between devices, swap_cores(): return lax.ppermute(x, 'core', [(0, 1), (1, 0)])  8.25 us
    pallas_call x1, Pallas kernels, transform(): pl.pallas_call(transform_body, in_specs=[HELD] * 3, out_specs=[HELD] * 2,...  5.81 us
  transfers between devices with their start and end apart: 11, of which 7 were waited for; matrix products, arithmetic and copies ran while one was open for 0% of the time, Pallas kernels for 7%

profile of v5, /device:TPU:1, one launch (start us, length us, event | category | flops | bytes accessed | tf_op | source)
XLA Modules:
  0.0 141.7 jit_solution(18096797173450797174)
XLA Ops:
  0.6 2.8 %code_down.1 = s16[64,144,128]{2,1,0:T(8,128)(2,1)} custom-call(f32[4,2,64,128]{3,2,1,0:T(8,128)} %in_ref.1), custom_call_target="tpu_custom_call" | custom-call | flops 1000000 | bytes 3000000 | tf_op jit(solution)/shard_map/code_down/pallas_call | solution.py:206
  3.4 0.0 copy-start.1
  3.4 0.0 copy-start.2
  3.4 12.1 %all-to-all-start = ((s16[64,144,128]{2,1,0:T(8,128)(2,1)}), s16[64,144,128]{2,1,0:T(8,128)(2,1)S(1)}, u32[]{:S(2)}, u32[]{:S(2)}) async-start(s16[64,144,128]{2,1,0:T(8,128)(2,1)} %code_down.1), calls=%async_computation | async-start | bytes 4718592 | tf_op jit(solution)/shard_map/all_to_all | solution.py:487
  15.5 0.0 copy-done.1
  15.6 0.1 cosine_convert_fusion
  15.7 0.0 copy-done.2
  15.7 0.1 select_reduce_fusion
  15.8 0.0 copy-start
  15.8 3.4 %copy-done = bf16[1024,32,128]{2,1,0:T(8,128)(2,1)S(1)} copy-done((bf16[1024,32,128]{2,1,0:T(8,128)(2,1)S(1)}, bf16[1024,32,128]{2,1,0:T(8,128)(2,1)}, u32[]{:S(2)}) %copy-start) | copy-done | bytes 8388632
  19.2 5.8 %transform.1 = (s16[8,528,128]{2,1,0:T(8,128)(2,1)S(1)}, s16[8,528,128]{2,1,0:T(8,128)(2,1)S(1)}) custom-call(bf16[2,4,2,64,32,128]{5,4,3,2,1,0:T(8,128)(2,1)S(1)} %bitcast.8, bf16[8,32]{1,0:T(8,128)(2,1)S(1)} %bitcast.12, s32[1,128]{1,0:T(1,128)S(1)} %bitcast.13), custom_call_target="tpu_custom_call" | custom-call | flops 600000000 | bytes 10000000 | tf_op jit(solution)/shard_map/transform/pallas_call | solution.py:130
  25.0 1.0 collective-permute-start
  26.0 2.3 %collective-permute-done.other_ref = s16[8,528,128]{2,1,0:T(8,128)(2,1)S(1)} collective-permute-done((s16[8,528,128]{2,1,0:T(8,128)(2,1)S(1)}, s16[8,528,128]{2,1,0:T(8,128)(2,1)S(1)}, u32[]{:S(2)}, u32[]{:S(2)}) %collective-permute-start) | collective-permute-done | bytes 1081376 | tf_op jit(solution)/shard_map/ppermute | solution.py:483
  28.4 1.2 merge.1
  29.6 3.9 %collective-permute-start.1 = (s16[528,128]{1,0:T(8,128)(2,1)S(1)}, s16[528,128]{1,0:T(8,128)(2,1)S(1)}, u32[]{:S(2)}, u32[]{:S(2)}) collective-permute-start(s16[528,128]{1,0:T(8,128)(2,1)S(1)} %get-tuple-element.33), channel_id=1, source_target_pairs={{0,96},{16,112},{32,64},{48,80},{64,32},{80,48},{96,0},{112,16},{1... | collective-permute-start | bytes 405512 | tf_op jit(solution)/shard_map/ppermute | solution.py:494
  33.5 0.8 collective-permute-start.2
  34.3 0.0 collective-permute-start.3
  34.3 4.0 %collective-permute-start.4 = (s16[528,128]{1,0:T(8,128)(2,1)S(1)}, s16[528,128]{1,0:T(8,128)(2,1)S(1)}, u32[]{:S(2)}, u32[]{:S(2)}) collective-permute-start(s16[528,128]{1,0:T(8,128)(2,1)S(1)} %get-tuple-element.36), channel_id=1, source_target_pairs={{0,32},{16,48},{32,0},{48,16},{64,96},{80,112},{96,64},{112,80},{1... | collective-permute-start | bytes 405512 | tf_op jit(solution)/shard_map/ppermute | solution.py:494
  38.3 9.8 %collective-permute-done.1.refs_1_ = s16[528,128]{1,0:T(8,128)(2,1)S(1)} collective-permute-done((s16[528,128]{1,0:T(8,128)(2,1)S(1)}, s16[528,128]{1,0:T(8,128)(2,1)S(1)}, u32[]{:S(2)}, u32[]{:S(2)}) %collective-permute-start.1) | collective-permute-done | bytes 135200 | tf_op jit(solution)/shard_map/ppermute | solution.py:494
  48.1 3.6 %collective-permute-done.2.refs_2_ = s16[528,128]{1,0:T(8,128)(2,1)S(1)} collective-permute-done((s16[528,128]{1,0:T(8,128)(2,1)S(1)}, s16[528,128]{1,0:T(8,128)(2,1)S(1)}, u32[]{:S(2)}, u32[]{:S(2)}) %collective-permute-start.2) | collective-permute-done | bytes 135200 | tf_op jit(solution)/shard_map/ppermute | solution.py:494
  51.7 0.9 collective-permute-done.3.refs_3_
  52.6 4.4 %collective-permute-done.4.refs_4_ = s16[528,128]{1,0:T(8,128)(2,1)S(1)} collective-permute-done((s16[528,128]{1,0:T(8,128)(2,1)S(1)}, s16[528,128]{1,0:T(8,128)(2,1)S(1)}, u32[]{:S(2)}, u32[]{:S(2)}) %collective-permute-start.4) | collective-permute-done | bytes 135200 | tf_op jit(solution)/shard_map/ppermute | solution.py:494
  57.0 0.0 all-to-all-done
  57.0 0.6 collective-permute-start.8
  57.6 0.8 collective-permute-start.5
  58.4 0.0 collective-permute-start.6
  58.4 0.0 collective-permute-start.7
  58.4 3.4 %collective-permute-done.8 = s16[64,144,128]{2,1,0:T(8,128)(2,1)S(1)} collective-permute-done((s16[64,144,128]{2,1,0:T(8,128)(2,1)S(1)}, s16[64,144,128]{2,1,0:T(8,128)(2,1)S(1)}, u32[]{:S(2)}, u32[]{:S(2)}) %collective-permute-start.8) | collective-permute-done | bytes 2359328 | tf_op jit(solution)/shard_map/ppermute | solution.py:483
  61.8 2.7 %decode.1.down_ref = bf16[2,2,1024,1024]{3,2,1,0:T(8,128)(2,1)S(1)} custom-call(s16[4,8,2,144,128]{4,3,2,1,0:T(8,128)(2,1)S(1)} %bitcast.7, s16[4,8,2,144,128]{4,3,2,1,0:T(8,128)(2,1)S(1)} %bitcast.10), custom_call_target="tpu_custom_call" | custom-call | flops 20000000 | bytes 13000000 | tf_op jit(solution)/shard_map/decode/pallas_call | solution.py:279
  64.5 0.0 collective-permute-done.5.refs_5_
  64.5 0.0 collective-permute-done.6.refs_6_
  64.5 0.0 collective-permute-done.7.refs_7_
  64.6 0.3 collect.1.data_ref
  64.8 1.7 %first_adjoint.1 = (f32[64,1024]{1,0:T(8,128)S(1)}, f32[32,16,128]{2,1,0:T(8,128)S(1)}) custom-call(f32[64,1024]{1,0:T(8,128)S(1)} %collect.1.data_ref, bf16[2,2,1024,1024]{3,2,1,0:T(8,128)(2,1)S(1)} %decode.1.down_ref), custom_call_target="tpu_custom_call" | custom-call | flops 800000000 | bytes 9000000 | tf_op jit(solution)/shard_map/first_adjoint/pallas_call | solution.py:300
  66.5 14.4 %all_to_all.25.in_ref = f32[32,16,128]{2,1,0:T(8,128)S(1)} all-to-all(f32[32,16,128]{2,1,0:T(8,128)S(1)} %get-tuple-element.50), channel_id=1, replica_groups=mesh['xl'=2,'z'=4,'core'=2,'y'=4,'xh'=2] {'y','xh','xl','core'}, dimensions={0} | all-to-all | bytes 524288 | tf_op jit(solution)/shard_map/all_to_all | solution.py:501
  81.0 4.6 %second.1 = (f32[64,1024]{1,0:T(8,128)S(1)}, f32[64,1024]{1,0:T(8,128)S(1)}, f32[64,1024]{1,0:T(8,128)S(1)}, f32[32,24,128]{2,1,0:T(8,128)S(1)}) custom-call(f32[64,1024]{1,0:T(8,128)S(1)} %get-tuple-element.49.field_ref, f32[32,16,128]{2,1,0:T(8,128)S(1)} %all_to_all.25.in_ref, bf16[2,2,1024,1024]{3,2,1,0:T(8,128)(2,1)S(1)} %decode.1.down_ref), custom_call_target="tpu_custom_call" | custom-call | flops 1600000000 | bytes 18000000 | tf_op jit(solution)/shard_map/second/pallas_call | solution.py:333
  85.6 13.7 %all_to_all.26.in_ref = f32[32,24,128]{2,1,0:T(8,128)S(1)} all-to-all(f32[32,24,128]{2,1,0:T(8,128)S(1)} %get-tuple-element.54), channel_id=1, replica_groups=mesh['xl'=2,'z'=4,'core'=2,'y'=4,'xh'=2] {'y','xh','xl','core'}, dimensions={0} | all-to-all | bytes 786432 | tf_op jit(solution)/shard_map/all_to_all | solution.py:503
  99.3 3.1 %change.1 = (f32[64,1024]{1,0:T(8,128)S(1)}, f32[64,1024]{1,0:T(8,128)S(1)}, f32[32,8,128]{2,1,0:T(8,128)S(1)}) custom-call(f32[64,1024]{1,0:T(8,128)S(1)} %get-tuple-element.51.gradient_ref, f32[64,1024]{1,0:T(8,128)S(1)} %get-tuple-element.52.field_ref, f32[64,1024]{1,0:T(8,128)S(1)} %get-tuple-element.53.image_ref, f32[32,24,128]{2,1,0:T(8,128)S(1)} %all_to_all.26.in_ref, ...), custom_call_target="tpu_custom_call" | custom-call | flops 800000000 | bytes 9000000 | tf_op jit(solution)/shard_map/change/pallas_call | solution.py:373
  102.4 11.2 %all_to_all.27.sums_ref = f32[32,8,128]{2,1,0:T(8,128)S(1)} all-to-all(f32[32,8,128]{2,1,0:T(8,128)S(1)} %get-tuple-element.57), channel_id=1, replica_groups=mesh['xl'=2,'z'=4,'core'=2,'y'=4,'xh'=2] {'y','xh','xl','core'}, dimensions={0} | all-to-all | bytes 262144 | tf_op jit(solution)/shard_map/all_to_all | solution.py:505
  113.6 1.0 update.1
  114.6 19.7 %all_to_all.28 = s16[8,592,128]{2,1,0:T(8,128)(2,1)S(1)} all-to-all(s16[8,592,128]{2,1,0:T(8,128)(2,1)S(1)} %update.1), channel_id=1, replica_groups=mesh['xl'=2,'z'=4,'core'=2,'y'=4,'xh'=2] {'xl','z'}, dimensions={0} | all-to-all | bytes 2424832 | tf_op jit(solution)/shard_map/all_to_all | solution.py:507
  134.3 1.9 %collective-permute-start.9 = (s16[8,592,128]{2,1,0:T(8,128)(2,1)S(1)}, s16[8,592,128]{2,1,0:T(8,128)(2,1)S(1)}, u32[]{:S(2)}, u32[]{:S(2)}) collective-permute-start(s16[8,592,128]{2,1,0:T(8,128)(2,1)S(1)} %all_to_all.28), channel_id=1, source_target_pairs={{0,8},{8,0},{1,9},{9,1},{2,10},{10,2},{3,11},{11,3},{4,12},{12,4},... | collective-permute-start | bytes 3637256 | tf_op jit(solution)/shard_map/ppermute | solution.py:483
  136.2 2.5 %collective-permute-done.9 = s16[8,592,128]{2,1,0:T(8,128)(2,1)S(1)} collective-permute-done((s16[8,592,128]{2,1,0:T(8,128)(2,1)S(1)}, s16[8,592,128]{2,1,0:T(8,128)(2,1)S(1)}, u32[]{:S(2)}, u32[]{:S(2)}) %collective-permute-start.9) | collective-permute-done | bytes 1212448 | tf_op jit(solution)/shard_map/ppermute | solution.py:483
  138.7 3.0 %finish.1 = (f32[4,2,1024,128]{3,2,1,0:T(8,128)}, f32[4,2,64,128]{3,2,1,0:T(8,128)}) custom-call(s16[2,4,592,128]{3,2,1,0:T(8,128)(2,1)S(1)} %bitcast.9, s16[2,4,592,128]{3,2,1,0:T(8,128)(2,1)S(1)} %bitcast.11), custom_call_target="tpu_custom_call" | custom-call | flops 10000000 | bytes 7000000 | tf_op jit(solution)/shard_map/finish/pallas_call | solution.py:467
  (3 shorter events, 0.0 us)
Async XLA Ops:
  3.4 12.1 %copy-start.1 = (s32[4]{0:T(128)S(1)}, s32[4]{0:T(128)}, u32[]{:S(2)}) copy-start(s32[4]{0:T(128)} %param.6) | copy-start | bytes 52
  3.4 12.3 %copy-start.2 = (s32[128]{0:T(128)S(1)}, s32[128]{0:T(128)}, u32[]{:S(2)}) copy-start(s32[128]{0:T(128)} %param.7) | copy-start | bytes 1540
  3.4 53.6 %all-to-all-start = ((s16[64,144,128]{2,1,0:T(8,128)(2,1)}), s16[64,144,128]{2,1,0:T(8,128)(2,1)S(1)}, u32[]{:S(2)}, u32[]{:S(2)}) async-start(s16[64,144,128]{2,1,0:T(8,128)(2,1)} %code_down.1), calls=%async_computation | async-start | bytes 4718592 | tf_op jit(solution)/shard_map/all_to_all | solution.py:487
  15.8 3.4 %copy-start = (bf16[1024,32,128]{2,1,0:T(8,128)(2,1)S(1)}, bf16[1024,32,128]{2,1,0:T(8,128)(2,1)}, u32[]{:S(2)}) copy-start(bf16[1024,32,128]{2,1,0:T(8,128)(2,1)} %param.4) | copy-start | bytes 25165828
  25.0 3.4 %collective-permute-start = (s16[8,528,128]{2,1,0:T(8,128)(2,1)S(1)}, s16[8,528,128]{2,1,0:T(8,128)(2,1)S(1)}, u32[]{:S(2)}, u32[]{:S(2)}) collective-permute-start(s16[8,528,128]{2,1,0:T(8,128)(2,1)S(1)} %get-tuple-element.31), channel_id=1, source_target_pairs={{0,8},{8,0},{1,9},{9,1},{2,10},{10,2},{3,11},{11,3},{4,12},{12,4},... | collective-permute-start | bytes 3244040 | tf_op jit(solution)/shard_map/ppermute | solution.py:483
  29.6 18.5 %collective-permute-start.1 = (s16[528,128]{1,0:T(8,128)(2,1)S(1)}, s16[528,128]{1,0:T(8,128)(2,1)S(1)}, u32[]{:S(2)}, u32[]{:S(2)}) collective-permute-start(s16[528,128]{1,0:T(8,128)(2,1)S(1)} %get-tuple-element.33), channel_id=1, source_target_pairs={{0,96},{16,112},{32,64},{48,80},{64,32},{80,48},{96,0},{112,16},{1... | collective-permute-start | bytes 405512 | tf_op jit(solution)/shard_map/ppermute | solution.py:494
  33.5 18.2 %collective-permute-start.2 = (s16[528,128]{1,0:T(8,128)(2,1)S(1)}, s16[528,128]{1,0:T(8,128)(2,1)S(1)}, u32[]{:S(2)}, u32[]{:S(2)}) collective-permute-start(s16[528,128]{1,0:T(8,128)(2,1)S(1)} %get-tuple-element.34), channel_id=1, source_target_pairs={{0,112},{16,96},{32,80},{48,64},{64,48},{80,32},{96,16},{112,0},{1... | collective-permute-start | bytes 405512 | tf_op jit(solution)/shard_map/ppermute | solution.py:494
  34.3 18.3 %collective-permute-start.3 = (s16[528,128]{1,0:T(8,128)(2,1)S(1)}, s16[528,128]{1,0:T(8,128)(2,1)S(1)}, u32[]{:S(2)}, u32[]{:S(2)}) collective-permute-start(s16[528,128]{1,0:T(8,128)(2,1)S(1)} %get-tuple-element.35), channel_id=1, source_target_pairs={{0,80},{16,64},{32,112},{48,96},{64,16},{80,0},{96,48},{112,32},{1... | collective-permute-start | bytes 405512 | tf_op jit(solution)/shard_map/ppermute | solution.py:494
  34.3 22.8 %collective-permute-start.4 = (s16[528,128]{1,0:T(8,128)(2,1)S(1)}, s16[528,128]{1,0:T(8,128)(2,1)S(1)}, u32[]{:S(2)}, u32[]{:S(2)}) collective-permute-start(s16[528,128]{1,0:T(8,128)(2,1)S(1)} %get-tuple-element.36), channel_id=1, source_target_pairs={{0,32},{16,48},{32,0},{48,16},{64,96},{80,112},{96,64},{112,80},{1... | collective-permute-start | bytes 405512 | tf_op jit(solution)/shard_map/ppermute | solution.py:494
  57.0 4.8 %collective-permute-start.8 = (s16[64,144,128]{2,1,0:T(8,128)(2,1)S(1)}, s16[64,144,128]{2,1,0:T(8,128)(2,1)S(1)}, u32[]{:S(2)}, u32[]{:S(2)}) collective-permute-start(s16[64,144,128]{2,1,0:T(8,128)(2,1)S(1)} %all-to-all-done), channel_id=1, source_target_pairs={{0,8},{8,0},{1,9},{9,1},{2,10},{10,2},{3,11},{11,3},{4,12},{12,4},... | collective-permute-start | bytes 7077896 | tf_op jit(solution)/shard_map/ppermute | solution.py:483
  57.6 6.9 %collective-permute-start.5 = (s16[528,128]{1,0:T(8,128)(2,1)S(1)}, s16[528,128]{1,0:T(8,128)(2,1)S(1)}, u32[]{:S(2)}, u32[]{:S(2)}) collective-permute-start(s16[528,128]{1,0:T(8,128)(2,1)S(1)} %get-tuple-element.41), channel_id=1, source_target_pairs={{0,48},{16,32},{32,16},{48,0},{64,112},{80,96},{96,80},{112,64},{1... | collective-permute-start | bytes 405512 | tf_op jit(solution)/shard_map/ppermute | solution.py:494
  58.4 6.1 %collective-permute-start.6 = (s16[528,128]{1,0:T(8,128)(2,1)S(1)}, s16[528,128]{1,0:T(8,128)(2,1)S(1)}, u32[]{:S(2)}, u32[]{:S(2)}) collective-permute-start(s16[528,128]{1,0:T(8,128)(2,1)S(1)} %get-tuple-element.42), channel_id=1, source_target_pairs={{0,16},{16,0},{32,48},{48,32},{64,80},{80,64},{96,112},{112,96},{1... | collective-permute-start | bytes 405512 | tf_op jit(solution)/shard_map/ppermute | solution.py:494
  58.4 6.1 %collective-permute-start.7 = (s16[528,128]{1,0:T(8,128)(2,1)S(1)}, s16[528,128]{1,0:T(8,128)(2,1)S(1)}, u32[]{:S(2)}, u32[]{:S(2)}) collective-permute-start(s16[528,128]{1,0:T(8,128)(2,1)S(1)} %get-tuple-element.43), channel_id=1, source_target_pairs={{0,64},{16,80},{32,96},{48,112},{64,0},{80,16},{96,32},{112,48},{1... | collective-permute-start | bytes 405512 | tf_op jit(solution)/shard_map/ppermute | solution.py:494
  134.3 4.4 %collective-permute-start.9 = (s16[8,592,128]{2,1,0:T(8,128)(2,1)S(1)}, s16[8,592,128]{2,1,0:T(8,128)(2,1)S(1)}, u32[]{:S(2)}, u32[]{:S(2)}) collective-permute-start(s16[8,592,128]{2,1,0:T(8,128)(2,1)S(1)} %all_to_all.28), channel_id=1, source_target_pairs={{0,8},{8,0},{1,9},{9,1},{2,10},{10,2},{3,11},{11,3},{4,12},{12,4},... | collective-permute-start | bytes 3637256 | tf_op jit(solution)/shard_map/ppermute | solution.py:483

commit v6 on v5

--- a/solution.py
+++ b/solution.py
@@ -14,7 +14,7 @@
 NODE = ("y", "xh")
 CHIPS = ("xl", "z")
 ORDER = (6, 7, 5, 2, 3, 1, 4)
-PLANE_CHIPS = ("y", "xh", "xl")
+ALL_CHIPS = ("xl", "xh", "y", "z")
 PLANE = ("y", "xh", "xl", "core")
 BF = jnp.bfloat16
 F32 = jnp.float32
@@ -191,21 +191,28 @@
     )(*received)
 
 
-def code_down_body(in_ref, out_ref):
+def code_down_body(in_ref, out_ref, coded, sent):
     for f in range(F):
         field = in_ref[f].reshape(128, 128)
         exponent = exponent_of(peak_of(field))
-        coded = code(field * jnp.exp2(-exponent))
-        tile = exponent_tile([exponent], 128)
-        for i in range(16):
-            out_ref[f * 16 + i, 0:128, :] = coded
-            out_ref[f * 16 + i, 128:144, :] = tile
+        coded[f, 0:128, :] = code(field * jnp.exp2(-exponent))
+        coded[f, 128:144, :] = exponent_tile([exponent], 128)
+    copies = [
+        pltpu.make_async_copy(coded, out_ref.at[pl.ds(i * F, F)], sent.at[i]) for i in range(16)
+    ]
+    for copy in copies:
+        copy.start()
+    for copy in copies:
+        copy.wait()
 
 
 def code_down(downgoing):
     return pl.pallas_call(
         code_down_body,
+        in_specs=[HELD],
+        out_specs=pl.BlockSpec(memory_space=pl.ANY),
         out_shape=struct((64, 144, 128), jnp.int16),
+        scratch_shapes=[pltpu.VMEM((F, 144, 128), jnp.int16), pltpu.SemaphoreType.DMA((16,))],
         compiler_params=FULL,
         cost_estimate=cost(1_000_000, 3_000_000),
         name="code_down",
@@ -236,15 +243,20 @@
     return jnp.concatenate(split(field.T), axis=1)
 
 
-def pack(field, out_ref, first):
+def pack(field, out_ref, first, scale=None):
     turned = field.T
     for k in range(8):
         piece = turned[k * 32 : k * 32 + 32]
-        out_ref[first + k, 0:16, :] = jnp.concatenate([piece[:16], piece[16:]], axis=1)
+        piece = jnp.concatenate([piece[:16], piece[16:]], axis=1)
+        out_ref[first + k, 0:16, :] = piece if scale is None else code(piece * scale)
 
 
 def unpack(in_ref, first):
-    pieces = [in_ref[first + k, 0:16, :] for k in range(4)]
+    pieces = [in_ref[first + k, 0:16, :].astype(F32) for k in range(4)]
+    if in_ref.dtype == jnp.int16:
+        for k in range(4):
+            scale = jnp.exp2(in_ref[first + k, 16:32, :].astype(F32)[0:1])
+            pieces[k] = pieces[k] * scale
     rows = []
     for c in range(2):
         for half in range(2):
@@ -265,11 +277,11 @@
         for source, core in ((mine_ref, me), (other_ref, 1 - me)):
             for x in range(2):
                 for z in range(4):
-                    scale = jnp.exp2(source[z, n, x, 128:144, :].astype(F32))[0:1]
+                    scale = jnp.exp2(source[x, n % 2, n // 2, z, 128:144, :].astype(F32))[0:1]
                     first = x * 512 + core * 256 + z * 64
                     rows = pl.ds(pl.multiple_of(first, 64), 64)
                     for c in range(2):
-                        field = source[z, n, x, c * 64 : c * 64 + 64, :].astype(F32) * scale
+                        field = source[x, n % 2, n // 2, z, c * 64 : c * 64 + 64, :].astype(F32) * scale
                         high, low = split(field)
                         down_ref[0, c, rows, lanes] = high
                         down_ref[1, c, rows, lanes] = low
@@ -284,7 +296,7 @@
         compiler_params=SMALL,
         cost_estimate=cost(20_000_000, 13_000_000),
         name="decode",
-    )(mine.reshape(4, 8, 2, 144, 128), other.reshape(4, 8, 2, 144, 128))
+    )(mine.reshape(2, 2, 4, 4, 144, 128), other.reshape(2, 2, 4, 4, 144, 128))
 
 
 def first_adjoint_body(data_ref, down_ref, field_ref, pieces_ref):
@@ -319,14 +331,20 @@
         image_ref[:, at] = image
         both[:, at] = stacked_split(image)
     gradient, image = gradient_ref[...], image_ref[...]
-    rows = [lanes_sum(gradient * gradient), lanes_sum(image * image), jnp.zeros((6, 128), F32)]
-    norm = jnp.concatenate(rows, axis=0)
+    for at in blocks:
+        again_ref[:, at] = adjoint_step(down_ref, both[...], at)
+    exponent = exponent_of(peak_of(again_ref[...]))
+    rows = [exponent]
+    for row in (lanes_sum(gradient * gradient), lanes_sum(image * image)):
+        rows.append(exponent_of(peak_of(row)))
+        scaled = row * jnp.exp2(-rows[-1])
+        rows.append(jnp.minimum(jnp.floor(scaled), 32767.0))
+        rows.append(jnp.minimum(jnp.floor((scaled - rows[-1]) * 32768.0), 32767.0))
+    tile = exponent_tile(rows, 128)
     for i, at in enumerate(blocks):
-        field = adjoint_step(down_ref, both[...], at)
-        again_ref[:, at] = field
-        pack(field, out_ref, i * 8)
+        pack(again_ref[:, at], out_ref, i * 8, jnp.exp2(-exponent))
     for k in range(32):
-        out_ref[k, 16:24, :] = norm
+        out_ref[k, 16:32, :] = tile
 
 
 def second(field, received, down):
@@ -334,7 +352,7 @@
         second_body,
         in_specs=[HELD] * 3,
         out_specs=[HELD] * 4,
-        out_shape=[struct((64, 1024))] * 3 + [struct((32, 24, 128))],
+        out_shape=[struct((64, 1024))] * 3 + [struct((32, 32, 128), jnp.int16)],
         scratch_shapes=[pltpu.VMEM((1024, 128), BF), pltpu.VMEM((128, 1024), BF)],
         compiler_params=SMALL,
         cost_estimate=cost(1_600_000_000, 18_000_000),
@@ -343,9 +361,14 @@
 
 
 def first_step(in_ref):
-    norm = total(jnp.sum(in_ref[:, 16:17, :], axis=0))
-    curvature = total(jnp.sum(in_ref[:, 17:18, :], axis=0))
-    return norm, curvature
+    sums = [jnp.zeros((1, 128), F32)] * 2
+    for k in range(32):
+        tile = in_ref[k, 16:32, :].astype(F32)
+        for i in range(2):
+            at = 1 + 3 * i
+            value = tile[at + 1 : at + 2] + tile[at + 2 : at + 3] * (1.0 / 32768.0)
+            sums[i] = sums[i] + value * jnp.exp2(tile[at : at + 1])
+    return total(sums[0]), total(sums[1])
 
 
 def change_body(
@@ -408,7 +431,7 @@
     for dest in range(8):
         out_ref[dest, 0:512, :] = coded
         for core in range(2):
-            at = (dest // 4 * 2 + core) * 256 + dest % 4 * 64
+            at = (dest % 2 * 2 + core) * 256 + dest // 2 * 64
             piece = jnp.concatenate([turned[at : at + 32], turned[at + 32 : at + 64]], axis=1)
             out_ref[dest, 512 + core * 32 : 544 + core * 32, :] = code(piece)
         out_ref[dest, 576:592, :] = tile
@@ -425,7 +448,7 @@
 
 
 def place(f, first_ref, second_ref, core, reflectivity_ref, residual_ref):
-    refs = [ref.at[x, f] for x in range(2) for ref in (first_ref, second_ref)]
+    refs = [ref.at[f, x] for x in range(2) for ref in (first_ref, second_ref)]
     scales = [jnp.exp2(ref[576:592, :].astype(F32)) for ref in refs]
     owner = lax.broadcasted_iota(jnp.int32, (64, 128), 1) // 32
     spread = scales[3][0:1]
@@ -476,7 +499,7 @@
         compiler_params=SMALL,
         cost_estimate=cost(10_000_000, 7_000_000),
         name="finish",
-    )(mine.reshape(2, F, 592, 128), other.reshape(2, F, 592, 128))
+    )(mine.reshape(F, 2, 592, 128), other.reshape(F, 2, 592, 128))
 
 
 def swap_cores(x):
@@ -484,7 +507,7 @@
 
 
 def shards(up_time, downgoing, freq_idx, node_map):
-    mine = lax.all_to_all(code_down(downgoing), ("z",) + PLANE_CHIPS, 0, 0, tiled=True)
+    mine = lax.all_to_all(code_down(downgoing), ALL_CHIPS, 0, 0, tiled=True)
     count = up_time.shape[1]
     table = local_table(freq_idx, lax.axis_index(SHOT) * count, count)
     slots = jnp.arange(128, dtype=jnp.int32)
@@ -504,7 +527,7 @@
     again, change, sums = changed(gradient, field, image, received, down)
     sums = lax.all_to_all(sums, PLANE, 0, 0, tiled=True)
     pieces = updated(data, gradient, again, image, change, received, sums)
-    mine = lax.all_to_all(pieces, CHIPS, 0, 0, tiled=True)
+    mine = lax.all_to_all(pieces, ("z", "xl"), 0, 0, tiled=True)
     return tuple(finish(mine, swap_cores(mine)))
 
 

time: 142 us -> 140 us (0.986)
  waiting for transfers between devices: 27 us -> 24 us
  starting transfers between devices: 25 us -> 27.2 us
    ppermute x7, starting transfers between devices: 9.41 us -> 11.8 us  [shards(): lax.ppermute(pieces[i], CHIPS, [(k, k ^ i) for k in range(8)])]
    ppermute x3, waiting for transfers between devices: 8.25 us -> 5.89 us  [swap_cores(): return lax.ppermute(x, 'core', [(0, 1), (1, 0)])]
  transfers between devices with their start and end apart: 11 -> 11, of which waited for: 7 -> 9; matrix products, arithmetic and copies ran while one was open for 0% -> 0% of each run, Pallas kernels for 7% -> 7%
where the time goes in v6:
time: 140 us
  blocking collectives  58.2 us (42%)
  starting transfers between devices  27.2 us (19%)
  Pallas kernels  26.2 us (19%)
  waiting for transfers between devices  24 us (17%)
  local copies, waits for them, and re-layouts  3.4 us (2%)
    all_to_all x2, blocking collectives, shards(): received = lax.all_to_all(pieces, PLANE, 0, 0, tiled=True)  27.2 us
    all_to_all x1, blocking collectives, shards(): mine = lax.all_to_all(pieces, ('z', 'xl'), 0, 0, tiled=True)  19.9 us
    ppermute x7, waiting for transfers between devices, shards(): lax.ppermute(pieces[i], CHIPS, [(k, k ^ i) for k in range(8)])  18.1 us
    all_to_all x1, starting transfers between devices, shards(): mine = lax.all_to_all(code_down(downgoing), ALL_CHIPS, 0, 0, tiled=True)  12 us
    ppermute x7, starting transfers between devices, shards(): lax.ppermute(pieces[i], CHIPS, [(k, k ^ i) for k in range(8)])  11.8 us
    all_to_all x1, blocking collectives, shards(): sums = lax.all_to_all(sums, PLANE, 0, 0, tiled=True)  11.2 us
    ppermute x3, waiting for transfers between devices, swap_cores(): return lax.ppermute(x, 'core', [(0, 1), (1, 0)])  5.89 us
    pallas_call x1, Pallas kernels, transform(): pl.pallas_call(transform_body, in_specs=[HELD] * 3, out_specs=[HELD] * 2,...  5.81 us
  transfers between devices with their start and end apart: 11, of which 9 were waited for; matrix products, arithmetic and copies ran while one was open for 0% of the time, Pallas kernels for 7%

profile of v6, /device:TPU:1, one launch (start us, length us, event | category | flops | bytes accessed | tf_op | source)
XLA Modules:
  0.0 140.0 jit_solution(3202714445329923346)
XLA Ops:
  0.6 2.7 %code_down.1 = s16[64,144,128]{2,1,0:T(8,128)(2,1)} custom-call(f32[4,2,64,128]{3,2,1,0:T(8,128)} %in_ref.1), custom_call_target="tpu_custom_call" | custom-call | flops 1000000 | bytes 3000000 | tf_op jit(solution)/shard_map/code_down/pallas_call | solution.py:210
  3.3 0.0 copy-start.1
  3.3 0.0 copy-start.2
  3.3 12.0 %all-to-all-start = ((s16[64,144,128]{2,1,0:T(8,128)(2,1)}), s16[64,144,128]{2,1,0:T(8,128)(2,1)S(1)}, u32[]{:S(2)}, u32[]{:S(2)}) async-start(s16[64,144,128]{2,1,0:T(8,128)(2,1)} %code_down.1), calls=%async_computation | async-start | bytes 4718592 | tf_op jit(solution)/shard_map/all_to_all | solution.py:510
  15.3 0.0 copy-done.1
  15.4 0.1 cosine_convert_fusion
  15.5 0.0 copy-done.2
  15.5 0.1 select_reduce_fusion
  15.6 0.0 copy-start
  15.6 3.4 %copy-done = bf16[1024,32,128]{2,1,0:T(8,128)(2,1)S(1)} copy-done((bf16[1024,32,128]{2,1,0:T(8,128)(2,1)S(1)}, bf16[1024,32,128]{2,1,0:T(8,128)(2,1)}, u32[]{:S(2)}) %copy-start) | copy-done | bytes 8388632
  19.0 5.8 %transform.1 = (s16[8,528,128]{2,1,0:T(8,128)(2,1)S(1)}, s16[8,528,128]{2,1,0:T(8,128)(2,1)S(1)}) custom-call(bf16[2,4,2,64,32,128]{5,4,3,2,1,0:T(8,128)(2,1)S(1)} %bitcast.8, bf16[8,32]{1,0:T(8,128)(2,1)S(1)} %bitcast.12, s32[1,128]{1,0:T(1,128)S(1)} %bitcast.13), custom_call_target="tpu_custom_call" | custom-call | flops 600000000 | bytes 10000000 | tf_op jit(solution)/shard_map/transform/pallas_call | solution.py:130
  24.8 1.0 collective-permute-start
  25.9 2.3 %collective-permute-done.other_ref = s16[8,528,128]{2,1,0:T(8,128)(2,1)S(1)} collective-permute-done((s16[8,528,128]{2,1,0:T(8,128)(2,1)S(1)}, s16[8,528,128]{2,1,0:T(8,128)(2,1)S(1)}, u32[]{:S(2)}, u32[]{:S(2)}) %collective-permute-start) | collective-permute-done | bytes 1081376 | tf_op jit(solution)/shard_map/ppermute | solution.py:506
  28.2 1.2 merge.1
  29.4 3.9 %collective-permute-start.1 = (s16[528,128]{1,0:T(8,128)(2,1)S(1)}, s16[528,128]{1,0:T(8,128)(2,1)S(1)}, u32[]{:S(2)}, u32[]{:S(2)}) collective-permute-start(s16[528,128]{1,0:T(8,128)(2,1)S(1)} %get-tuple-element.33), channel_id=1, source_target_pairs={{0,96},{16,112},{32,64},{48,80},{64,32},{80,48},{96,0},{112,16},{1... | collective-permute-start | bytes 405512 | tf_op jit(solution)/shard_map/ppermute | solution.py:517
  33.3 0.8 collective-permute-start.2
  34.1 0.1 collective-permute-start.3
  34.2 3.9 %collective-permute-start.4 = (s16[528,128]{1,0:T(8,128)(2,1)S(1)}, s16[528,128]{1,0:T(8,128)(2,1)S(1)}, u32[]{:S(2)}, u32[]{:S(2)}) collective-permute-start(s16[528,128]{1,0:T(8,128)(2,1)S(1)} %get-tuple-element.36), channel_id=1, source_target_pairs={{0,32},{16,48},{32,0},{48,16},{64,96},{80,112},{96,64},{112,80},{1... | collective-permute-start | bytes 405512 | tf_op jit(solution)/shard_map/ppermute | solution.py:517
  38.1 9.6 %collective-permute-done.1.refs_1_ = s16[528,128]{1,0:T(8,128)(2,1)S(1)} collective-permute-done((s16[528,128]{1,0:T(8,128)(2,1)S(1)}, s16[528,128]{1,0:T(8,128)(2,1)S(1)}, u32[]{:S(2)}, u32[]{:S(2)}) %collective-permute-start.1) | collective-permute-done | bytes 135200 | tf_op jit(solution)/shard_map/ppermute | solution.py:517
  47.7 4.2 %collective-permute-done.2.refs_2_ = s16[528,128]{1,0:T(8,128)(2,1)S(1)} collective-permute-done((s16[528,128]{1,0:T(8,128)(2,1)S(1)}, s16[528,128]{1,0:T(8,128)(2,1)S(1)}, u32[]{:S(2)}, u32[]{:S(2)}) %collective-permute-start.2) | collective-permute-done | bytes 135200 | tf_op jit(solution)/shard_map/ppermute | solution.py:517
  51.8 1.5 %collective-permute-done.3.refs_3_ = s16[528,128]{1,0:T(8,128)(2,1)S(1)} collective-permute-done((s16[528,128]{1,0:T(8,128)(2,1)S(1)}, s16[528,128]{1,0:T(8,128)(2,1)S(1)}, u32[]{:S(2)}, u32[]{:S(2)}) %collective-permute-start.3) | collective-permute-done | bytes 135200 | tf_op jit(solution)/shard_map/ppermute | solution.py:517
  53.3 1.8 %collective-permute-done.4.refs_4_ = s16[528,128]{1,0:T(8,128)(2,1)S(1)} collective-permute-done((s16[528,128]{1,0:T(8,128)(2,1)S(1)}, s16[528,128]{1,0:T(8,128)(2,1)S(1)}, u32[]{:S(2)}, u32[]{:S(2)}) %collective-permute-start.4) | collective-permute-done | bytes 135200 | tf_op jit(solution)/shard_map/ppermute | solution.py:517
  55.1 0.0 all-to-all-done
  55.2 0.9 collective-permute-start.8
  56.0 2.8 %collective-permute-start.5 = (s16[528,128]{1,0:T(8,128)(2,1)S(1)}, s16[528,128]{1,0:T(8,128)(2,1)S(1)}, u32[]{:S(2)}, u32[]{:S(2)}) collective-permute-start(s16[528,128]{1,0:T(8,128)(2,1)S(1)} %get-tuple-element.41), channel_id=1, source_target_pairs={{0,48},{16,32},{32,16},{48,0},{64,112},{80,96},{96,80},{112,64},{1... | collective-permute-start | bytes 405512 | tf_op jit(solution)/shard_map/ppermute | solution.py:517
  58.9 0.2 collective-permute-start.6
  59.1 0.1 collective-permute-start.7
  59.2 1.0 collective-permute-done.8
  60.2 2.7 %decode.1.down_ref = bf16[2,2,1024,1024]{3,2,1,0:T(8,128)(2,1)S(1)} custom-call(s16[2,2,4,4,144,128]{5,4,3,2,1,0:T(8,128)(2,1)S(1)} %bitcast.7, s16[2,2,4,4,144,128]{5,4,3,2,1,0:T(8,128)(2,1)S(1)} %bitcast.10), custom_call_target="tpu_custom_call" | custom-call | flops 20000000 | bytes 13000000 | tf_op jit(solution)/shard_map/decode/pallas_call | solution.py:291
  62.9 0.0 collective-permute-done.5.refs_5_
  62.9 0.8 collective-permute-done.6.refs_6_
  63.7 0.2 collective-permute-done.7.refs_7_
  63.9 0.3 collect.1.data_ref
  64.2 1.7 %first_adjoint.1 = (f32[64,1024]{1,0:T(8,128)S(1)}, f32[32,16,128]{2,1,0:T(8,128)S(1)}) custom-call(f32[64,1024]{1,0:T(8,128)S(1)} %collect.1.data_ref, bf16[2,2,1024,1024]{3,2,1,0:T(8,128)(2,1)S(1)} %decode.1.down_ref), custom_call_target="tpu_custom_call" | custom-call | flops 800000000 | bytes 9000000 | tf_op jit(solution)/shard_map/first_adjoint/pallas_call | solution.py:312
  65.8 14.7 %all_to_all.25.in_ref = f32[32,16,128]{2,1,0:T(8,128)S(1)} all-to-all(f32[32,16,128]{2,1,0:T(8,128)S(1)} %get-tuple-element.50), channel_id=1, replica_groups=mesh['xl'=2,'z'=4,'core'=2,'y'=4,'xh'=2] {'y','xh','xl','core'}, dimensions={0} | all-to-all | bytes 524288 | tf_op jit(solution)/shard_map/all_to_all | solution.py:524
  80.6 4.7 %second.1 = (f32[64,1024]{1,0:T(8,128)S(1)}, f32[64,1024]{1,0:T(8,128)S(1)}, f32[64,1024]{1,0:T(8,128)S(1)}, s16[32,32,128]{2,1,0:T(8,128)(2,1)S(1)}) custom-call(f32[64,1024]{1,0:T(8,128)S(1)} %get-tuple-element.49.field_ref, f32[32,16,128]{2,1,0:T(8,128)S(1)} %all_to_all.25.in_ref, bf16[2,2,1024,1024]{3,2,1,0:T(8,128)(2,1)S(1)} %decode.1.down_ref), custom_call_target="tpu_custom_call" | custom-call | flops 1600000000 | bytes 18000000 | tf_op jit(solution)/shard_map/second/pallas_call | solution.py:351
  85.3 12.4 %all_to_all.26.in_ref = s16[32,32,128]{2,1,0:T(8,128)(2,1)S(1)} all-to-all(s16[32,32,128]{2,1,0:T(8,128)(2,1)S(1)} %get-tuple-element.54), channel_id=1, replica_groups=mesh['xl'=2,'z'=4,'core'=2,'y'=4,'xh'=2] {'y','xh','xl','core'}, dimensions={0} | all-to-all | bytes 524288 | tf_op jit(solution)/shard_map/all_to_all | solution.py:526
  97.7 3.1 %change.1 = (f32[64,1024]{1,0:T(8,128)S(1)}, f32[64,1024]{1,0:T(8,128)S(1)}, f32[32,8,128]{2,1,0:T(8,128)S(1)}) custom-call(f32[64,1024]{1,0:T(8,128)S(1)} %get-tuple-element.51.gradient_ref, f32[64,1024]{1,0:T(8,128)S(1)} %get-tuple-element.52.field_ref, f32[64,1024]{1,0:T(8,128)S(1)} %get-tuple-element.53.image_ref, ...), custom_call_target="tpu_custom_call" | custom-call | flops 800000000 | bytes 9000000 | tf_op jit(solution)/shard_map/change/pallas_call | solution.py:396
  100.8 11.2 %all_to_all.27.sums_ref = f32[32,8,128]{2,1,0:T(8,128)S(1)} all-to-all(f32[32,8,128]{2,1,0:T(8,128)S(1)} %get-tuple-element.57), channel_id=1, replica_groups=mesh['xl'=2,'z'=4,'core'=2,'y'=4,'xh'=2] {'y','xh','xl','core'}, dimensions={0} | all-to-all | bytes 262144 | tf_op jit(solution)/shard_map/all_to_all | solution.py:528
  112.0 1.1 update.1
  113.1 19.9 %all_to_all.28 = s16[8,592,128]{2,1,0:T(8,128)(2,1)S(1)} all-to-all(s16[8,592,128]{2,1,0:T(8,128)(2,1)S(1)} %update.1), channel_id=1, replica_groups=mesh['xl'=2,'z'=4,'core'=2,'y'=4,'xh'=2] {'z','xl'}, dimensions={0} | all-to-all | bytes 2424832 | tf_op jit(solution)/shard_map/all_to_all | solution.py:530
  133.0 1.6 %collective-permute-start.9 = (s16[8,592,128]{2,1,0:T(8,128)(2,1)S(1)}, s16[8,592,128]{2,1,0:T(8,128)(2,1)S(1)}, u32[]{:S(2)}, u32[]{:S(2)}) collective-permute-start(s16[8,592,128]{2,1,0:T(8,128)(2,1)S(1)} %all_to_all.28), channel_id=1, source_target_pairs={{0,8},{8,0},{1,9},{9,1},{2,10},{10,2},{3,11},{11,3},{4,12},{12,4},... | collective-permute-start | bytes 3637256 | tf_op jit(solution)/shard_map/ppermute | solution.py:506
  134.5 2.5 %collective-permute-done.9 = s16[8,592,128]{2,1,0:T(8,128)(2,1)S(1)} collective-permute-done((s16[8,592,128]{2,1,0:T(8,128)(2,1)S(1)}, s16[8,592,128]{2,1,0:T(8,128)(2,1)S(1)}, u32[]{:S(2)}, u32[]{:S(2)}) %collective-permute-start.9) | collective-permute-done | bytes 1212448 | tf_op jit(solution)/shard_map/ppermute | solution.py:506
  137.1 3.0 %finish.1 = (f32[4,2,1024,128]{3,2,1,0:T(8,128)}, f32[4,2,64,128]{3,2,1,0:T(8,128)}) custom-call(s16[4,2,592,128]{3,2,1,0:T(8,128)(2,1)S(1)} %bitcast.9, s16[4,2,592,128]{3,2,1,0:T(8,128)(2,1)S(1)} %bitcast.11), custom_call_target="tpu_custom_call" | custom-call | flops 10000000 | bytes 7000000 | tf_op jit(solution)/shard_map/finish/pallas_call | solution.py:490
  (3 shorter events, 0.0 us)
Async XLA Ops:
  3.3 12.0 %copy-start.1 = (s32[4]{0:T(128)S(1)}, s32[4]{0:T(128)}, u32[]{:S(2)}) copy-start(s32[4]{0:T(128)} %param.6) | copy-start | bytes 52
  3.3 12.2 %copy-start.2 = (s32[128]{0:T(128)S(1)}, s32[128]{0:T(128)}, u32[]{:S(2)}) copy-start(s32[128]{0:T(128)} %param.7) | copy-start | bytes 1540
  3.3 51.8 %all-to-all-start = ((s16[64,144,128]{2,1,0:T(8,128)(2,1)}), s16[64,144,128]{2,1,0:T(8,128)(2,1)S(1)}, u32[]{:S(2)}, u32[]{:S(2)}) async-start(s16[64,144,128]{2,1,0:T(8,128)(2,1)} %code_down.1), calls=%async_computation | async-start | bytes 4718592 | tf_op jit(solution)/shard_map/all_to_all | solution.py:510
  15.6 3.4 %copy-start = (bf16[1024,32,128]{2,1,0:T(8,128)(2,1)S(1)}, bf16[1024,32,128]{2,1,0:T(8,128)(2,1)}, u32[]{:S(2)}) copy-start(bf16[1024,32,128]{2,1,0:T(8,128)(2,1)} %param.4) | copy-start | bytes 25165828
  24.8 3.4 %collective-permute-start = (s16[8,528,128]{2,1,0:T(8,128)(2,1)S(1)}, s16[8,528,128]{2,1,0:T(8,128)(2,1)S(1)}, u32[]{:S(2)}, u32[]{:S(2)}) collective-permute-start(s16[8,528,128]{2,1,0:T(8,128)(2,1)S(1)} %get-tuple-element.31), channel_id=1, source_target_pairs={{0,8},{8,0},{1,9},{9,1},{2,10},{10,2},{3,11},{11,3},{4,12},{12,4},... | collective-permute-start | bytes 3244040 | tf_op jit(solution)/shard_map/ppermute | solution.py:506
  29.4 18.2 %collective-permute-start.1 = (s16[528,128]{1,0:T(8,128)(2,1)S(1)}, s16[528,128]{1,0:T(8,128)(2,1)S(1)}, u32[]{:S(2)}, u32[]{:S(2)}) collective-permute-start(s16[528,128]{1,0:T(8,128)(2,1)S(1)} %get-tuple-element.33), channel_id=1, source_target_pairs={{0,96},{16,112},{32,64},{48,80},{64,32},{80,48},{96,0},{112,16},{1... | collective-permute-start | bytes 405512 | tf_op jit(solution)/shard_map/ppermute | solution.py:517
  33.3 18.5 %collective-permute-start.2 = (s16[528,128]{1,0:T(8,128)(2,1)S(1)}, s16[528,128]{1,0:T(8,128)(2,1)S(1)}, u32[]{:S(2)}, u32[]{:S(2)}) collective-permute-start(s16[528,128]{1,0:T(8,128)(2,1)S(1)} %get-tuple-element.34), channel_id=1, source_target_pairs={{0,112},{16,96},{32,80},{48,64},{64,48},{80,32},{96,16},{112,0},{1... | collective-permute-start | bytes 405512 | tf_op jit(solution)/shard_map/ppermute | solution.py:517
  34.1 19.2 %collective-permute-start.3 = (s16[528,128]{1,0:T(8,128)(2,1)S(1)}, s16[528,128]{1,0:T(8,128)(2,1)S(1)}, u32[]{:S(2)}, u32[]{:S(2)}) collective-permute-start(s16[528,128]{1,0:T(8,128)(2,1)S(1)} %get-tuple-element.35), channel_id=1, source_target_pairs={{0,80},{16,64},{32,112},{48,96},{64,16},{80,0},{96,48},{112,32},{1... | collective-permute-start | bytes 405512 | tf_op jit(solution)/shard_map/ppermute | solution.py:517
  34.2 21.0 %collective-permute-start.4 = (s16[528,128]{1,0:T(8,128)(2,1)S(1)}, s16[528,128]{1,0:T(8,128)(2,1)S(1)}, u32[]{:S(2)}, u32[]{:S(2)}) collective-permute-start(s16[528,128]{1,0:T(8,128)(2,1)S(1)} %get-tuple-element.36), channel_id=1, source_target_pairs={{0,32},{16,48},{32,0},{48,16},{64,96},{80,112},{96,64},{112,80},{1... | collective-permute-start | bytes 405512 | tf_op jit(solution)/shard_map/ppermute | solution.py:517
  55.2 5.0 %collective-permute-start.8 = (s16[64,144,128]{2,1,0:T(8,128)(2,1)S(1)}, s16[64,144,128]{2,1,0:T(8,128)(2,1)S(1)}, u32[]{:S(2)}, u32[]{:S(2)}) collective-permute-start(s16[64,144,128]{2,1,0:T(8,128)(2,1)S(1)} %all-to-all-done), channel_id=1, source_target_pairs={{0,8},{8,0},{1,9},{9,1},{2,10},{10,2},{3,11},{11,3},{4,12},{12,4},... | collective-permute-start | bytes 7077896 | tf_op jit(solution)/shard_map/ppermute | solution.py:506
  56.0 6.9 %collective-permute-start.5 = (s16[528,128]{1,0:T(8,128)(2,1)S(1)}, s16[528,128]{1,0:T(8,128)(2,1)S(1)}, u32[]{:S(2)}, u32[]{:S(2)}) collective-permute-start(s16[528,128]{1,0:T(8,128)(2,1)S(1)} %get-tuple-element.41), channel_id=1, source_target_pairs={{0,48},{16,32},{32,16},{48,0},{64,112},{80,96},{96,80},{112,64},{1... | collective-permute-start | bytes 405512 | tf_op jit(solution)/shard_map/ppermute | solution.py:517
  58.9 4.9 %collective-permute-start.6 = (s16[528,128]{1,0:T(8,128)(2,1)S(1)}, s16[528,128]{1,0:T(8,128)(2,1)S(1)}, u32[]{:S(2)}, u32[]{:S(2)}) collective-permute-start(s16[528,128]{1,0:T(8,128)(2,1)S(1)} %get-tuple-element.42), channel_id=1, source_target_pairs={{0,16},{16,0},{32,48},{48,32},{64,80},{80,64},{96,112},{112,96},{1... | collective-permute-start | bytes 405512 | tf_op jit(solution)/shard_map/ppermute | solution.py:517
  59.1 4.8 %collective-permute-start.7 = (s16[528,128]{1,0:T(8,128)(2,1)S(1)}, s16[528,128]{1,0:T(8,128)(2,1)S(1)}, u32[]{:S(2)}, u32[]{:S(2)}) collective-permute-start(s16[528,128]{1,0:T(8,128)(2,1)S(1)} %get-tuple-element.43), channel_id=1, source_target_pairs={{0,64},{16,80},{32,96},{48,112},{64,0},{80,16},{96,32},{112,48},{1... | collective-permute-start | bytes 405512 | tf_op jit(solution)/shard_map/ppermute | solution.py:517
  133.0 4.1 %collective-permute-start.9 = (s16[8,592,128]{2,1,0:T(8,128)(2,1)S(1)}, s16[8,592,128]{2,1,0:T(8,128)(2,1)S(1)}, u32[]{:S(2)}, u32[]{:S(2)}) collective-permute-start(s16[8,592,128]{2,1,0:T(8,128)(2,1)S(1)} %all_to_all.28), channel_id=1, source_target_pairs={{0,8},{8,0},{1,9},{9,1},{2,10},{10,2},{3,11},{11,3},{4,12},{12,4},... | collective-permute-start | bytes 3637256 | tf_op jit(solution)/shard_map/ppermute | solution.py:506

commit v7 on v6

--- a/solution.py
+++ b/solution.py
@@ -232,8 +232,9 @@
 def forward_step(down_ref, both, shots):
     sums = []
     for c in range(2):
-        first = dot(down_ref[0, c, shots, :], both) + dot(down_ref[1, c, shots, :], both)
-        sums.append((first[:, :64] + first[:, 64:]).T)
+        first = dot(down_ref[0, c, shots, :], both)
+        first = first[:, :64] + first[:, 64:] + dot(down_ref[1, c, shots, :], both[:, :64])
+        sums.append(first.T)
     real = sums[0][:32] - sums[1][32:]
     imaginary = sums[0][32:] + sums[1][:32]
     return jnp.concatenate([real, imaginary], axis=0)

time: 140 us -> 140 us (level)
  no operation moved by 1% of the time
where the time goes in v7:
time: 140 us
  blocking collectives  58.2 us (42%)
  starting transfers between devices  27.2 us (19%)
  Pallas kernels  26.1 us (19%)
  waiting for transfers between devices  24 us (17%)
  local copies, waits for them, and re-layouts  3.4 us (2%)
    all_to_all x2, blocking collectives, shards(): received = lax.all_to_all(pieces, PLANE, 0, 0, tiled=True)  27.2 us
    all_to_all x1, blocking collectives, shards(): mine = lax.all_to_all(pieces, ('z', 'xl'), 0, 0, tiled=True)  19.9 us
    ppermute x7, waiting for transfers between devices, shards(): lax.ppermute(pieces[i], CHIPS, [(k, k ^ i) for k in range(8)])  18.1 us
    all_to_all x1, starting transfers between devices, shards(): mine = lax.all_to_all(code_down(downgoing), ALL_CHIPS, 0, 0, tiled=True)  12 us
    ppermute x7, starting transfers between devices, shards(): lax.ppermute(pieces[i], CHIPS, [(k, k ^ i) for k in range(8)])  11.8 us
    all_to_all x1, blocking collectives, shards(): sums = lax.all_to_all(sums, PLANE, 0, 0, tiled=True)  11.2 us
    ppermute x3, waiting for transfers between devices, swap_cores(): return lax.ppermute(x, 'core', [(0, 1), (1, 0)])  5.89 us
    pallas_call x1, Pallas kernels, transform(): pl.pallas_call(transform_body, in_specs=[HELD] * 3, out_specs=[HELD] * 2,...  5.81 us
  transfers between devices with their start and end apart: 11, of which 9 were waited for; matrix products, arithmetic and copies ran while one was open for 0% of the time, Pallas kernels for 7%

profile of v7, /device:TPU:1, one launch (start us, length us, event | category | flops | bytes accessed | tf_op | source)
XLA Modules:
  0.0 139.9 jit_solution(2506173146307660743)
XLA Ops:
  0.6 2.7 %code_down.1 = s16[64,144,128]{2,1,0:T(8,128)(2,1)} custom-call(f32[4,2,64,128]{3,2,1,0:T(8,128)} %in_ref.1), custom_call_target="tpu_custom_call" | custom-call | flops 1000000 | bytes 3000000 | tf_op jit(solution)/shard_map/code_down/pallas_call | solution.py:210
  3.3 0.0 copy-start.1
  3.3 0.0 copy-start.2
  3.3 12.0 %all-to-all-start = ((s16[64,144,128]{2,1,0:T(8,128)(2,1)}), s16[64,144,128]{2,1,0:T(8,128)(2,1)S(1)}, u32[]{:S(2)}, u32[]{:S(2)}) async-start(s16[64,144,128]{2,1,0:T(8,128)(2,1)} %code_down.1), calls=%async_computation | async-start | bytes 4718592 | tf_op jit(solution)/shard_map/all_to_all | solution.py:511
  15.3 0.0 copy-done.1
  15.4 0.1 cosine_convert_fusion
  15.5 0.0 copy-done.2
  15.5 0.1 select_reduce_fusion
  15.6 0.0 copy-start
  15.6 3.4 %copy-done = bf16[1024,32,128]{2,1,0:T(8,128)(2,1)S(1)} copy-done((bf16[1024,32,128]{2,1,0:T(8,128)(2,1)S(1)}, bf16[1024,32,128]{2,1,0:T(8,128)(2,1)}, u32[]{:S(2)}) %copy-start) | copy-done | bytes 8388632
  19.0 5.8 %transform.1 = (s16[8,528,128]{2,1,0:T(8,128)(2,1)S(1)}, s16[8,528,128]{2,1,0:T(8,128)(2,1)S(1)}) custom-call(bf16[2,4,2,64,32,128]{5,4,3,2,1,0:T(8,128)(2,1)S(1)} %bitcast.8, bf16[8,32]{1,0:T(8,128)(2,1)S(1)} %bitcast.12, s32[1,128]{1,0:T(1,128)S(1)} %bitcast.13), custom_call_target="tpu_custom_call" | custom-call | flops 600000000 | bytes 10000000 | tf_op jit(solution)/shard_map/transform/pallas_call | solution.py:130
  24.8 1.0 collective-permute-start
  25.9 2.3 %collective-permute-done.other_ref = s16[8,528,128]{2,1,0:T(8,128)(2,1)S(1)} collective-permute-done((s16[8,528,128]{2,1,0:T(8,128)(2,1)S(1)}, s16[8,528,128]{2,1,0:T(8,128)(2,1)S(1)}, u32[]{:S(2)}, u32[]{:S(2)}) %collective-permute-start) | collective-permute-done | bytes 1081376 | tf_op jit(solution)/shard_map/ppermute | solution.py:507
  28.2 1.2 merge.1
  29.4 3.9 %collective-permute-start.1 = (s16[528,128]{1,0:T(8,128)(2,1)S(1)}, s16[528,128]{1,0:T(8,128)(2,1)S(1)}, u32[]{:S(2)}, u32[]{:S(2)}) collective-permute-start(s16[528,128]{1,0:T(8,128)(2,1)S(1)} %get-tuple-element.33), channel_id=1, source_target_pairs={{0,96},{16,112},{32,64},{48,80},{64,32},{80,48},{96,0},{112,16},{1... | collective-permute-start | bytes 405512 | tf_op jit(solution)/shard_map/ppermute | solution.py:518
  33.3 0.8 collective-permute-start.2
  34.1 0.1 collective-permute-start.3
  34.2 3.9 %collective-permute-start.4 = (s16[528,128]{1,0:T(8,128)(2,1)S(1)}, s16[528,128]{1,0:T(8,128)(2,1)S(1)}, u32[]{:S(2)}, u32[]{:S(2)}) collective-permute-start(s16[528,128]{1,0:T(8,128)(2,1)S(1)} %get-tuple-element.36), channel_id=1, source_target_pairs={{0,32},{16,48},{32,0},{48,16},{64,96},{80,112},{96,64},{112,80},{1... | collective-permute-start | bytes 405512 | tf_op jit(solution)/shard_map/ppermute | solution.py:518
  38.1 9.6 %collective-permute-done.1.refs_1_ = s16[528,128]{1,0:T(8,128)(2,1)S(1)} collective-permute-done((s16[528,128]{1,0:T(8,128)(2,1)S(1)}, s16[528,128]{1,0:T(8,128)(2,1)S(1)}, u32[]{:S(2)}, u32[]{:S(2)}) %collective-permute-start.1) | collective-permute-done | bytes 135200 | tf_op jit(solution)/shard_map/ppermute | solution.py:518
  47.7 4.2 %collective-permute-done.2.refs_2_ = s16[528,128]{1,0:T(8,128)(2,1)S(1)} collective-permute-done((s16[528,128]{1,0:T(8,128)(2,1)S(1)}, s16[528,128]{1,0:T(8,128)(2,1)S(1)}, u32[]{:S(2)}, u32[]{:S(2)}) %collective-permute-start.2) | collective-permute-done | bytes 135200 | tf_op jit(solution)/shard_map/ppermute | solution.py:518
  51.8 1.5 %collective-permute-done.3.refs_3_ = s16[528,128]{1,0:T(8,128)(2,1)S(1)} collective-permute-done((s16[528,128]{1,0:T(8,128)(2,1)S(1)}, s16[528,128]{1,0:T(8,128)(2,1)S(1)}, u32[]{:S(2)}, u32[]{:S(2)}) %collective-permute-start.3) | collective-permute-done | bytes 135200 | tf_op jit(solution)/shard_map/ppermute | solution.py:518
  53.3 1.8 %collective-permute-done.4.refs_4_ = s16[528,128]{1,0:T(8,128)(2,1)S(1)} collective-permute-done((s16[528,128]{1,0:T(8,128)(2,1)S(1)}, s16[528,128]{1,0:T(8,128)(2,1)S(1)}, u32[]{:S(2)}, u32[]{:S(2)}) %collective-permute-start.4) | collective-permute-done | bytes 135200 | tf_op jit(solution)/shard_map/ppermute | solution.py:518
  55.1 0.0 all-to-all-done
  55.2 0.9 collective-permute-start.8
  56.0 2.8 %collective-permute-start.5 = (s16[528,128]{1,0:T(8,128)(2,1)S(1)}, s16[528,128]{1,0:T(8,128)(2,1)S(1)}, u32[]{:S(2)}, u32[]{:S(2)}) collective-permute-start(s16[528,128]{1,0:T(8,128)(2,1)S(1)} %get-tuple-element.41), channel_id=1, source_target_pairs={{0,48},{16,32},{32,16},{48,0},{64,112},{80,96},{96,80},{112,64},{1... | collective-permute-start | bytes 405512 | tf_op jit(solution)/shard_map/ppermute | solution.py:518
  58.9 0.2 collective-permute-start.6
  59.1 0.1 collective-permute-start.7
  59.2 1.0 collective-permute-done.8
  60.2 2.7 %decode.1.down_ref = bf16[2,2,1024,1024]{3,2,1,0:T(8,128)(2,1)S(1)} custom-call(s16[2,2,4,4,144,128]{5,4,3,2,1,0:T(8,128)(2,1)S(1)} %bitcast.7, s16[2,2,4,4,144,128]{5,4,3,2,1,0:T(8,128)(2,1)S(1)} %bitcast.10), custom_call_target="tpu_custom_call" | custom-call | flops 20000000 | bytes 13000000 | tf_op jit(solution)/shard_map/decode/pallas_call | solution.py:292
  62.9 0.0 collective-permute-done.5.refs_5_
  62.9 0.8 collective-permute-done.6.refs_6_
  63.7 0.2 collective-permute-done.7.refs_7_
  63.9 0.3 collect.1.data_ref
  64.2 1.7 %first_adjoint.1 = (f32[64,1024]{1,0:T(8,128)S(1)}, f32[32,16,128]{2,1,0:T(8,128)S(1)}) custom-call(f32[64,1024]{1,0:T(8,128)S(1)} %collect.1.data_ref, bf16[2,2,1024,1024]{3,2,1,0:T(8,128)(2,1)S(1)} %decode.1.down_ref), custom_call_target="tpu_custom_call" | custom-call | flops 800000000 | bytes 9000000 | tf_op jit(solution)/shard_map/first_adjoint/pallas_call | solution.py:313
  65.8 14.7 %all_to_all.25.in_ref = f32[32,16,128]{2,1,0:T(8,128)S(1)} all-to-all(f32[32,16,128]{2,1,0:T(8,128)S(1)} %get-tuple-element.50), channel_id=1, replica_groups=mesh['xl'=2,'z'=4,'core'=2,'y'=4,'xh'=2] {'y','xh','xl','core'}, dimensions={0} | all-to-all | bytes 524288 | tf_op jit(solution)/shard_map/all_to_all | solution.py:525
  80.6 4.6 %second.1 = (f32[64,1024]{1,0:T(8,128)S(1)}, f32[64,1024]{1,0:T(8,128)S(1)}, f32[64,1024]{1,0:T(8,128)S(1)}, s16[32,32,128]{2,1,0:T(8,128)(2,1)S(1)}) custom-call(f32[64,1024]{1,0:T(8,128)S(1)} %get-tuple-element.49.field_ref, f32[32,16,128]{2,1,0:T(8,128)S(1)} %all_to_all.25.in_ref, bf16[2,2,1024,1024]{3,2,1,0:T(8,128)(2,1)S(1)} %decode.1.down_ref), custom_call_target="tpu_custom_call" | custom-call | flops 1600000000 | bytes 18000000 | tf_op jit(solution)/shard_map/second/pallas_call | solution.py:352
  85.2 12.5 %all_to_all.26.in_ref = s16[32,32,128]{2,1,0:T(8,128)(2,1)S(1)} all-to-all(s16[32,32,128]{2,1,0:T(8,128)(2,1)S(1)} %get-tuple-element.54), channel_id=1, replica_groups=mesh['xl'=2,'z'=4,'core'=2,'y'=4,'xh'=2] {'y','xh','xl','core'}, dimensions={0} | all-to-all | bytes 524288 | tf_op jit(solution)/shard_map/all_to_all | solution.py:527
  97.7 3.0 %change.1 = (f32[64,1024]{1,0:T(8,128)S(1)}, f32[64,1024]{1,0:T(8,128)S(1)}, f32[32,8,128]{2,1,0:T(8,128)S(1)}) custom-call(f32[64,1024]{1,0:T(8,128)S(1)} %get-tuple-element.51.gradient_ref, f32[64,1024]{1,0:T(8,128)S(1)} %get-tuple-element.52.field_ref, f32[64,1024]{1,0:T(8,128)S(1)} %get-tuple-element.53.image_ref, ...), custom_call_target="tpu_custom_call" | custom-call | flops 800000000 | bytes 9000000 | tf_op jit(solution)/shard_map/change/pallas_call | solution.py:397
  100.7 11.2 %all_to_all.27.sums_ref = f32[32,8,128]{2,1,0:T(8,128)S(1)} all-to-all(f32[32,8,128]{2,1,0:T(8,128)S(1)} %get-tuple-element.57), channel_id=1, replica_groups=mesh['xl'=2,'z'=4,'core'=2,'y'=4,'xh'=2] {'y','xh','xl','core'}, dimensions={0} | all-to-all | bytes 262144 | tf_op jit(solution)/shard_map/all_to_all | solution.py:529
  111.9 1.1 update.1
  112.9 19.9 %all_to_all.28 = s16[8,592,128]{2,1,0:T(8,128)(2,1)S(1)} all-to-all(s16[8,592,128]{2,1,0:T(8,128)(2,1)S(1)} %update.1), channel_id=1, replica_groups=mesh['xl'=2,'z'=4,'core'=2,'y'=4,'xh'=2] {'z','xl'}, dimensions={0} | all-to-all | bytes 2424832 | tf_op jit(solution)/shard_map/all_to_all | solution.py:531
  132.8 1.6 %collective-permute-start.9 = (s16[8,592,128]{2,1,0:T(8,128)(2,1)S(1)}, s16[8,592,128]{2,1,0:T(8,128)(2,1)S(1)}, u32[]{:S(2)}, u32[]{:S(2)}) collective-permute-start(s16[8,592,128]{2,1,0:T(8,128)(2,1)S(1)} %all_to_all.28), channel_id=1, source_target_pairs={{0,8},{8,0},{1,9},{9,1},{2,10},{10,2},{3,11},{11,3},{4,12},{12,4},... | collective-permute-start | bytes 3637256 | tf_op jit(solution)/shard_map/ppermute | solution.py:507
  134.4 2.5 %collective-permute-done.9 = s16[8,592,128]{2,1,0:T(8,128)(2,1)S(1)} collective-permute-done((s16[8,592,128]{2,1,0:T(8,128)(2,1)S(1)}, s16[8,592,128]{2,1,0:T(8,128)(2,1)S(1)}, u32[]{:S(2)}, u32[]{:S(2)}) %collective-permute-start.9) | collective-permute-done | bytes 1212448 | tf_op jit(solution)/shard_map/ppermute | solution.py:507
  136.9 3.0 %finish.1 = (f32[4,2,1024,128]{3,2,1,0:T(8,128)}, f32[4,2,64,128]{3,2,1,0:T(8,128)}) custom-call(s16[4,2,592,128]{3,2,1,0:T(8,128)(2,1)S(1)} %bitcast.9, s16[4,2,592,128]{3,2,1,0:T(8,128)(2,1)S(1)} %bitcast.11), custom_call_target="tpu_custom_call" | custom-call | flops 10000000 | bytes 7000000 | tf_op jit(solution)/shard_map/finish/pallas_call | solution.py:491
  (3 shorter events, 0.0 us)
Async XLA Ops:
  3.3 12.0 %copy-start.1 = (s32[4]{0:T(128)S(1)}, s32[4]{0:T(128)}, u32[]{:S(2)}) copy-start(s32[4]{0:T(128)} %param.6) | copy-start | bytes 52
  3.3 12.2 %copy-start.2 = (s32[128]{0:T(128)S(1)}, s32[128]{0:T(128)}, u32[]{:S(2)}) copy-start(s32[128]{0:T(128)} %param.7) | copy-start | bytes 1540
  3.3 51.8 %all-to-all-start = ((s16[64,144,128]{2,1,0:T(8,128)(2,1)}), s16[64,144,128]{2,1,0:T(8,128)(2,1)S(1)}, u32[]{:S(2)}, u32[]{:S(2)}) async-start(s16[64,144,128]{2,1,0:T(8,128)(2,1)} %code_down.1), calls=%async_computation | async-start | bytes 4718592 | tf_op jit(solution)/shard_map/all_to_all | solution.py:511
  15.6 3.4 %copy-start = (bf16[1024,32,128]{2,1,0:T(8,128)(2,1)S(1)}, bf16[1024,32,128]{2,1,0:T(8,128)(2,1)}, u32[]{:S(2)}) copy-start(bf16[1024,32,128]{2,1,0:T(8,128)(2,1)} %param.4) | copy-start | bytes 25165828
  24.8 3.4 %collective-permute-start = (s16[8,528,128]{2,1,0:T(8,128)(2,1)S(1)}, s16[8,528,128]{2,1,0:T(8,128)(2,1)S(1)}, u32[]{:S(2)}, u32[]{:S(2)}) collective-permute-start(s16[8,528,128]{2,1,0:T(8,128)(2,1)S(1)} %get-tuple-element.31), channel_id=1, source_target_pairs={{0,8},{8,0},{1,9},{9,1},{2,10},{10,2},{3,11},{11,3},{4,12},{12,4},... | collective-permute-start | bytes 3244040 | tf_op jit(solution)/shard_map/ppermute | solution.py:507
  29.4 18.2 %collective-permute-start.1 = (s16[528,128]{1,0:T(8,128)(2,1)S(1)}, s16[528,128]{1,0:T(8,128)(2,1)S(1)}, u32[]{:S(2)}, u32[]{:S(2)}) collective-permute-start(s16[528,128]{1,0:T(8,128)(2,1)S(1)} %get-tuple-element.33), channel_id=1, source_target_pairs={{0,96},{16,112},{32,64},{48,80},{64,32},{80,48},{96,0},{112,16},{1... | collective-permute-start | bytes 405512 | tf_op jit(solution)/shard_map/ppermute | solution.py:518
  33.3 18.5 %collective-permute-start.2 = (s16[528,128]{1,0:T(8,128)(2,1)S(1)}, s16[528,128]{1,0:T(8,128)(2,1)S(1)}, u32[]{:S(2)}, u32[]{:S(2)}) collective-permute-start(s16[528,128]{1,0:T(8,128)(2,1)S(1)} %get-tuple-element.34), channel_id=1, source_target_pairs={{0,112},{16,96},{32,80},{48,64},{64,48},{80,32},{96,16},{112,0},{1... | collective-permute-start | bytes 405512 | tf_op jit(solution)/shard_map/ppermute | solution.py:518
  34.1 19.2 %collective-permute-start.3 = (s16[528,128]{1,0:T(8,128)(2,1)S(1)}, s16[528,128]{1,0:T(8,128)(2,1)S(1)}, u32[]{:S(2)}, u32[]{:S(2)}) collective-permute-start(s16[528,128]{1,0:T(8,128)(2,1)S(1)} %get-tuple-element.35), channel_id=1, source_target_pairs={{0,80},{16,64},{32,112},{48,96},{64,16},{80,0},{96,48},{112,32},{1... | collective-permute-start | bytes 405512 | tf_op jit(solution)/shard_map/ppermute | solution.py:518
  34.2 21.0 %collective-permute-start.4 = (s16[528,128]{1,0:T(8,128)(2,1)S(1)}, s16[528,128]{1,0:T(8,128)(2,1)S(1)}, u32[]{:S(2)}, u32[]{:S(2)}) collective-permute-start(s16[528,128]{1,0:T(8,128)(2,1)S(1)} %get-tuple-element.36), channel_id=1, source_target_pairs={{0,32},{16,48},{32,0},{48,16},{64,96},{80,112},{96,64},{112,80},{1... | collective-permute-start | bytes 405512 | tf_op jit(solution)/shard_map/ppermute | solution.py:518
  55.2 5.0 %collective-permute-start.8 = (s16[64,144,128]{2,1,0:T(8,128)(2,1)S(1)}, s16[64,144,128]{2,1,0:T(8,128)(2,1)S(1)}, u32[]{:S(2)}, u32[]{:S(2)}) collective-permute-start(s16[64,144,128]{2,1,0:T(8,128)(2,1)S(1)} %all-to-all-done), channel_id=1, source_target_pairs={{0,8},{8,0},{1,9},{9,1},{2,10},{10,2},{3,11},{11,3},{4,12},{12,4},... | collective-permute-start | bytes 7077896 | tf_op jit(solution)/shard_map/ppermute | solution.py:507
  56.0 6.9 %collective-permute-start.5 = (s16[528,128]{1,0:T(8,128)(2,1)S(1)}, s16[528,128]{1,0:T(8,128)(2,1)S(1)}, u32[]{:S(2)}, u32[]{:S(2)}) collective-permute-start(s16[528,128]{1,0:T(8,128)(2,1)S(1)} %get-tuple-element.41), channel_id=1, source_target_pairs={{0,48},{16,32},{32,16},{48,0},{64,112},{80,96},{96,80},{112,64},{1... | collective-permute-start | bytes 405512 | tf_op jit(solution)/shard_map/ppermute | solution.py:518
  58.9 4.9 %collective-permute-start.6 = (s16[528,128]{1,0:T(8,128)(2,1)S(1)}, s16[528,128]{1,0:T(8,128)(2,1)S(1)}, u32[]{:S(2)}, u32[]{:S(2)}) collective-permute-start(s16[528,128]{1,0:T(8,128)(2,1)S(1)} %get-tuple-element.42), channel_id=1, source_target_pairs={{0,16},{16,0},{32,48},{48,32},{64,80},{80,64},{96,112},{112,96},{1... | collective-permute-start | bytes 405512 | tf_op jit(solution)/shard_map/ppermute | solution.py:518
  59.1 4.8 %collective-permute-start.7 = (s16[528,128]{1,0:T(8,128)(2,1)S(1)}, s16[528,128]{1,0:T(8,128)(2,1)S(1)}, u32[]{:S(2)}, u32[]{:S(2)}) collective-permute-start(s16[528,128]{1,0:T(8,128)(2,1)S(1)} %get-tuple-element.43), channel_id=1, source_target_pairs={{0,64},{16,80},{32,96},{48,112},{64,0},{80,16},{96,32},{112,48},{1... | collective-permute-start | bytes 405512 | tf_op jit(solution)/shard_map/ppermute | solution.py:518
  132.8 4.1 %collective-permute-start.9 = (s16[8,592,128]{2,1,0:T(8,128)(2,1)S(1)}, s16[8,592,128]{2,1,0:T(8,128)(2,1)S(1)}, u32[]{:S(2)}, u32[]{:S(2)}) collective-permute-start(s16[8,592,128]{2,1,0:T(8,128)(2,1)S(1)} %all_to_all.28), channel_id=1, source_target_pairs={{0,8},{8,0},{1,9},{9,1},{2,10},{10,2},{3,11},{11,3},{4,12},{12,4},... | collective-permute-start | bytes 3637256 | tf_op jit(solution)/shard_map/ppermute | solution.py:507
